TPU v7x, 256 devices: a whole 4x4x8 slice. The times are simulated.
256 devices in a mesh: seq: 8 (over y, core), tensor: 8 (over z), adapter: 4 (over x).
Axes of the slice: x: 4, y: 4, z: 8, core: 2. Of those that a mesh axis runs over, the one named last changes fastest.
Arguments:
- tokens: bfloat16 [4, 8192, 4096], P('adapter', 'seq', 'tensor'), may hold values from -6 to 6
- in_weight: bfloat16 [4096, 3, 2048], P(None, None, 'tensor'), may hold values from -0.09375 to 0.09375
- adapter_down_maps: bfloat16 [32, 4096, 64], P(('seq', 'adapter'), 'tensor'), may hold values from -0.09375 to 0.09375
- adapter_up_maps: bfloat16 [32, 64, 3, 2048], P(('seq', 'adapter'), None, None, 'tensor'), may hold values from -0.359375 to 0.359375
- short_filter: float32 [7, 3, 2048], P(None, None, 'tensor'), may hold values from -2.4 to 2.4
- long_filter: float32 [128, 2048], P(None, 'tensor'), may hold values from -0.53033006 to 0.53033006
- skip: float32 [2048], P('tensor'), may hold values from -1 to 1
- out_weight: bfloat16 [2048, 4096], P('tensor'), may hold values from -0.1875 to 0.1875
- adapter_ids: int32 [4, 8192, 1], P('adapter', 'seq'), may hold values from 0 to 31; in each aligned block of 1024 rows (0 to 1023, 1024 to 2047, ..., all dimensions but the last counted through in order) at most 96 rows name the same one
Outputs:
- mixed: bfloat16 [4, 8192, 4096], P('adapter', 'seq', 'tensor')
Inputs may be any that keep to these rules, and one draw needn't show every extreme that they name: `adapter_ids`: among the rows of one device, no adapter set is named by more than 96 rows.
All inputs are finite; a program needn't handle non-finite values.
Results may differ from a plain program's by a relative error of at most 0.0082.
Values may be sent and summed in bfloat16 or wider, within the bound.
No kernel may reach another device: no remote copies, remote signals or barrier semaphores. Data moves between devices by JAX's collectives and lax.ppermute only.
A program may use at most 128 MiB of HBM per device.

v0:
```python
import jax
import jax.numpy as jnp
import numpy as np
from jax import lax
from jax.experimental import pallas as pl
from jax.experimental.pallas import tpu as pltpu
from jax.sharding import PartitionSpec as P

F32 = jnp.float32
BF16 = jnp.bfloat16
PARAMS = pltpu.CompilerParams(vmem_limit_bytes=24 * 1024 * 1024)


def cost(micros):
    return pl.CostEstimate(
        flops=int(micros * 2e9), transcendentals=0, bytes_accessed=int(micros * 2e6)
    )


def in_hbm(array):
    return pltpu.with_memory_space_constraint(array, pltpu.HBM)


def moved(block, axis, distance):
    n = lax.axis_size(axis)
    return lax.ppermute(block, axis, [(i, (i + distance) % n) for i in range(n)])


def nt_dot(a, b):
    return lax.dot_general(a, b, (((1,), (1,)), ((), ())), preferred_element_type=F32)


def codes_kernel(tok_ref, ids_ref, down_ref, *refs):
    out_ref = refs[-1]
    tok = tok_ref[...]
    ids = ids_ref[...]
    total = jnp.zeros((64, tok.shape[0]), F32)
    half = down_ref.shape[0] // 2
    for side in range(2):
        products = nt_dot(down_ref[side * half : (side + 1) * half], tok)
        for own in range(half // 64):
            total = total + jnp.where(
                ids == side * (half // 64) + own, products[own * 64 : own * 64 + 64], 0.0
            )
    for j in range(out_ref.shape[0]):
        out_ref[j] = total[:, 128 * j : 128 * j + 128]


def partial_codes(tok, ids, down, after):
    rows, depth = tok.shape
    block = 256
    return pl.pallas_call(
        codes_kernel,
        grid=(rows // block,),
        in_specs=[
            pl.BlockSpec((block, depth), lambda i: (i, 0)),
            pl.BlockSpec((1, block), lambda i: (0, i)),
            pl.BlockSpec(down.shape, lambda i: (0, 0)),
        ]
        + [pl.BlockSpec(memory_space=pl.ANY) for _ in after],
        out_specs=pl.BlockSpec((block // 128, 64, 128), lambda i: (i, 0, 0)),
        out_shape=jax.ShapeDtypeStruct((rows // 128, 64, 128), F32),
        compiler_params=PARAMS,
        cost_estimate=cost(4.0),
    )(in_hbm(tok), ids, down, *after)


def sum_kernel(parts_ref, *refs):
    out_ref = refs[-1]
    total = parts_ref[0]
    for j in range(1, parts_ref.shape[0]):
        total = total + parts_ref[j]
    total = total.astype(BF16)
    for j in range(out_ref.shape[0]):
        out_ref[j] = total


def summed_codes(parts, after):
    whole = pl.BlockSpec(parts.shape, lambda i: (0, 0, 0))
    return pl.pallas_call(
        sum_kernel,
        grid=(1,),
        in_specs=[whole] + [pl.BlockSpec(memory_space=pl.ANY) for _ in after],
        out_specs=whole,
        out_shape=jax.ShapeDtypeStruct(parts.shape, BF16),
        compiler_params=PARAMS,
        cost_estimate=cost(0.5),
    )(parts, *after)


def weight_spec(weight, k):
    parts, depth, channels = weight.shape
    return pl.BlockSpec(
        (parts, depth // 8, channels), lambda i, place: (0, (place[0] + 8 - k) % 8, 0)
    )


def projecting(place, acc, pieces, ks, weight):
    rows, depth = pieces[0].shape
    block = 256
    parts, _, channels = weight.shape
    width = parts * channels
    old = [] if acc is None else [in_hbm(acc)]
    n = len(pieces)

    def kernel(place_ref, *refs):
        total_in, refs = refs[: len(old)], refs[len(old) :]
        weights, out_ref = refs[n : 2 * n], refs[-1]
        loaded = [piece[...] for piece in refs[:n]]
        for c in range(parts):
            lanes = slice(c * channels, (c + 1) * channels)
            total = jnp.dot(loaded[0], weights[0][c], preferred_element_type=F32)
            for piece, ref in zip(loaded[1:], weights[1:]):
                total = total + jnp.dot(piece, ref[c], preferred_element_type=F32)
            if old:
                total = total + total_in[0][:, lanes]
            out_ref[:, lanes] = total

    acc_spec = pl.BlockSpec((block, width), lambda i, place: (i, 0))
    return pl.pallas_call(
        kernel,
        grid_spec=pltpu.PrefetchScalarGridSpec(
            num_scalar_prefetch=1,
            grid=(rows // block,),
            in_specs=[acc_spec for _ in old]
            + [pl.BlockSpec((block, depth), lambda i, place: (i, 0)) for _ in pieces]
            + [weight_spec(weight, k) for k in ks],
            out_specs=acc_spec,
        ),
        out_shape=jax.ShapeDtypeStruct((rows, width), F32),
        compiler_params=PARAMS,
        cost_estimate=cost(0.0045 * rows),
    )(place, *old, *[in_hbm(piece) for piece in pieces], *[weight for _ in ks])


def mixing(place, acc, last, k, weight, codes, ids, gathered, taps, first_block):
    rows, width = last.shape[0], acc.shape[1]
    block = 256
    steps = rows // block
    depth = last.shape[1]
    channels = width // 3

    def kernel(
        place_ref, acc_ref, last_ref, weight_ref, codes_ref, ids_ref,
        u0_ref, u1_ref, u2_ref, taps_ref, mixed_ref, rim_ref,
    ):
        step = pl.program_id(0)
        packed = codes_ref[...].astype(F32)
        low = jnp.concatenate([packed[j].T for j in range(2)], axis=0).astype(BF16)
        low = jnp.concatenate([low, low], axis=1)
        upper = (lax.broadcasted_iota(jnp.int32, (1, 128), 1) // 64).astype(F32)
        ids_block = jnp.broadcast_to(ids_ref[...].astype(F32), (128, block)).T
        zero = jnp.zeros_like(low)
        spread = jnp.concatenate(
            [jnp.where(ids_block == upper + 2.0 * pair, low, zero) for pair in range(16)], axis=1
        )
        for c, ref in enumerate((u0_ref, u1_ref, u2_ref)):
            lanes = slice(c * channels, (c + 1) * channels)
            total = acc_ref[:, lanes]
            total = total + jnp.dot(last_ref[...], weight_ref[c], preferred_element_type=F32)
            up = ref[...].reshape(-1, channels)
            delta = jnp.dot(spread, up, preferred_element_type=F32).astype(BF16)
            mixed_ref[:, lanes] = (total + delta.astype(F32)).astype(BF16)

        @pl.when(step == steps - 1)
        def _():
            branches = []
            for c in (1, 2):
                lanes = slice(c * channels, (c + 1) * channels)
                tail = mixed_ref[:, lanes].astype(F32)
                running = jnp.zeros((128, channels), F32)
                for tap in range(7):
                    running = (
                        running
                        + taps_ref[c, tap : tap + 1, :] * tail[block - 128 - tap : block - tap]
                    )
                branches.append(running)
            rim_ref[:128] = (branches[0] * branches[1]).astype(BF16)
            for c in range(3):
                rim_ref[128 + 16 * c : 144 + 16 * c] = mixed_ref[
                    block - 16 :, c * channels : (c + 1) * channels
                ]

    def up_spec(c):
        return pl.BlockSpec((32, 64, channels), lambda i, place: (0, c, 0))

    return pl.pallas_call(
        kernel,
        grid_spec=pltpu.PrefetchScalarGridSpec(
            num_scalar_prefetch=1,
            grid=(steps,),
            in_specs=[
                pl.BlockSpec((block, width), lambda i, place: (i + first_block, 0)),
                pl.BlockSpec((block, depth), lambda i, place: (i, 0)),
                weight_spec(weight, k),
                pl.BlockSpec((2, 64, 128), lambda i, place: (i + first_block, 0, 0)),
                pl.BlockSpec((1, block), lambda i, place: (0, i + first_block)),
                up_spec(0),
                up_spec(1),
                up_spec(2),
                pl.BlockSpec(taps.shape, lambda i, place: (0, 0, 0)),
            ],
            out_specs=[
                pl.BlockSpec((block, width), lambda i, place: (i, 0)),
                pl.BlockSpec((176, channels), lambda i, place: (0, 0)),
            ],
        ),
        out_shape=[
            jax.ShapeDtypeStruct((rows, width), BF16),
            jax.ShapeDtypeStruct((176, channels), BF16),
        ],
        compiler_params=PARAMS,
        cost_estimate=cost(4.0),
    )(place, in_hbm(acc), last, weight, codes, ids, *[in_hbm(gathered)] * 3, taps)


def split(array):
    high = array.astype(BF16)
    return high, (array - high.astype(F32)).astype(BF16)


def waves():
    size = 256
    half = size // 2
    k, t = np.arange(half)[:, None], np.arange(size)[None, :]
    angle = 2.0 * np.pi * ((k * t) % size) / size
    cosine, sine = np.cos(angle), np.sin(angle)
    alternating = 1.0 - 2.0 * (np.arange(size) % 2)
    nyquist_first = sine.copy()
    nyquist_first[0] = -alternating
    forward = np.concatenate([cosine, -nyquist_first], 0)
    last = cosine.copy()
    last[0] = alternating
    of_taps = np.concatenate([cosine, -sine, last], 0)[:, :half]
    weights = np.full((half, 1), 2.0 / size)
    weights[0] = 1.0 / size
    inverse = np.concatenate([cosine * weights, -nyquist_first * weights], 0).T[half:]
    return [np.asarray(a, np.float32) for a in (forward, of_taps, inverse)]


def filtering(mixed, rim, taps, spectrum, forward, inverse):
    block = 128
    rows, width = mixed.shape
    channels = width // 3
    steps = rows // block

    def kernel(
        mixed_ref, rim_ref, taps_ref, spectrum_ref, fwd_hi_ref, fwd_lo_ref, inv_hi_ref, inv_lo_ref,
        gated_ref, before_ref, window_ref,
    ):
        step = pl.program_id(0)
        current = mixed_ref[...].astype(F32)

        @pl.when(step == 0)
        def _():
            window_ref[:128] = rim_ref[:128]
            for c in range(3):
                before_ref[:, c * channels : (c + 1) * channels] = rim_ref[
                    128 + 16 * c : 144 + 16 * c
                ].astype(F32)

        @pl.when(step > 0)
        def _():
            window_ref[:128] = window_ref[block:]

        filtered = []
        for c in range(3):
            lanes = slice(c * channels, (c + 1) * channels)
            extended = jnp.concatenate([before_ref[:, lanes], current[:, lanes]], axis=0)
            running = jnp.zeros((block, channels), F32)
            for tap in range(7):
                running = running + taps_ref[c, tap : tap + 1, :] * extended[16 - tap : 16 - tap + block]
            filtered.append(running)
        before_ref[...] = current[block - 16 :]
        window_ref[block:] = (filtered[1] * filtered[2]).astype(BF16)
        window = window_ref[...]
        waves_in = jnp.dot(fwd_hi_ref[...], window, preferred_element_type=F32)
        waves_in = waves_in + jnp.dot(fwd_lo_ref[...], window, preferred_element_type=F32)
        real, imaginary = waves_in[:128], waves_in[128:]
        first, second, third = (spectrum_ref[128 * j : 128 * j + 128] for j in range(3))
        product = jnp.concatenate(
            [real * first - imaginary * second, real * second + imaginary * third], axis=0
        )
        high, low = split(product)
        out = jnp.dot(inv_hi_ref[...], high, preferred_element_type=F32)
        out = out + jnp.dot(inv_hi_ref[...], low, preferred_element_type=F32)
        out = out + jnp.dot(inv_lo_ref[...], high, preferred_element_type=F32)
        gated_ref[...] = (filtered[0] * out).astype(BF16)

    whole = lambda a: pl.BlockSpec(a.shape, lambda i: (0,) * a.ndim)
    operands = [rim, taps, spectrum, *forward, *inverse]
    return pl.pallas_call(
        kernel,
        grid=(steps,),
        in_specs=[pl.BlockSpec((block, width), lambda i: (i, 0))] + [whole(a) for a in operands],
        out_specs=pl.BlockSpec((block, channels), lambda i: (i, 0)),
        out_shape=jax.ShapeDtypeStruct((rows, channels), BF16),
        scratch_shapes=[
            pltpu.VMEM((16, width), F32),
            pltpu.VMEM((256, channels), BF16),
        ],
        compiler_params=PARAMS,
        cost_estimate=cost(3.5),
    )(mixed, *operands)


def out_kernel(*refs):
    pieces, (low_ref, high_ref), out_ref = refs[:8], refs[8:10], refs[-1]
    channels = low_ref.shape[2]
    for side, ref in enumerate((low_ref, high_ref)):
        total = jnp.zeros((out_ref.shape[0], channels), F32)
        for k, piece in zip((0, 1, 7, 2, 6, 3, 5, 4), pieces):
            weight = ref[4 * k : 4 * k + 4].reshape(-1, channels)
            total = total + jnp.dot(piece[...], weight, preferred_element_type=F32)
        out_ref[:, side * channels : (side + 1) * channels] = total.astype(BF16)


def out_projection(pieces, gathered, previous, first_block, rows_all):
    rows, channels = pieces[0].shape
    block = rows // 2
    operands = [in_hbm(a) for a in (*pieces, gathered, gathered)]
    in_specs = (
        [pl.BlockSpec((block, channels), lambda i: (i, 0))] * 8
        + [
            pl.BlockSpec((32, 64, channels), lambda i: (0, 3, 0)),
            pl.BlockSpec((32, 64, channels), lambda i: (0, 4, 0)),
        ]
    )
    aliases = {}
    if previous is not None:
        aliases = {len(operands): 0}
        operands.append(previous)
        in_specs.append(pl.BlockSpec(memory_space=pl.ANY))
    return pl.pallas_call(
        out_kernel,
        grid=(2,),
        in_specs=in_specs,
        out_specs=pl.BlockSpec((block, 2 * channels), lambda i: (i + first_block, 0)),
        out_shape=jax.ShapeDtypeStruct((rows_all, 2 * channels), BF16),
        input_output_aliases=aliases,
        compiler_params=PARAMS,
        cost_estimate=cost(2.3),
    )(*operands)


def parcel_kernel(up_ref, rows_ref, out_ref):
    height, channels = up_ref.shape
    out_ref[:height] = up_ref[...]
    depth = rows_ref.shape[0]
    out_ref[height : height + depth] = rows_ref[:, :channels]
    out_ref[height + depth :] = rows_ref[:, channels:]


def parcel(up, rows):
    height = up.shape[0] + 2 * rows.shape[0]
    return pl.pallas_call(
        parcel_kernel,
        grid=(1,),
        in_specs=[
            pl.BlockSpec(up.shape, lambda i: (0, 0)),
            pl.BlockSpec(rows.shape, lambda i: (0, 0)),
        ],
        out_specs=pl.BlockSpec((height, up.shape[1]), lambda i: (0, 0)),
        out_shape=jax.ShapeDtypeStruct((height, up.shape[1]), BF16),
        compiler_params=PARAMS,
        cost_estimate=cost(0.5),
    )(up, rows)


def both_ways(ahead, back):
    return moved(ahead, "tensor", 1), moved(back, "tensor", -1)


def ring(block, last):
    ahead = back = block
    pieces = [block]
    for _ in range(3):
        ahead, back = both_ways(ahead, back)
        pieces += [ahead, back]
    return pieces + [moved(ahead if last > 0 else back, "tensor", last)]


def per_device(
    tokens,
    in_weight,
    adapter_down_maps,
    adapter_up_maps,
    short_filter,
    long_filter,
    skip,
    out_weight,
    adapter_ids,
):
    tok = tokens[0]
    ids = adapter_ids.reshape(1, -1)
    rows, depth = tok.shape
    channels = in_weight.shape[2]
    rank = adapter_down_maps.shape[2]
    seq, tensor, adapter = (lax.axis_index(name) for name in ("seq", "tensor", "adapter"))
    place = tensor.astype(jnp.int32).reshape(1)
    weight = in_hbm(in_weight.transpose(1, 0, 2))
    taps = short_filter.transpose(1, 0, 2)

    half = rows // 2
    f1, b1 = both_ways(tok, tok)
    f2, b2 = both_ways(f1, b1)
    f3, b3 = both_ways(f2, b2)
    f4, b4 = both_ways(f3[half:], b3[:half])

    acc = projecting(place, None, (tok, f1, b1), (0, 1, 7), weight)
    down_all = lax.all_to_all(
        jnp.broadcast_to(adapter_down_maps[0].T[None], (32, rank, depth)),
        ("seq", "adapter"), split_axis=0, concat_axis=0, tiled=True,
    )
    forward, of_taps, inverse = (jnp.asarray(a) for a in waves())
    spectrum = jnp.dot(
        of_taps, long_filter.at[0].add(skip), precision=lax.Precision.HIGHEST
    )
    partials = partial_codes(tok, ids, down_all.reshape(-1, depth), (acc, spectrum, f2, b2))
    received = lax.all_to_all(partials, "tensor", split_axis=0, concat_axis=0, tiled=True)
    acc = projecting(place, acc, (f2, b2), (2, 6), weight)
    codes = lax.all_to_all(
        summed_codes(received, (acc, f3, b3)), "tensor", split_axis=0, concat_axis=0, tiled=True
    )

    acc = projecting(place, acc, (f3, b3), (3, 5), weight)
    quarter = out_weight.shape[0] // 4
    out_rows = lax.dynamic_slice(
        out_weight,
        (adapter * quarter, ((tensor + seq) % 8) * depth),
        (quarter, depth),
    )
    out_rows = lax.ppermute(
        out_rows,
        ("seq", "tensor"),
        [(s * 8 + z, s * 8 + (z + s) % 8) for s in range(8) for z in range(8)],
    )
    up = adapter_up_maps[0].transpose(1, 0, 2).reshape(-1, channels)
    gathered = lax.all_gather(parcel(up, out_rows), ("seq", "adapter"), axis=0)

    shared = (weight, codes, ids, gathered, taps)
    mixed_late, rim_late = mixing(place, acc, f4, 4, *shared, half // 256)
    rim_in = lax.ppermute(rim_late, "seq", [(i, i + 1) for i in range(7)])
    mixed_early, rim_early = mixing(place, acc, b4, 4, *shared, 0)

    filters = (taps, spectrum, split(forward), split(inverse))
    gated_early = ring(filtering(mixed_early, rim_in, *filters), 1)
    gated_late = ring(filtering(mixed_late, rim_early, *filters), -1)
    out = out_projection(gated_early, gathered, None, 0, rows)
    out = out_projection(gated_late, gathered, out, 2, rows)
    return out[None]


def solution(mesh):
    return jax.shard_map(
        per_device,
        mesh=mesh,
        in_specs=(
            P("adapter", "seq", "tensor"),
            P(None, None, "tensor"),
            P(("seq", "adapter"), "tensor", None),
            P(("seq", "adapter"), None, None, "tensor"),
            P(None, None, "tensor"),
            P(None, "tensor"),
            P("tensor"),
            P("tensor", None),
            P("adapter", "seq", None),
        ),
        out_specs=P("adapter", "seq", "tensor"),
        check_vma=False,
    )
```

profile of v0, /device:TPU:1, one launch (start us, length us, event | category | flops | bytes accessed | tf_op | source)
XLA Modules:
  0.0 197.9 jit_solution(2518959935683640748)
XLA Ops:
  8.3 4.4 %collective-permute-start.7 = (bf16[64,512]{1,0:T(8,128)(2,1)S(1)}, bf16[64,512]{1,0:T(8,128)(2,1)S(1)}, u32[]{:S(2)}, u32[]{:S(2)}) collective-permute-start(bf16[64,512]{1,0:T(8,128)(2,1)S(1)} %dynamic_slice.3), channel_id=1, source_target_pairs={{0,0},{4,4},{8,8},{12,12},{16,16},{20,20},{24,24},{28,28},{32,36},... | collective-permute-start | bytes 196616 | tf_op jit(solution)/shard_map/ppermute | solution.py:433
  12.7 5.6 %collective-permute-done.7.rows_ref = bf16[64,512]{1,0:T(8,128)(2,1)S(1)} collective-permute-done((bf16[64,512]{1,0:T(8,128)(2,1)S(1)}, bf16[64,512]{1,0:T(8,128)(2,1)S(1)}, u32[]{:S(2)}, u32[]{:S(2)}) %collective-permute-start.7) | collective-permute-done | bytes 65568 | tf_op jit(solution)/shard_map/ppermute | solution.py:433
  23.0 13.1 %all-to-all-start = ((bf16[32,64,512]{2,1,0:T(8,128)(2,1)}), bf16[32,64,512]{2,1,0:T(8,128)(2,1)S(1)}, u32[]{:S(2)}, u32[]{:S(2)}) async-start(bf16[32,64,512]{2,1,0:T(8,128)(2,1)} %broadcast_in_dim.4), calls=%async_computation | async-start | bytes 4194304 | tf_op jit(solution)/shard_map/all_to_all | solution.py:411
  36.2 5.3 %collective-permute-done.1.refs_2_ = bf16[1024,512]{1,0:T(8,128)(2,1)} collective-permute-done((bf16[1024,512]{1,0:T(8,128)(2,1)}, bf16[1024,512]{1,0:T(8,128)(2,1)}, u32[]{:S(2)}, u32[]{:S(2)}) %collective-permute-start.1) | collective-permute-done | bytes 1048608 | tf_op jit(solution)/shard_map/ppermute | solution.py:26
  41.5 3.4 %collective-permute-start.3 = (bf16[1024,512]{1,0:T(8,128)(2,1)}, bf16[1024,512]{1,0:T(8,128)(2,1)}, u32[]{:S(2)}, u32[]{:S(2)}) collective-permute-start(bf16[1024,512]{1,0:T(8,128)(2,1)} %collective-permute-done.1.refs_2_), channel_id=1, source_target_pairs={{0,28},{4,0},{8,4},{12,8},{16,12},{20,16},{24,20},{28,24},{1,29},{... | collective-permute-start | bytes 3145736 | tf_op jit(solution)/shard_map/ppermute | solution.py:26
  45.7 5.6 %shard_map.118.refs_0_ = f32[1024,768]{1,0:T(8,128)S(1)} custom-call(s32[1]{0:T(128)} %bitcast.place_ref, bf16[1024,512]{1,0:T(8,128)(2,1)} %bitcast.1.refs_0_.tok_ref, bf16[1024,512]{1,0:T(8,128)(2,1)} %collective-permute-done.refs_1_, bf16[1024,512]{1,0:T(8,128)(2,1)} %collective-permute-done.1.refs_2_, bf16[3,4096,256]{2,1,0:T(8,128)(2,1)} %bitcast.30, ...), custom_call_target="tpu_custom_call" | custom-call | flops 9216000000 | bytes 9216000 | tf_op jit(solution)/shard_map/pallas_call | solution.py:120
  53.0 12.8 %collective-permute-done.3.refs_2_.refs_3_ = bf16[1024,512]{1,0:T(8,128)(2,1)} collective-permute-done((bf16[1024,512]{1,0:T(8,128)(2,1)}, bf16[1024,512]{1,0:T(8,128)(2,1)}, u32[]{:S(2)}, u32[]{:S(2)}) %collective-permute-start.3) | collective-permute-done | bytes 1048608 | tf_op jit(solution)/shard_map/ppermute | solution.py:26
  65.8 3.3 %collective-permute-start.5 = (bf16[1024,512]{1,0:T(8,128)(2,1)}, bf16[1024,512]{1,0:T(8,128)(2,1)}, u32[]{:S(2)}, u32[]{:S(2)}) collective-permute-start(bf16[1024,512]{1,0:T(8,128)(2,1)} %collective-permute-done.3.refs_2_.refs_3_), channel_id=1, source_target_pairs={{0,28},{4,0},{8,4},{12,8},{16,12},{20,16},{24,20},{28,24},{1,29},{... | collective-permute-start | bytes 3145736 | tf_op jit(solution)/shard_map/ppermute | solution.py:26
  71.4 5.0 %shard_map.121 = f32[8,64,128]{2,1,0:T(8,128)} custom-call(bf16[1024,512]{1,0:T(8,128)(2,1)} %bitcast.1.refs_0_.tok_ref, s32[1,1024]{1,0:T(1,128)S(1)} %bitcast.25, bf16[2048,512]{1,0:T(8,128)(2,1)S(1)} %bitcast.19, f32[1024,768]{1,0:T(8,128)S(1)} %copy-done.14, f32[384,256]{1,0:T(8,128)S(1)} %fusion.refs_1_.spectrum_ref, ...), custom_call_target="tpu_custom_call" | custom-call | flops 8000000000 | bytes 8000000 | tf_op jit(solution)/shard_map/pallas_call | solution.py:52
  76.4 3.9 %all-to-all-start.1 = ((f32[8,64,128]{2,1,0:T(8,128)}), f32[8,64,128]{2,1,0:T(8,128)S(1)}, u32[]{:S(2)}, u32[]{:S(2)}) async-start(f32[8,64,128]{2,1,0:T(8,128)} %shard_map.121), calls=%async_computation.1 | async-start | bytes 524288 | tf_op jit(solution)/shard_map/all_to_all | solution.py:420
  80.4 5.2 %shard_map.119.refs_0_ = f32[1024,768]{1,0:T(8,128)S(1)} custom-call(s32[1]{0:T(128)} %bitcast.place_ref, f32[1024,768]{1,0:T(8,128)} %copy-done.13, bf16[1024,512]{1,0:T(8,128)(2,1)} %collective-permute-done.2.refs_1_.refs_2_, bf16[1024,512]{1,0:T(8,128)(2,1)} %collective-permute-done.3.refs_2_.refs_3_, bf16[3,4096,256]{2,1,0:T(8,128)(2,1)} %bitcast.33, ...), custom_call_target="tpu_custom_call" | custom-call | flops 9216000000 | bytes 9216000 | tf_op jit(solution)/shard_map/pallas_call | solution.py:120
  85.6 9.9 %collective-permute-done.5.refs_2_ = bf16[1024,512]{1,0:T(8,128)(2,1)} collective-permute-done((bf16[1024,512]{1,0:T(8,128)(2,1)}, bf16[1024,512]{1,0:T(8,128)(2,1)}, u32[]{:S(2)}, u32[]{:S(2)}) %collective-permute-start.5) | collective-permute-done | bytes 1048608 | tf_op jit(solution)/shard_map/ppermute | solution.py:26
  97.3 3.1 %collective-permute-start.8 = (bf16[512,512]{1,0:T(8,128)(2,1)}, bf16[512,512]{1,0:T(8,128)(2,1)}, u32[]{:S(2)}, u32[]{:S(2)}) collective-permute-start(bf16[512,512]{1,0:T(8,128)(2,1)} %slice.27), channel_id=1, source_target_pairs={{0,28},{4,0},{8,4},{12,8},{16,12},{20,16},{24,20},{28,24},{1,29},{... | collective-permute-start | bytes 1572872 | tf_op jit(solution)/shard_map/ppermute | solution.py:26
  103.0 4.0 %all-to-all-start.2 = ((bf16[8,64,128]{2,1,0:T(8,128)(2,1)}), bf16[8,64,128]{2,1,0:T(8,128)(2,1)S(1)}, u32[]{:S(2)}, u32[]{:S(2)}) async-start(bf16[8,64,128]{2,1,0:T(8,128)(2,1)} %shard_map.122), calls=%async_computation.2 | async-start | bytes 262144 | tf_op jit(solution)/shard_map/all_to_all | solution.py:422
  106.9 5.0 %shard_map.120.acc_ref = f32[1024,768]{1,0:T(8,128)S(1)} custom-call(s32[1]{0:T(128)} %bitcast.place_ref, f32[1024,768]{1,0:T(8,128)} %copy-done, bf16[1024,512]{1,0:T(8,128)(2,1)} %collective-permute-done.4.refs_1_, bf16[1024,512]{1,0:T(8,128)(2,1)} %collective-permute-done.5.refs_2_, bf16[3,4096,256]{2,1,0:T(8,128)(2,1)} %bitcast.35, ...), custom_call_target="tpu_custom_call" | custom-call | flops 9216000000 | bytes 9216000 | tf_op jit(solution)/shard_map/pallas_call | solution.py:120
  113.7 3.2 %all-to-all-done.2.codes_ref = bf16[8,64,128]{2,1,0:T(8,128)(2,1)S(1)} async-done(((bf16[8,64,128]{2,1,0:T(8,128)(2,1)}), bf16[8,64,128]{2,1,0:T(8,128)(2,1)S(1)}, u32[]{:S(2)}, u32[]{:S(2)}) %all-to-all-start.2) | async-done | bytes 131104 | tf_op jit(solution)/shard_map/all_to_all | solution.py:422
  116.9 5.6 %shard_map.124 = (bf16[512,768]{1,0:T(8,128)(2,1)S(1)}, bf16[176,256]{1,0:T(8,128)(2,1)S(1)}) custom-call(s32[1]{0:T(128)} %bitcast.place_ref, f32[1024,768]{1,0:T(8,128)} %copy-done.12, bf16[512,512]{1,0:T(8,128)(2,1)} %collective-permute-done.6.last_ref, bf16[3,4096,256]{2,1,0:T(8,128)(2,1)} %bitcast.37, bf16[8,64,128]{2,1,0:T(8,128)(2,1)S(1)} %all-to-all-done.2.codes_ref, ...), custom_call_target="tpu_custom_call" | custom-call | flops 8000000000 | bytes 8000000 | tf_op jit(solution)/shard_map/pallas_call | solution.py:187
  122.6 10.5 %collective-permute-start.16 = (bf16[176,256]{1,0:T(8,128)(2,1)S(1)}, bf16[176,256]{1,0:T(8,128)(2,1)S(1)}, u32[]{:S(2)}, u32[]{:S(2)}) collective-permute-start(bf16[176,256]{1,0:T(8,128)(2,1)S(1)} %get-tuple-element.24), channel_id=1, source_target_pairs={{0,32},{32,64},{64,96},{96,128},{128,160},{160,192},{192,224},{1,3... | collective-permute-start | bytes 270344 | tf_op jit(solution)/shard_map/ppermute | solution.py:443
  133.1 5.6 %shard_map.125 = (bf16[512,768]{1,0:T(8,128)(2,1)S(1)}, bf16[176,256]{1,0:T(8,128)(2,1)S(1)}) custom-call(s32[1]{0:T(128)} %bitcast.place_ref, f32[1024,768]{1,0:T(8,128)} %copy-done.12, bf16[512,512]{1,0:T(8,128)(2,1)} %collective-permute-done.8.last_ref, bf16[3,4096,256]{2,1,0:T(8,128)(2,1)} %bitcast.38, bf16[8,64,128]{2,1,0:T(8,128)(2,1)S(1)} %all-to-all-done.2.codes_ref, ...), custom_call_target="tpu_custom_call" | custom-call | flops 8000000000 | bytes 8000000 | tf_op jit(solution)/shard_map/pallas_call | solution.py:187
  138.7 3.3 %shard_map.127.refs_0_ = bf16[512,256]{1,0:T(8,128)(2,1)S(1)} custom-call(bf16[512,768]{1,0:T(8,128)(2,1)S(1)} %get-tuple-element.23.mixed_ref, bf16[176,256]{1,0:T(8,128)(2,1)S(1)} %collective-permute-done.16.rim_ref, f32[3,7,256]{2,1,0:T(8,128)S(1)} %bitcast.23, f32[384,256]{1,0:T(8,128)S(1)} %copy-done.2, bf16[256,256]{1,0:T(8,128)(2,1)S(1)} %copy-done.9, ...), custom_call_target="tpu_custom_call" | custom-call | flops 7000000000 | bytes 7000000 | tf_op jit(solution)/shard_map/pallas_call | solution.py:292
  142.4 3.2 %shard_map.126.refs_0_ = bf16[512,256]{1,0:T(8,128)(2,1)S(1)} custom-call(bf16[512,768]{1,0:T(8,128)(2,1)S(1)} %get-tuple-element.21.mixed_ref, bf16[176,256]{1,0:T(8,128)(2,1)S(1)} %get-tuple-element.22.rim_ref, f32[3,7,256]{2,1,0:T(8,128)S(1)} %bitcast.24, f32[384,256]{1,0:T(8,128)S(1)} %copy-done.2, bf16[256,256]{1,0:T(8,128)(2,1)S(1)} %copy-done.9, ...), custom_call_target="tpu_custom_call" | custom-call | flops 7000000000 | bytes 7000000 | tf_op jit(solution)/shard_map/pallas_call | solution.py:292
  145.6 2.5 %collective-permute-start.10 = (bf16[512,256]{1,0:T(8,128)(2,1)S(1)}, bf16[512,256]{1,0:T(8,128)(2,1)S(1)}, u32[]{:S(2)}, u32[]{:S(2)}) collective-permute-start(bf16[512,256]{1,0:T(8,128)(2,1)S(1)} %shard_map.126.refs_0_), channel_id=1, source_target_pairs={{0,28},{4,0},{8,4},{12,8},{16,12},{20,16},{24,20},{28,24},{1,29},{... | collective-permute-start | bytes 786440 | tf_op jit(solution)/shard_map/ppermute | solution.py:26
  148.2 3.1 %collective-permute-done.17.refs_1_ = bf16[512,256]{1,0:T(8,128)(2,1)S(1)} collective-permute-done((bf16[512,256]{1,0:T(8,128)(2,1)S(1)}, bf16[512,256]{1,0:T(8,128)(2,1)S(1)}, u32[]{:S(2)}, u32[]{:S(2)}) %collective-permute-start.17) | collective-permute-done | bytes 262176 | tf_op jit(solution)/shard_map/ppermute | solution.py:26
  151.3 2.6 %collective-permute-done.10.refs_2_ = bf16[512,256]{1,0:T(8,128)(2,1)S(1)} collective-permute-done((bf16[512,256]{1,0:T(8,128)(2,1)S(1)}, bf16[512,256]{1,0:T(8,128)(2,1)S(1)}, u32[]{:S(2)}, u32[]{:S(2)}) %collective-permute-start.10) | collective-permute-done | bytes 262176 | tf_op jit(solution)/shard_map/ppermute | solution.py:26
  153.9 3.3 %collective-permute-start.12 = (bf16[512,256]{1,0:T(8,128)(2,1)S(1)}, bf16[512,256]{1,0:T(8,128)(2,1)S(1)}, u32[]{:S(2)}, u32[]{:S(2)}) collective-permute-start(bf16[512,256]{1,0:T(8,128)(2,1)S(1)} %collective-permute-done.10.refs_2_), channel_id=1, source_target_pairs={{0,28},{4,0},{8,4},{12,8},{16,12},{20,16},{24,20},{28,24},{1,29},{... | collective-permute-start | bytes 786440 | tf_op jit(solution)/shard_map/ppermute | solution.py:26
  159.5 3.3 %collective-permute-start.20 = (bf16[512,256]{1,0:T(8,128)(2,1)S(1)}, bf16[512,256]{1,0:T(8,128)(2,1)S(1)}, u32[]{:S(2)}, u32[]{:S(2)}) collective-permute-start(bf16[512,256]{1,0:T(8,128)(2,1)S(1)} %collective-permute-done.18.refs_2_), channel_id=1, source_target_pairs={{0,28},{4,0},{8,4},{12,8},{16,12},{20,16},{24,20},{28,24},{1,29},{... | collective-permute-start | bytes 786440 | tf_op jit(solution)/shard_map/ppermute | solution.py:26
  162.8 2.5 %collective-permute-done.9.refs_1_ = bf16[512,256]{1,0:T(8,128)(2,1)S(1)} collective-permute-done((bf16[512,256]{1,0:T(8,128)(2,1)S(1)}, bf16[512,256]{1,0:T(8,128)(2,1)S(1)}, u32[]{:S(2)}, u32[]{:S(2)}) %collective-permute-start.9) | collective-permute-done | bytes 262176 | tf_op jit(solution)/shard_map/ppermute | solution.py:26
  165.3 3.1 %collective-permute-start.14 = (bf16[512,256]{1,0:T(8,128)(2,1)S(1)}, bf16[512,256]{1,0:T(8,128)(2,1)S(1)}, u32[]{:S(2)}, u32[]{:S(2)}) collective-permute-start(bf16[512,256]{1,0:T(8,128)(2,1)S(1)} %collective-permute-done.12.refs_4_), channel_id=1, source_target_pairs={{0,28},{4,0},{8,4},{12,8},{16,12},{20,16},{24,20},{28,24},{1,29},{... | collective-permute-start | bytes 786440 | tf_op jit(solution)/shard_map/ppermute | solution.py:26
  170.8 3.3 %collective-permute-start.22 = (bf16[512,256]{1,0:T(8,128)(2,1)S(1)}, bf16[512,256]{1,0:T(8,128)(2,1)S(1)}, u32[]{:S(2)}, u32[]{:S(2)}) collective-permute-start(bf16[512,256]{1,0:T(8,128)(2,1)S(1)} %collective-permute-done.20.refs_4_), channel_id=1, source_target_pairs={{0,28},{4,0},{8,4},{12,8},{16,12},{20,16},{24,20},{28,24},{1,29},{... | collective-permute-start | bytes 786440 | tf_op jit(solution)/shard_map/ppermute | solution.py:26
  176.4 3.3 %collective-permute-start.15 = (bf16[512,256]{1,0:T(8,128)(2,1)S(1)}, bf16[512,256]{1,0:T(8,128)(2,1)S(1)}, u32[]{:S(2)}, u32[]{:S(2)}) collective-permute-start(bf16[512,256]{1,0:T(8,128)(2,1)S(1)} %collective-permute-done.14.refs_6_), channel_id=1, source_target_pairs={{0,28},{4,0},{8,4},{12,8},{16,12},{20,16},{24,20},{28,24},{1,29},{... | collective-permute-start | bytes 786440 | tf_op jit(solution)/shard_map/ppermute | solution.py:26
  181.2 4.2 %shard_map.128.refs_10_ = bf16[1024,512]{1,0:T(8,128)(2,1)} custom-call(bf16[512,256]{1,0:T(8,128)(2,1)} %copy-done.4, bf16[512,256]{1,0:T(8,128)(2,1)} %copy-done.19, bf16[512,256]{1,0:T(8,128)(2,1)} %copy-done.21, bf16[512,256]{1,0:T(8,128)(2,1)} %copy-done.23, bf16[512,256]{1,0:T(8,128)(2,1)} %copy-done.25, bf16[512,256]{1,0:T(8,128)(2,1)} %copy-done.27, ...), custom_call_target="tpu_custom_call" | custom-call | flops 4600000000 | bytes 4600000 | tf_op jit(solution)/shard_map/pallas_call | solution.py:334
  186.9 4.2 %shard_map.129 = bf16[1024,512]{1,0:T(8,128)(2,1)} custom-call(bf16[512,256]{1,0:T(8,128)(2,1)} %copy-done.3, bf16[512,256]{1,0:T(8,128)(2,1)} %copy-done.20, bf16[512,256]{1,0:T(8,128)(2,1)} %copy-done.18, bf16[512,256]{1,0:T(8,128)(2,1)} %copy-done.24, bf16[512,256]{1,0:T(8,128)(2,1)} %copy-done.22, ...), custom_call_target="tpu_custom_call", output_to_operand_aliasing={{}: (10, {})} | custom-call | flops 4600000000 | bytes 4600000 | tf_op jit(solution)/shard_map/pallas_call | solution.py:334
  (109 shorter events, 27.9 us)
Async XLA Ops:
  6.5 110.4 %all-gather.3.cloned.1.call-start = ((), (), s32[]{:S(2)}) async-start(), calls=%async_computation.3 | async-start | bytes 5406720 | tf_op jit(solution)/shard_map/all_gather | solution.py:439
  8.3 9.9 %collective-permute-start.7 = (bf16[64,512]{1,0:T(8,128)(2,1)S(1)}, bf16[64,512]{1,0:T(8,128)(2,1)S(1)}, u32[]{:S(2)}, u32[]{:S(2)}) collective-permute-start(bf16[64,512]{1,0:T(8,128)(2,1)S(1)} %dynamic_slice.3), channel_id=1, source_target_pairs={{0,0},{4,4},{8,8},{12,12},{16,16},{20,20},{24,24},{28,28},{32,36},... | collective-permute-start | bytes 196616 | tf_op jit(solution)/shard_map/ppermute | solution.py:433
  19.9 21.6 %collective-permute-start.1 = (bf16[1024,512]{1,0:T(8,128)(2,1)}, bf16[1024,512]{1,0:T(8,128)(2,1)}, u32[]{:S(2)}, u32[]{:S(2)}) collective-permute-start(bf16[1024,512]{1,0:T(8,128)(2,1)} %bitcast.1.refs_0_.tok_ref), channel_id=1, source_target_pairs={{0,28},{4,0},{8,4},{12,8},{16,12},{20,16},{24,20},{28,24},{1,29},{... | collective-permute-start | bytes 3145736 | tf_op jit(solution)/shard_map/ppermute | solution.py:26
  21.4 23.8 %collective-permute-start = (bf16[1024,512]{1,0:T(8,128)(2,1)}, bf16[1024,512]{1,0:T(8,128)(2,1)}, u32[]{:S(2)}, u32[]{:S(2)}) collective-permute-start(bf16[1024,512]{1,0:T(8,128)(2,1)} %bitcast.1.refs_0_.tok_ref), channel_id=1, source_target_pairs={{0,4},{4,8},{8,12},{12,16},{16,20},{20,24},{24,28},{28,0},{1,5},{5... | collective-permute-start | bytes 3145736 | tf_op jit(solution)/shard_map/ppermute | solution.py:26
  23.0 46.5 %all-to-all-start = ((bf16[32,64,512]{2,1,0:T(8,128)(2,1)}), bf16[32,64,512]{2,1,0:T(8,128)(2,1)S(1)}, u32[]{:S(2)}, u32[]{:S(2)}) async-start(bf16[32,64,512]{2,1,0:T(8,128)(2,1)} %broadcast_in_dim.4), calls=%async_computation | async-start | bytes 4194304 | tf_op jit(solution)/shard_map/all_to_all | solution.py:411
  41.5 24.3 %collective-permute-start.3 = (bf16[1024,512]{1,0:T(8,128)(2,1)}, bf16[1024,512]{1,0:T(8,128)(2,1)}, u32[]{:S(2)}, u32[]{:S(2)}) collective-permute-start(bf16[1024,512]{1,0:T(8,128)(2,1)} %collective-permute-done.1.refs_2_), channel_id=1, source_target_pairs={{0,28},{4,0},{8,4},{12,8},{16,12},{20,16},{24,20},{28,24},{1,29},{... | collective-permute-start | bytes 3145736 | tf_op jit(solution)/shard_map/ppermute | solution.py:26
  45.2 24.3 %collective-permute-start.2 = (bf16[1024,512]{1,0:T(8,128)(2,1)}, bf16[1024,512]{1,0:T(8,128)(2,1)}, u32[]{:S(2)}, u32[]{:S(2)}) collective-permute-start(bf16[1024,512]{1,0:T(8,128)(2,1)} %collective-permute-done.refs_1_), channel_id=1, source_target_pairs={{0,4},{4,8},{8,12},{12,16},{16,20},{20,24},{24,28},{28,0},{1,5},{5... | collective-permute-start | bytes 3145736 | tf_op jit(solution)/shard_map/ppermute | solution.py:26
  45.7 23.8 %copy-start.1 = (f32[384,256]{1,0:T(8,128)}, f32[384,256]{1,0:T(8,128)S(1)}, u32[]{:S(2)}) copy-start(f32[384,256]{1,0:T(8,128)S(1)} %fusion.refs_1_.spectrum_ref) | copy-start | bytes 1179652
  65.8 29.7 %collective-permute-start.5 = (bf16[1024,512]{1,0:T(8,128)(2,1)}, bf16[1024,512]{1,0:T(8,128)(2,1)}, u32[]{:S(2)}, u32[]{:S(2)}) collective-permute-start(bf16[1024,512]{1,0:T(8,128)(2,1)} %collective-permute-done.3.refs_2_.refs_3_), channel_id=1, source_target_pairs={{0,28},{4,0},{8,4},{12,8},{16,12},{20,16},{24,20},{28,24},{1,29},{... | collective-permute-start | bytes 3145736 | tf_op jit(solution)/shard_map/ppermute | solution.py:26
  69.5 30.9 %collective-permute-start.4 = (bf16[1024,512]{1,0:T(8,128)(2,1)}, bf16[1024,512]{1,0:T(8,128)(2,1)}, u32[]{:S(2)}, u32[]{:S(2)}) collective-permute-start(bf16[1024,512]{1,0:T(8,128)(2,1)} %collective-permute-done.2.refs_1_.refs_2_), channel_id=1, source_target_pairs={{0,4},{4,8},{8,12},{12,16},{16,20},{20,24},{24,28},{28,0},{1,5},{5... | collective-permute-start | bytes 3145736 | tf_op jit(solution)/shard_map/ppermute | solution.py:26
  76.4 25.9 %all-to-all-start.1 = ((f32[8,64,128]{2,1,0:T(8,128)}), f32[8,64,128]{2,1,0:T(8,128)S(1)}, u32[]{:S(2)}, u32[]{:S(2)}) async-start(f32[8,64,128]{2,1,0:T(8,128)} %shard_map.121), calls=%async_computation.1 | async-start | bytes 524288 | tf_op jit(solution)/shard_map/all_to_all | solution.py:420
  97.3 35.7 %collective-permute-start.8 = (bf16[512,512]{1,0:T(8,128)(2,1)}, bf16[512,512]{1,0:T(8,128)(2,1)}, u32[]{:S(2)}, u32[]{:S(2)}) collective-permute-start(bf16[512,512]{1,0:T(8,128)(2,1)} %slice.27), channel_id=1, source_target_pairs={{0,28},{4,0},{8,4},{12,8},{16,12},{20,16},{24,20},{28,24},{1,29},{... | collective-permute-start | bytes 1572872 | tf_op jit(solution)/shard_map/ppermute | solution.py:26
  102.3 14.6 %collective-permute-start.6 = (bf16[512,512]{1,0:T(8,128)(2,1)}, bf16[512,512]{1,0:T(8,128)(2,1)}, u32[]{:S(2)}, u32[]{:S(2)}) collective-permute-start(bf16[512,512]{1,0:T(8,128)(2,1)} %slice.26), channel_id=1, source_target_pairs={{0,4},{4,8},{8,12},{12,16},{16,20},{20,24},{24,28},{28,0},{1,5},{5... | collective-permute-start | bytes 1572872 | tf_op jit(solution)/shard_map/ppermute | solution.py:26
  103.0 13.9 %all-to-all-start.2 = ((bf16[8,64,128]{2,1,0:T(8,128)(2,1)}), bf16[8,64,128]{2,1,0:T(8,128)(2,1)S(1)}, u32[]{:S(2)}, u32[]{:S(2)}) async-start(bf16[8,64,128]{2,1,0:T(8,128)(2,1)} %shard_map.122), calls=%async_computation.2 | async-start | bytes 262144 | tf_op jit(solution)/shard_map/all_to_all | solution.py:422
  122.6 16.1 %collective-permute-start.16 = (bf16[176,256]{1,0:T(8,128)(2,1)S(1)}, bf16[176,256]{1,0:T(8,128)(2,1)S(1)}, u32[]{:S(2)}, u32[]{:S(2)}) collective-permute-start(bf16[176,256]{1,0:T(8,128)(2,1)S(1)} %get-tuple-element.24), channel_id=1, source_target_pairs={{0,32},{32,64},{64,96},{96,128},{128,160},{160,192},{192,224},{1,3... | collective-permute-start | bytes 270344 | tf_op jit(solution)/shard_map/ppermute | solution.py:443
  142.0 9.3 %collective-permute-start.17 = (bf16[512,256]{1,0:T(8,128)(2,1)S(1)}, bf16[512,256]{1,0:T(8,128)(2,1)S(1)}, u32[]{:S(2)}, u32[]{:S(2)}) collective-permute-start(bf16[512,256]{1,0:T(8,128)(2,1)S(1)} %shard_map.127.refs_0_), channel_id=1, source_target_pairs={{0,4},{4,8},{8,12},{12,16},{16,20},{20,24},{24,28},{28,0},{1,5},{5... | collective-permute-start | bytes 786440 | tf_op jit(solution)/shard_map/ppermute | solution.py:26
  145.6 39.8 %copy-start.3 = (bf16[512,256]{1,0:T(8,128)(2,1)}, bf16[512,256]{1,0:T(8,128)(2,1)S(1)}, u32[]{:S(2)}) copy-start(bf16[512,256]{1,0:T(8,128)(2,1)S(1)} %shard_map.126.refs_0_) | copy-start | bytes 786436
  145.6 8.3 %collective-permute-start.10 = (bf16[512,256]{1,0:T(8,128)(2,1)S(1)}, bf16[512,256]{1,0:T(8,128)(2,1)S(1)}, u32[]{:S(2)}, u32[]{:S(2)}) collective-permute-start(bf16[512,256]{1,0:T(8,128)(2,1)S(1)} %shard_map.126.refs_0_), channel_id=1, source_target_pairs={{0,28},{4,0},{8,4},{12,8},{16,12},{20,16},{24,20},{28,24},{1,29},{... | collective-permute-start | bytes 786440 | tf_op jit(solution)/shard_map/ppermute | solution.py:26
  148.1 11.4 %collective-permute-start.18 = (bf16[512,256]{1,0:T(8,128)(2,1)S(1)}, bf16[512,256]{1,0:T(8,128)(2,1)S(1)}, u32[]{:S(2)}, u32[]{:S(2)}) collective-permute-start(bf16[512,256]{1,0:T(8,128)(2,1)S(1)} %shard_map.127.refs_0_), channel_id=1, source_target_pairs={{0,28},{4,0},{8,4},{12,8},{16,12},{20,16},{24,20},{28,24},{1,29},{... | collective-permute-start | bytes 786440 | tf_op jit(solution)/shard_map/ppermute | solution.py:26
  151.3 29.1 %copy-start.19 = (bf16[512,256]{1,0:T(8,128)(2,1)}, bf16[512,256]{1,0:T(8,128)(2,1)S(1)}, u32[]{:S(2)}) copy-start(bf16[512,256]{1,0:T(8,128)(2,1)S(1)} %collective-permute-done.17.refs_1_) | copy-start | bytes 786436
  151.3 11.5 %collective-permute-start.19 = (bf16[512,256]{1,0:T(8,128)(2,1)S(1)}, bf16[512,256]{1,0:T(8,128)(2,1)S(1)}, u32[]{:S(2)}, u32[]{:S(2)}) collective-permute-start(bf16[512,256]{1,0:T(8,128)(2,1)S(1)} %collective-permute-done.17.refs_1_), channel_id=1, source_target_pairs={{0,4},{4,8},{8,12},{12,16},{16,20},{20,24},{24,28},{28,0},{1,5},{5... | collective-permute-start | bytes 786440 | tf_op jit(solution)/shard_map/ppermute | solution.py:26
  151.3 14.0 %collective-permute-start.9 = (bf16[512,256]{1,0:T(8,128)(2,1)S(1)}, bf16[512,256]{1,0:T(8,128)(2,1)S(1)}, u32[]{:S(2)}, u32[]{:S(2)}) collective-permute-start(bf16[512,256]{1,0:T(8,128)(2,1)S(1)} %shard_map.126.refs_0_), channel_id=1, source_target_pairs={{0,4},{4,8},{8,12},{12,16},{16,20},{20,24},{24,28},{28,0},{1,5},{5... | collective-permute-start | bytes 786440 | tf_op jit(solution)/shard_map/ppermute | solution.py:26
  153.9 31.5 %copy-start.18 = (bf16[512,256]{1,0:T(8,128)(2,1)}, bf16[512,256]{1,0:T(8,128)(2,1)S(1)}, u32[]{:S(2)}) copy-start(bf16[512,256]{1,0:T(8,128)(2,1)S(1)} %collective-permute-done.10.refs_2_) | copy-start | bytes 786436
  153.9 11.4 %collective-permute-start.12 = (bf16[512,256]{1,0:T(8,128)(2,1)S(1)}, bf16[512,256]{1,0:T(8,128)(2,1)S(1)}, u32[]{:S(2)}, u32[]{:S(2)}) collective-permute-start(bf16[512,256]{1,0:T(8,128)(2,1)S(1)} %collective-permute-done.10.refs_2_), channel_id=1, source_target_pairs={{0,28},{4,0},{8,4},{12,8},{16,12},{20,16},{24,20},{28,24},{1,29},{... | collective-permute-start | bytes 786440 | tf_op jit(solution)/shard_map/ppermute | solution.py:26
  159.5 11.2 %collective-permute-start.20 = (bf16[512,256]{1,0:T(8,128)(2,1)S(1)}, bf16[512,256]{1,0:T(8,128)(2,1)S(1)}, u32[]{:S(2)}, u32[]{:S(2)}) collective-permute-start(bf16[512,256]{1,0:T(8,128)(2,1)S(1)} %collective-permute-done.18.refs_2_), channel_id=1, source_target_pairs={{0,28},{4,0},{8,4},{12,8},{16,12},{20,16},{24,20},{28,24},{1,29},{... | collective-permute-start | bytes 786440 | tf_op jit(solution)/shard_map/ppermute | solution.py:26
  162.8 11.2 %collective-permute-start.21 = (bf16[512,256]{1,0:T(8,128)(2,1)S(1)}, bf16[512,256]{1,0:T(8,128)(2,1)S(1)}, u32[]{:S(2)}, u32[]{:S(2)}) collective-permute-start(bf16[512,256]{1,0:T(8,128)(2,1)S(1)} %collective-permute-done.19.refs_3_), channel_id=1, source_target_pairs={{0,4},{4,8},{8,12},{12,16},{16,20},{20,24},{24,28},{28,0},{1,5},{5... | collective-permute-start | bytes 786440 | tf_op jit(solution)/shard_map/ppermute | solution.py:26
  165.3 10.5 %collective-permute-start.11 = (bf16[512,256]{1,0:T(8,128)(2,1)S(1)}, bf16[512,256]{1,0:T(8,128)(2,1)S(1)}, u32[]{:S(2)}, u32[]{:S(2)}) collective-permute-start(bf16[512,256]{1,0:T(8,128)(2,1)S(1)} %collective-permute-done.9.refs_1_), channel_id=1, source_target_pairs={{0,4},{4,8},{8,12},{12,16},{16,20},{20,24},{24,28},{28,0},{1,5},{5... | collective-permute-start | bytes 786440 | tf_op jit(solution)/shard_map/ppermute | solution.py:26
  165.3 11.1 %collective-permute-start.14 = (bf16[512,256]{1,0:T(8,128)(2,1)S(1)}, bf16[512,256]{1,0:T(8,128)(2,1)S(1)}, u32[]{:S(2)}, u32[]{:S(2)}) collective-permute-start(bf16[512,256]{1,0:T(8,128)(2,1)S(1)} %collective-permute-done.12.refs_4_), channel_id=1, source_target_pairs={{0,28},{4,0},{8,4},{12,8},{16,12},{20,16},{24,20},{28,24},{1,29},{... | collective-permute-start | bytes 786440 | tf_op jit(solution)/shard_map/ppermute | solution.py:26
  170.8 8.9 %collective-permute-start.22 = (bf16[512,256]{1,0:T(8,128)(2,1)S(1)}, bf16[512,256]{1,0:T(8,128)(2,1)S(1)}, u32[]{:S(2)}, u32[]{:S(2)}) collective-permute-start(bf16[512,256]{1,0:T(8,128)(2,1)S(1)} %collective-permute-done.20.refs_4_), channel_id=1, source_target_pairs={{0,28},{4,0},{8,4},{12,8},{16,12},{20,16},{24,20},{28,24},{1,29},{... | collective-permute-start | bytes 786440 | tf_op jit(solution)/shard_map/ppermute | solution.py:26
  174.0 6.4 %collective-permute-start.23 = (bf16[512,256]{1,0:T(8,128)(2,1)S(1)}, bf16[512,256]{1,0:T(8,128)(2,1)S(1)}, u32[]{:S(2)}, u32[]{:S(2)}) collective-permute-start(bf16[512,256]{1,0:T(8,128)(2,1)S(1)} %collective-permute-done.21.refs_5_), channel_id=1, source_target_pairs={{0,4},{4,8},{8,12},{12,16},{16,20},{20,24},{24,28},{28,0},{1,5},{5... | collective-permute-start | bytes 786440 | tf_op jit(solution)/shard_map/ppermute | solution.py:26
  175.8 9.6 %collective-permute-start.13 = (bf16[512,256]{1,0:T(8,128)(2,1)S(1)}, bf16[512,256]{1,0:T(8,128)(2,1)S(1)}, u32[]{:S(2)}, u32[]{:S(2)}) collective-permute-start(bf16[512,256]{1,0:T(8,128)(2,1)S(1)} %collective-permute-done.11.refs_3_), channel_id=1, source_target_pairs={{0,4},{4,8},{8,12},{12,16},{16,20},{20,24},{24,28},{28,0},{1,5},{5... | collective-permute-start | bytes 786440 | tf_op jit(solution)/shard_map/ppermute | solution.py:26
  176.4 9.1 %collective-permute-start.15 = (bf16[512,256]{1,0:T(8,128)(2,1)S(1)}, bf16[512,256]{1,0:T(8,128)(2,1)S(1)}, u32[]{:S(2)}, u32[]{:S(2)}) collective-permute-start(bf16[512,256]{1,0:T(8,128)(2,1)S(1)} %collective-permute-done.14.refs_6_), channel_id=1, source_target_pairs={{0,28},{4,0},{8,4},{12,8},{16,12},{20,16},{24,20},{28,24},{1,29},{... | collective-permute-start | bytes 786440 | tf_op jit(solution)/shard_map/ppermute | solution.py:26
  (28 other events, 314.3 us)
Sparse Core Ops, SparseCore 0:
  20.0 70.7 all-gather.2
where the time goes:
time: 202 us; the launch traced here: 198 us
  starting transfers between devices  66.2 us (33%)
  waiting for transfers between devices  53.6 us (27%)
  Pallas kernels  48.2 us (24%)
  local copies, waits for them, and re-layouts  15.5 us (8%)
  between operations  13.8 us (7%)
    ppermute x22, waiting for transfers between devices, moved(): lax.ppermute(block, axis, [(i, (i + distance) % n) for i in range(n)])  44.8 us
    ppermute x22, starting transfers between devices, moved(): lax.ppermute(block, axis, [(i, (i + distance) % n) for i in range(n)])  30.4 us
    pallas_call x3, Pallas kernels, projecting(): pl.pallas_call(kernel, grid_spec=pltpu.PrefetchScalarGridSpec(num_scalar_...  15.8 us
    all_to_all x1, starting transfers between devices, per_device(): lax.all_to_all(jnp.broadcast_to(adapter_down_maps[0].T[None], (32, rank,...  13.1 us
    pallas_call x2, Pallas kernels, mixing(): pl.pallas_call(kernel, grid_spec=pltpu.PrefetchScalarGridSpec(num_scalar_...  11.2 us
    ppermute x1, starting transfers between devices, per_device(): rim_in = lax.ppermute(rim_late, 'seq', [(i, i + 1) for i in range(7)])  10.5 us
    unnamed x65, local copies, waits for them, and re-layouts  9.33 us
    pallas_call x2, Pallas kernels, out_projection(): pl.pallas_call(out_kernel, grid=(2,), in_specs=in_specs, out_specs=pl.Blo...  8.34 us
  transfers between devices with their start and end apart: 28, of which 15 were waited for; matrix products, arithmetic and copies ran while one was open for 3% of the time, Pallas kernels for 20%

commit v1 on v0

--- a/solution.py
+++ b/solution.py
@@ -62,7 +62,7 @@
         out_shape=jax.ShapeDtypeStruct((rows // 128, 64, 128), F32),
         compiler_params=PARAMS,
         cost_estimate=cost(4.0),
-    )(in_hbm(tok), ids, down, *after)
+    )(in_hbm(tok), ids, down, *[in_hbm(a) for a in after])
 
 
 def sum_kernel(parts_ref, *refs):
@@ -85,7 +85,7 @@
         out_shape=jax.ShapeDtypeStruct(parts.shape, BF16),
         compiler_params=PARAMS,
         cost_estimate=cost(0.5),
-    )(parts, *after)
+    )(parts, *[in_hbm(a) for a in after])
 
 
 def weight_spec(weight, k):
@@ -318,12 +318,12 @@
 def out_projection(pieces, gathered, previous, first_block, rows_all):
     rows, channels = pieces[0].shape
     block = rows // 2
-    operands = [in_hbm(a) for a in (*pieces, gathered, gathered)]
+    operands = [*pieces, in_hbm(gathered), in_hbm(gathered)]
     in_specs = (
         [pl.BlockSpec((block, channels), lambda i: (i, 0))] * 8
         + [
-            pl.BlockSpec((32, 64, channels), lambda i: (0, 3, 0)),
-            pl.BlockSpec((32, 64, channels), lambda i: (0, 4, 0)),
+            pl.BlockSpec((32, 64, channels), lambda i: (0, 0, 0)),
+            pl.BlockSpec((32, 64, channels), lambda i: (0, 1, 0)),
         ]
     )
     aliases = {}
@@ -343,28 +343,50 @@
     )(*operands)
 
 
-def parcel_kernel(up_ref, rows_ref, out_ref):
-    height, channels = up_ref.shape
-    out_ref[:height] = up_ref[...]
-    depth = rows_ref.shape[0]
-    out_ref[height : height + depth] = rows_ref[:, :channels]
-    out_ref[height + depth :] = rows_ref[:, channels:]
-
-
-def parcel(up, rows):
-    height = up.shape[0] + 2 * rows.shape[0]
-    return pl.pallas_call(
-        parcel_kernel,
+def halves_kernel(ahead_ref, back_ref, ahead_out_ref, back_out_ref):
+    ahead_out_ref[...] = ahead_ref[...]
+    back_out_ref[...] = back_ref[...]
+
+
+def halves(ahead, back):
+    rows, depth = ahead.shape
+    block = rows // 4
+    return pl.pallas_call(
+        halves_kernel,
+        grid=(2,),
+        in_specs=[
+            pl.BlockSpec((block, depth), lambda i: (i + 2, 0)),
+            pl.BlockSpec((block, depth), lambda i: (i, 0)),
+        ],
+        out_specs=[pl.BlockSpec((block, depth), lambda i: (i, 0))] * 2,
+        out_shape=[jax.ShapeDtypeStruct((rows // 2, depth), BF16)] * 2,
+        compiler_params=PARAMS,
+        cost_estimate=cost(0.5),
+    )(in_hbm(ahead), in_hbm(back))
+
+
+def folding_kernel(rows_ref, after_ref, more_ref, out_ref):
+    depth, width = rows_ref.shape
+    out_ref[:depth] = rows_ref[:, : width // 2]
+    out_ref[depth:] = rows_ref[:, width // 2 :]
+
+
+def folded(rows, after, more):
+    depth, width = rows.shape
+    shape = (2 * depth, width // 2)
+    return pl.pallas_call(
+        folding_kernel,
         grid=(1,),
         in_specs=[
-            pl.BlockSpec(up.shape, lambda i: (0, 0)),
             pl.BlockSpec(rows.shape, lambda i: (0, 0)),
+            pl.BlockSpec(memory_space=pl.ANY),
+            pl.BlockSpec(memory_space=pl.ANY),
         ],
-        out_specs=pl.BlockSpec((height, up.shape[1]), lambda i: (0, 0)),
-        out_shape=jax.ShapeDtypeStruct((height, up.shape[1]), BF16),
+        out_specs=pl.BlockSpec(shape, lambda i: (0, 0)),
+        out_shape=jax.ShapeDtypeStruct(shape, BF16),
         compiler_params=PARAMS,
         cost_estimate=cost(0.5),
-    )(up, rows)
+    )(rows, in_hbm(after), in_hbm(more))
 
 
 def both_ways(ahead, back):
@@ -405,9 +427,12 @@
     f1, b1 = both_ways(tok, tok)
     f2, b2 = both_ways(f1, b1)
     f3, b3 = both_ways(f2, b2)
-    f4, b4 = both_ways(f3[half:], b3[:half])
-
-    acc = projecting(place, None, (tok, f1, b1), (0, 1, 7), weight)
+    f3_half, b3_half = halves(f3, b3)
+    f4, b4 = both_ways(f3_half, b3_half)
+
+    up = adapter_up_maps[0].transpose(1, 0, 2).reshape(-1, channels)
+    up_all = lax.all_gather(up, ("seq", "adapter"), axis=0)
+    acc = first_acc = projecting(place, None, (tok, f1, b1), (0, 1, 7), weight)
     down_all = lax.all_to_all(
         jnp.broadcast_to(adapter_down_maps[0].T[None], (32, rank, depth)),
         ("seq", "adapter"), split_axis=0, concat_axis=0, tiled=True,
@@ -416,11 +441,11 @@
     spectrum = jnp.dot(
         of_taps, long_filter.at[0].add(skip), precision=lax.Precision.HIGHEST
     )
-    partials = partial_codes(tok, ids, down_all.reshape(-1, depth), (acc, spectrum, f2, b2))
+    partials = partial_codes(tok, ids, down_all.reshape(-1, depth), (acc, f2, b2))
     received = lax.all_to_all(partials, "tensor", split_axis=0, concat_axis=0, tiled=True)
     acc = projecting(place, acc, (f2, b2), (2, 6), weight)
     codes = lax.all_to_all(
-        summed_codes(received, (acc, f3, b3)), "tensor", split_axis=0, concat_axis=0, tiled=True
+        summed_codes(received, (acc, f3_half, b3_half)), "tensor", split_axis=0, concat_axis=0, tiled=True
     )
 
     acc = projecting(place, acc, (f3, b3), (3, 5), weight)
@@ -431,14 +456,13 @@
         (quarter, depth),
     )
     out_rows = lax.ppermute(
-        out_rows,
+        folded(out_rows, first_acc, spectrum),
         ("seq", "tensor"),
         [(s * 8 + z, s * 8 + (z + s) % 8) for s in range(8) for z in range(8)],
     )
-    up = adapter_up_maps[0].transpose(1, 0, 2).reshape(-1, channels)
-    gathered = lax.all_gather(parcel(up, out_rows), ("seq", "adapter"), axis=0)
-
-    shared = (weight, codes, ids, gathered, taps)
+    out_all = lax.all_gather(out_rows, ("seq", "adapter"), axis=0)
+
+    shared = (weight, codes, ids, up_all, taps)
     mixed_late, rim_late = mixing(place, acc, f4, 4, *shared, half // 256)
     rim_in = lax.ppermute(rim_late, "seq", [(i, i + 1) for i in range(7)])
     mixed_early, rim_early = mixing(place, acc, b4, 4, *shared, 0)
@@ -446,8 +470,8 @@
     filters = (taps, spectrum, split(forward), split(inverse))
     gated_early = ring(filtering(mixed_early, rim_in, *filters), 1)
     gated_late = ring(filtering(mixed_late, rim_early, *filters), -1)
-    out = out_projection(gated_early, gathered, None, 0, rows)
-    out = out_projection(gated_late, gathered, out, 2, rows)
+    out = out_projection(gated_early, out_all, None, 0, rows)
+    out = out_projection(gated_late, out_all, out, 2, rows)
     return out[None]
 
 

time: 202 us -> 191 us (0.946); the launches traced: 198 us -> 190 us
  local copies, waits for them, and re-layouts: 15.5 us -> 9.9 us
  starting transfers between devices: 66.2 us -> 63.2 us
    ppermute x1, waiting for transfers between devices: 5.58 us -> 12.3 us  [per_device(): lax.ppermute(folded(out_rows, first_acc, spectrum), ('seq', 'tensor'), [(...]
    ppermute x22, waiting for transfers between devices: 44.8 us -> 38.7 us  [moved(): lax.ppermute(block, axis, [(i, (i + distance) % n) for i in range(n)])]
    all_to_all x1, starting transfers between devices: 13.1 us -> 8.04 us  [per_device(): lax.all_to_all(jnp.broadcast_to(adapter_down_maps[0].T[None], (32, rank,...]
    slice x2 -> x0, local copies, waits for them, and re-layouts: 3.72 us -> none  [per_device(): f4, b4 = both_ways(f3[half:], b3[:half])]
    ppermute x22, starting transfers between devices: 30.4 us -> 34 us  [moved(): lax.ppermute(block, axis, [(i, (i + distance) % n) for i in range(n)])]
    unnamed x65 -> x33, local copies, waits for them, and re-layouts: 9.33 us -> 6.58 us
    ppermute x1, starting transfers between devices: 4.36 us -> 2.05 us  [per_device(): lax.ppermute(folded(out_rows, first_acc, spectrum), ('seq', 'tensor'), [(...]
  transfers between devices with their start and end apart: 28 -> 29, of which waited for: 15 -> 15; matrix products, arithmetic and copies ran while one was open for 3% -> 2% of each run, Pallas kernels for 20% -> 23%
where the time goes in v1:
time: 191 us; the launch traced here: 190 us
  starting transfers between devices  63.2 us (33%)
  waiting for transfers between devices  54 us (28%)
  Pallas kernels  47.8 us (25%)
  between operations  13.7 us (7%)
  local copies, waits for them, and re-layouts  9.9 us (5%)
    ppermute x22, waiting for transfers between devices, moved(): lax.ppermute(block, axis, [(i, (i + distance) % n) for i in range(n)])  38.7 us
    ppermute x22, starting transfers between devices, moved(): lax.ppermute(block, axis, [(i, (i + distance) % n) for i in range(n)])  34 us
    pallas_call x3, Pallas kernels, projecting(): pl.pallas_call(kernel, grid_spec=pltpu.PrefetchScalarGridSpec(num_scalar_...  15.5 us
    ppermute x1, waiting for transfers between devices, per_device(): lax.ppermute(folded(out_rows, first_acc, spectrum), ('seq', 'tensor'), [(...  12.3 us
    pallas_call x2, Pallas kernels, mixing(): pl.pallas_call(kernel, grid_spec=pltpu.PrefetchScalarGridSpec(num_scalar_...  11.1 us
    ppermute x1, starting transfers between devices, per_device(): rim_in = lax.ppermute(rim_late, 'seq', [(i, i + 1) for i in range(7)])  9.66 us
    all_to_all x1, starting transfers between devices, per_device(): lax.all_to_all(jnp.broadcast_to(adapter_down_maps[0].T[None], (32, rank,...  8.04 us
    pallas_call x2, Pallas kernels, out_projection(): pl.pallas_call(out_kernel, grid=(2,), in_specs=in_specs, out_specs=pl.Blo...  7.67 us
  transfers between devices with their start and end apart: 29, of which 15 were waited for; matrix products, arithmetic and copies ran while one was open for 2% of the time, Pallas kernels for 23%

profile of v1, /device:TPU:1, one launch (start us, length us, event | category | flops | bytes accessed | tf_op | source)
XLA Modules:
  0.0 189.8 jit_solution(11979435056762773569)
XLA Ops:
  7.5 2.5 %collective-permute-start = (bf16[1024,512]{1,0:T(8,128)(2,1)}, bf16[1024,512]{1,0:T(8,128)(2,1)}, u32[]{:S(2)}, u32[]{:S(2)}) collective-permute-start(bf16[1024,512]{1,0:T(8,128)(2,1)} %bitcast.43), channel_id=1, source_target_pairs={{0,4},{4,8},{8,12},{12,16},{16,20},{20,24},{24,28},{28,0},{1,5},{5... | collective-permute-start | bytes 3145736 | tf_op jit(solution)/shard_map/ppermute | solution.py:26
  10.0 4.0 %collective-permute-start.1 = (bf16[1024,512]{1,0:T(8,128)(2,1)}, bf16[1024,512]{1,0:T(8,128)(2,1)}, u32[]{:S(2)}, u32[]{:S(2)}) collective-permute-start(bf16[1024,512]{1,0:T(8,128)(2,1)} %bitcast.44), channel_id=1, source_target_pairs={{0,28},{4,0},{8,4},{12,8},{16,12},{20,16},{24,20},{28,24},{1,29},{... | collective-permute-start | bytes 3145736 | tf_op jit(solution)/shard_map/ppermute | solution.py:26
  14.0 2.4 %broadcast_in_dim.4 = bf16[32,64,512]{2,1,0:T(8,128)(2,1)} broadcast(bf16[64,512]{1,0:T(8,128)(2,1)} %bitcast.28), dimensions={1,2} | broadcast | bytes 2162688 | tf_op jit(solution)/shard_map/broadcast_in_dim | solution.py:437
  16.5 8.0 %all-to-all-start = ((bf16[32,64,512]{2,1,0:T(8,128)(2,1)}), bf16[32,64,512]{2,1,0:T(8,128)(2,1)S(1)}, u32[]{:S(2)}, u32[]{:S(2)}) async-start(bf16[32,64,512]{2,1,0:T(8,128)(2,1)} %broadcast_in_dim.4), calls=%async_computation | async-start | bytes 4194304 | tf_op jit(solution)/shard_map/all_to_all | solution.py:436
  24.6 12.5 %collective-permute-done.refs_1_ = bf16[1024,512]{1,0:T(8,128)(2,1)} collective-permute-done((bf16[1024,512]{1,0:T(8,128)(2,1)}, bf16[1024,512]{1,0:T(8,128)(2,1)}, u32[]{:S(2)}, u32[]{:S(2)}) %collective-permute-start) | collective-permute-done | bytes 1048608 | tf_op jit(solution)/shard_map/ppermute | solution.py:26
  37.2 2.7 %collective-permute-start.3 = (bf16[1024,512]{1,0:T(8,128)(2,1)}, bf16[1024,512]{1,0:T(8,128)(2,1)}, u32[]{:S(2)}, u32[]{:S(2)}) collective-permute-start(bf16[1024,512]{1,0:T(8,128)(2,1)} %collective-permute-done.1.refs_2_), channel_id=1, source_target_pairs={{0,28},{4,0},{8,4},{12,8},{16,12},{20,16},{24,20},{28,24},{1,29},{... | collective-permute-start | bytes 3145736 | tf_op jit(solution)/shard_map/ppermute | solution.py:26
  41.9 5.5 %shard_map.118.refs_0_.after_ref = f32[1024,768]{1,0:T(8,128)S(1)} custom-call(s32[1]{0:T(128)} %bitcast.place_ref, bf16[1024,512]{1,0:T(8,128)(2,1)} %bitcast.45, bf16[1024,512]{1,0:T(8,128)(2,1)} %collective-permute-done.refs_1_, bf16[1024,512]{1,0:T(8,128)(2,1)} %collective-permute-done.1.refs_2_, bf16[3,4096,256]{2,1,0:T(8,128)(2,1)} %bitcast.30, ...), custom_call_target="tpu_custom_call" | custom-call | flops 9216000000 | bytes 9216000 | tf_op jit(solution)/shard_map/pallas_call | solution.py:120
  51.1 12.3 %collective-permute-done.15 = bf16[128,256]{1,0:T(8,128)(2,1)S(1)} collective-permute-done((bf16[128,256]{1,0:T(8,128)(2,1)S(1)}, bf16[128,256]{1,0:T(8,128)(2,1)S(1)}, u32[]{:S(2)}, u32[]{:S(2)}) %collective-permute-start.15) | collective-permute-done | bytes 65568 | tf_op jit(solution)/shard_map/ppermute | solution.py:458
  64.2 2.7 %collective-permute-start.5 = (bf16[1024,512]{1,0:T(8,128)(2,1)}, bf16[1024,512]{1,0:T(8,128)(2,1)}, u32[]{:S(2)}, u32[]{:S(2)}) collective-permute-start(bf16[1024,512]{1,0:T(8,128)(2,1)} %collective-permute-done.3.refs_2_), channel_id=1, source_target_pairs={{0,28},{4,0},{8,4},{12,8},{16,12},{20,16},{24,20},{28,24},{1,29},{... | collective-permute-start | bytes 3145736 | tf_op jit(solution)/shard_map/ppermute | solution.py:26
  66.9 5.0 %shard_map.122 = f32[8,64,128]{2,1,0:T(8,128)} custom-call(bf16[1024,512]{1,0:T(8,128)(2,1)} %bitcast.46, s32[1,1024]{1,0:T(1,128)S(1)} %bitcast.24, bf16[2048,512]{1,0:T(8,128)(2,1)S(1)} %bitcast.19, f32[1024,768]{1,0:T(8,128)} %copy-done.10, bf16[1024,512]{1,0:T(8,128)(2,1)} %copy-done.15, bf16[1024,512]{1,0:T(8,128)(2,1)} %collective-permute-done.3.refs_2_), custom_call_target="tpu_custom_call" | custom-call | flops 8000000000 | bytes 8000000 | tf_op jit(solution)/shard_map/pallas_call | solution.py:52
  71.9 4.6 %all-to-all-start.1 = ((f32[8,64,128]{2,1,0:T(8,128)}), f32[8,64,128]{2,1,0:T(8,128)S(1)}, u32[]{:S(2)}, u32[]{:S(2)}) async-start(f32[8,64,128]{2,1,0:T(8,128)} %shard_map.122), calls=%async_computation.1 | async-start | bytes 524288 | tf_op jit(solution)/shard_map/all_to_all | solution.py:445
  76.6 5.0 %shard_map.119.refs_0_ = f32[1024,768]{1,0:T(8,128)S(1)} custom-call(s32[1]{0:T(128)} %bitcast.place_ref, f32[1024,768]{1,0:T(8,128)} %copy-done.10, bf16[1024,512]{1,0:T(8,128)(2,1)} %copy-done.15, bf16[1024,512]{1,0:T(8,128)(2,1)} %collective-permute-done.3.refs_2_, bf16[3,4096,256]{2,1,0:T(8,128)(2,1)} %bitcast.33, bf16[3,4096,256]{2,1,0:T(8,128)(2,1)} %bitcast.34), custom_call_target="tpu_custom_call" | custom-call | flops 9216000000 | bytes 9216000 | tf_op jit(solution)/shard_map/pallas_call | solution.py:120
  83.2 7.7 %collective-permute-done.4.refs_1_.ahead_ref = bf16[1024,512]{1,0:T(8,128)(2,1)} collective-permute-done((bf16[1024,512]{1,0:T(8,128)(2,1)S(1)}, bf16[1024,512]{1,0:T(8,128)(2,1)}, u32[]{:S(2)}, u32[]{:S(2)}) %collective-permute-start.4) | collective-permute-done | bytes 1048608 | tf_op jit(solution)/shard_map/ppermute | solution.py:26
  95.5 4.8 %all-to-all-start.2 = ((bf16[8,64,128]{2,1,0:T(8,128)(2,1)}), bf16[8,64,128]{2,1,0:T(8,128)(2,1)S(1)}, u32[]{:S(2)}, u32[]{:S(2)}) async-start(bf16[8,64,128]{2,1,0:T(8,128)(2,1)} %shard_map.123), calls=%async_computation.2 | async-start | bytes 262144 | tf_op jit(solution)/shard_map/all_to_all | solution.py:447
  100.2 5.0 %shard_map.120.acc_ref = f32[1024,768]{1,0:T(8,128)S(1)} custom-call(s32[1]{0:T(128)} %bitcast.place_ref, f32[1024,768]{1,0:T(8,128)} %copy-done, bf16[1024,512]{1,0:T(8,128)(2,1)} %collective-permute-done.4.refs_1_.ahead_ref, bf16[1024,512]{1,0:T(8,128)(2,1)} %collective-permute-done.5.refs_2_.back_ref, bf16[3,4096,256]{2,1,0:T(8,128)(2,1)} %bitcast.35, ...), custom_call_target="tpu_custom_call" | custom-call | flops 9216000000 | bytes 9216000 | tf_op jit(solution)/shard_map/pallas_call | solution.py:120
  108.9 5.5 %shard_map.124 = (bf16[512,768]{1,0:T(8,128)(2,1)S(1)}, bf16[176,256]{1,0:T(8,128)(2,1)S(1)}) custom-call(s32[1]{0:T(128)} %bitcast.place_ref, f32[1024,768]{1,0:T(8,128)} %copy-done.11, bf16[512,512]{1,0:T(8,128)(2,1)S(1)} %collective-permute-done.6.last_ref, bf16[3,4096,256]{2,1,0:T(8,128)(2,1)} %bitcast.37, ...), custom_call_target="tpu_custom_call" | custom-call | flops 8000000000 | bytes 8000000 | tf_op jit(solution)/shard_map/pallas_call | solution.py:187
  114.5 9.7 %collective-permute-start.16 = (bf16[176,256]{1,0:T(8,128)(2,1)S(1)}, bf16[176,256]{1,0:T(8,128)(2,1)S(1)}, u32[]{:S(2)}, u32[]{:S(2)}) collective-permute-start(bf16[176,256]{1,0:T(8,128)(2,1)S(1)} %get-tuple-element.28), channel_id=1, source_target_pairs={{0,32},{32,64},{64,96},{96,128},{128,160},{160,192},{192,224},{1,3... | collective-permute-start | bytes 270344 | tf_op jit(solution)/shard_map/ppermute | solution.py:467
  124.2 5.6 %shard_map.125 = (bf16[512,768]{1,0:T(8,128)(2,1)S(1)}, bf16[176,256]{1,0:T(8,128)(2,1)S(1)}) custom-call(s32[1]{0:T(128)} %bitcast.place_ref, f32[1024,768]{1,0:T(8,128)} %copy-done.11, bf16[512,512]{1,0:T(8,128)(2,1)S(1)} %collective-permute-done.7.last_ref, bf16[3,4096,256]{2,1,0:T(8,128)(2,1)} %bitcast.38, ...), custom_call_target="tpu_custom_call" | custom-call | flops 8000000000 | bytes 8000000 | tf_op jit(solution)/shard_map/pallas_call | solution.py:187
  129.8 3.3 %shard_map.128.refs_0_ = bf16[512,256]{1,0:T(8,128)(2,1)S(1)} custom-call(bf16[512,768]{1,0:T(8,128)(2,1)S(1)} %get-tuple-element.27.mixed_ref, bf16[176,256]{1,0:T(8,128)(2,1)S(1)} %collective-permute-done.16.rim_ref, f32[3,7,256]{2,1,0:T(8,128)S(1)} %bitcast.22, f32[384,256]{1,0:T(8,128)S(1)} %copy-done.3, bf16[256,256]{1,0:T(8,128)(2,1)S(1)} %copy-done.6, ...), custom_call_target="tpu_custom_call" | custom-call | flops 7000000000 | bytes 7000000 | tf_op jit(solution)/shard_map/pallas_call | solution.py:292
  133.3 3.2 %shard_map.126.refs_0_ = bf16[512,256]{1,0:T(8,128)(2,1)S(1)} custom-call(bf16[512,768]{1,0:T(8,128)(2,1)S(1)} %get-tuple-element.25.mixed_ref, bf16[176,256]{1,0:T(8,128)(2,1)S(1)} %get-tuple-element.26.rim_ref, f32[3,7,256]{2,1,0:T(8,128)S(1)} %bitcast.23, f32[384,256]{1,0:T(8,128)S(1)} %copy-done.3, bf16[256,256]{1,0:T(8,128)(2,1)S(1)} %copy-done.6, ...), custom_call_target="tpu_custom_call" | custom-call | flops 7000000000 | bytes 7000000 | tf_op jit(solution)/shard_map/pallas_call | solution.py:292
  136.5 2.6 %collective-permute-start.9 = (bf16[512,256]{1,0:T(8,128)(2,1)S(1)}, bf16[512,256]{1,0:T(8,128)(2,1)S(1)}, u32[]{:S(2)}, u32[]{:S(2)}) collective-permute-start(bf16[512,256]{1,0:T(8,128)(2,1)S(1)} %shard_map.126.refs_0_), channel_id=1, source_target_pairs={{0,28},{4,0},{8,4},{12,8},{16,12},{20,16},{24,20},{28,24},{1,29},{... | collective-permute-start | bytes 786440 | tf_op jit(solution)/shard_map/ppermute | solution.py:26
  141.0 4.3 %collective-permute-done.9.refs_2_ = bf16[512,256]{1,0:T(8,128)(2,1)S(1)} collective-permute-done((bf16[512,256]{1,0:T(8,128)(2,1)S(1)}, bf16[512,256]{1,0:T(8,128)(2,1)S(1)}, u32[]{:S(2)}, u32[]{:S(2)}) %collective-permute-start.9) | collective-permute-done | bytes 262176 | tf_op jit(solution)/shard_map/ppermute | solution.py:26
  145.4 3.4 %collective-permute-start.11 = (bf16[512,256]{1,0:T(8,128)(2,1)S(1)}, bf16[512,256]{1,0:T(8,128)(2,1)S(1)}, u32[]{:S(2)}, u32[]{:S(2)}) collective-permute-start(bf16[512,256]{1,0:T(8,128)(2,1)S(1)} %collective-permute-done.9.refs_2_), channel_id=1, source_target_pairs={{0,28},{4,0},{8,4},{12,8},{16,12},{20,16},{24,20},{28,24},{1,29},{... | collective-permute-start | bytes 786440 | tf_op jit(solution)/shard_map/ppermute | solution.py:26
  148.8 2.2 %collective-permute-done.18.refs_2_ = bf16[512,256]{1,0:T(8,128)(2,1)S(1)} collective-permute-done((bf16[512,256]{1,0:T(8,128)(2,1)S(1)}, bf16[512,256]{1,0:T(8,128)(2,1)S(1)}, u32[]{:S(2)}, u32[]{:S(2)}) %collective-permute-start.18) | collective-permute-done | bytes 262176 | tf_op jit(solution)/shard_map/ppermute | solution.py:26
  151.0 3.4 %collective-permute-start.20 = (bf16[512,256]{1,0:T(8,128)(2,1)S(1)}, bf16[512,256]{1,0:T(8,128)(2,1)S(1)}, u32[]{:S(2)}, u32[]{:S(2)}) collective-permute-start(bf16[512,256]{1,0:T(8,128)(2,1)S(1)} %collective-permute-done.18.refs_2_), channel_id=1, source_target_pairs={{0,28},{4,0},{8,4},{12,8},{16,12},{20,16},{24,20},{28,24},{1,29},{... | collective-permute-start | bytes 786440 | tf_op jit(solution)/shard_map/ppermute | solution.py:26
  156.6 3.4 %collective-permute-start.13 = (bf16[512,256]{1,0:T(8,128)(2,1)S(1)}, bf16[512,256]{1,0:T(8,128)(2,1)S(1)}, u32[]{:S(2)}, u32[]{:S(2)}) collective-permute-start(bf16[512,256]{1,0:T(8,128)(2,1)S(1)} %collective-permute-done.11.refs_4_), channel_id=1, source_target_pairs={{0,28},{4,0},{8,4},{12,8},{16,12},{20,16},{24,20},{28,24},{1,29},{... | collective-permute-start | bytes 786440 | tf_op jit(solution)/shard_map/ppermute | solution.py:26
  160.0 2.2 %collective-permute-done.20.refs_4_ = bf16[512,256]{1,0:T(8,128)(2,1)S(1)} collective-permute-done((bf16[512,256]{1,0:T(8,128)(2,1)S(1)}, bf16[512,256]{1,0:T(8,128)(2,1)S(1)}, u32[]{:S(2)}, u32[]{:S(2)}) %collective-permute-start.20) | collective-permute-done | bytes 262176 | tf_op jit(solution)/shard_map/ppermute | solution.py:26
  162.2 3.4 %collective-permute-start.22 = (bf16[512,256]{1,0:T(8,128)(2,1)S(1)}, bf16[512,256]{1,0:T(8,128)(2,1)}, u32[]{:S(2)}, u32[]{:S(2)}) collective-permute-start(bf16[512,256]{1,0:T(8,128)(2,1)S(1)} %collective-permute-done.20.refs_4_), channel_id=1, source_target_pairs={{0,28},{4,0},{8,4},{12,8},{16,12},{20,16},{24,20},{28,24},{1,29},{... | collective-permute-start | bytes 786440 | tf_op jit(solution)/shard_map/ppermute | solution.py:26
  167.8 3.5 %collective-permute-start.14 = (bf16[512,256]{1,0:T(8,128)(2,1)S(1)}, bf16[512,256]{1,0:T(8,128)(2,1)}, u32[]{:S(2)}, u32[]{:S(2)}) collective-permute-start(bf16[512,256]{1,0:T(8,128)(2,1)S(1)} %collective-permute-done.13.refs_6_), channel_id=1, source_target_pairs={{0,28},{4,0},{8,4},{12,8},{16,12},{20,16},{24,20},{28,24},{1,29},{... | collective-permute-start | bytes 786440 | tf_op jit(solution)/shard_map/ppermute | solution.py:26
  171.4 2.1 %collective-permute-done.22.refs_6_ = bf16[512,256]{1,0:T(8,128)(2,1)} collective-permute-done((bf16[512,256]{1,0:T(8,128)(2,1)S(1)}, bf16[512,256]{1,0:T(8,128)(2,1)}, u32[]{:S(2)}, u32[]{:S(2)}) %collective-permute-start.22) | collective-permute-done | bytes 262176 | tf_op jit(solution)/shard_map/ppermute | solution.py:26
  175.2 3.9 %shard_map.129.refs_10_ = bf16[1024,512]{1,0:T(8,128)(2,1)} custom-call(bf16[512,256]{1,0:T(8,128)(2,1)S(1)} %shard_map.128.refs_0_, bf16[512,256]{1,0:T(8,128)(2,1)S(1)} %collective-permute-done.17.refs_1_, bf16[512,256]{1,0:T(8,128)(2,1)S(1)} %collective-permute-done.18.refs_2_, bf16[512,256]{1,0:T(8,128)(2,1)S(1)} %collective-permute-done.19.refs_3_, ...), custom_call_target="tpu_custom_call" | custom-call | flops 4600000000 | bytes 4600000 | tf_op jit(solution)/shard_map/pallas_call | solution.py:334
  179.1 3.8 %shard_map.130 = bf16[1024,512]{1,0:T(8,128)(2,1)} custom-call(bf16[512,256]{1,0:T(8,128)(2,1)S(1)} %shard_map.126.refs_0_, bf16[512,256]{1,0:T(8,128)(2,1)S(1)} %collective-permute-done.8.refs_1_, bf16[512,256]{1,0:T(8,128)(2,1)S(1)} %collective-permute-done.9.refs_2_, ...), custom_call_target="tpu_custom_call", output_to_operand_aliasing={{}: (10, {})} | custom-call | flops 4600000000 | bytes 4600000 | tf_op jit(solution)/shard_map/pallas_call | solution.py:334
  (79 shorter events, 25.7 us)
Async XLA Ops:
  6.5 102.4 %all-gather.4.cloned.1.call-start = ((), (), s32[]{:S(2)}) async-start(), calls=%async_computation.3 | async-start | bytes 3244032 | tf_op jit(solution)/shard_map/all_gather | solution.py:434
  7.5 29.7 %collective-permute-start = (bf16[1024,512]{1,0:T(8,128)(2,1)}, bf16[1024,512]{1,0:T(8,128)(2,1)}, u32[]{:S(2)}, u32[]{:S(2)}) collective-permute-start(bf16[1024,512]{1,0:T(8,128)(2,1)} %bitcast.43), channel_id=1, source_target_pairs={{0,4},{4,8},{8,12},{12,16},{16,20},{20,24},{24,28},{28,0},{1,5},{5... | collective-permute-start | bytes 3145736 | tf_op jit(solution)/shard_map/ppermute | solution.py:26
  10.0 27.1 %collective-permute-start.1 = (bf16[1024,512]{1,0:T(8,128)(2,1)}, bf16[1024,512]{1,0:T(8,128)(2,1)}, u32[]{:S(2)}, u32[]{:S(2)}) collective-permute-start(bf16[1024,512]{1,0:T(8,128)(2,1)} %bitcast.44), channel_id=1, source_target_pairs={{0,28},{4,0},{8,4},{12,8},{16,12},{20,16},{24,20},{28,24},{1,29},{... | collective-permute-start | bytes 3145736 | tf_op jit(solution)/shard_map/ppermute | solution.py:26
  14.0 25.8 %copy-start.12 = (f32[384,128]{1,0:T(8,128)S(1)}, f32[384,128]{1,0:T(8,128)}, u32[]{:S(2)}) copy-start(f32[384,128]{1,0:T(8,128)} %constant.69.clone) | copy-start | bytes 589828
  16.5 50.4 %all-to-all-start = ((bf16[32,64,512]{2,1,0:T(8,128)(2,1)}), bf16[32,64,512]{2,1,0:T(8,128)(2,1)S(1)}, u32[]{:S(2)}, u32[]{:S(2)}) async-start(bf16[32,64,512]{2,1,0:T(8,128)(2,1)} %broadcast_in_dim.4), calls=%async_computation | async-start | bytes 4194304 | tf_op jit(solution)/shard_map/all_to_all | solution.py:436
  24.5 146.8 %all-gather.6.cloned.1.call-start = ((), (), s32[]{:S(2)}) async-start(), calls=%async_computation.4 | async-start | bytes 2162688 | tf_op jit(solution)/shard_map/all_gather | solution.py:463
  37.2 26.9 %collective-permute-start.2 = (bf16[1024,512]{1,0:T(8,128)(2,1)}, bf16[1024,512]{1,0:T(8,128)(2,1)S(1)}, u32[]{:S(2)}, u32[]{:S(2)}) collective-permute-start(bf16[1024,512]{1,0:T(8,128)(2,1)} %collective-permute-done.refs_1_), channel_id=1, source_target_pairs={{0,4},{4,8},{8,12},{12,16},{16,20},{20,24},{24,28},{28,0},{1,5},{5... | collective-permute-start | bytes 3145736 | tf_op jit(solution)/shard_map/ppermute | solution.py:26
  37.2 27.0 %collective-permute-start.3 = (bf16[1024,512]{1,0:T(8,128)(2,1)}, bf16[1024,512]{1,0:T(8,128)(2,1)}, u32[]{:S(2)}, u32[]{:S(2)}) collective-permute-start(bf16[1024,512]{1,0:T(8,128)(2,1)} %collective-permute-done.1.refs_2_), channel_id=1, source_target_pairs={{0,28},{4,0},{8,4},{12,8},{16,12},{20,16},{24,20},{28,24},{1,29},{... | collective-permute-start | bytes 3145736 | tf_op jit(solution)/shard_map/ppermute | solution.py:26
  49.1 17.8 %copy-start.5 = (s32[1,1024,1]{1,2,0:T(1,128)S(1)}, s32[1,1024,1]{1,2,0:T(1,128)}, u32[]{:S(2)}) copy-start(s32[1,1024,1]{1,2,0:T(1,128)} %param.22) | copy-start | bytes 12292
  49.1 14.3 %collective-permute-start.15 = (bf16[128,256]{1,0:T(8,128)(2,1)S(1)}, bf16[128,256]{1,0:T(8,128)(2,1)S(1)}, u32[]{:S(2)}, u32[]{:S(2)}) collective-permute-start(bf16[128,256]{1,0:T(8,128)(2,1)S(1)} %shard_map.127), channel_id=1, source_target_pairs={{0,0},{4,4},{8,8},{12,12},{16,16},{20,20},{24,24},{28,28},{32,36},... | collective-permute-start | bytes 196616 | tf_op jit(solution)/shard_map/ppermute | solution.py:458
  64.1 26.8 %collective-permute-start.4 = (bf16[1024,512]{1,0:T(8,128)(2,1)S(1)}, bf16[1024,512]{1,0:T(8,128)(2,1)}, u32[]{:S(2)}, u32[]{:S(2)}) collective-permute-start(bf16[1024,512]{1,0:T(8,128)(2,1)S(1)} %collective-permute-done.2.refs_1_), channel_id=1, source_target_pairs={{0,4},{4,8},{8,12},{12,16},{16,20},{20,24},{24,28},{28,0},{1,5},{5... | collective-permute-start | bytes 3145736 | tf_op jit(solution)/shard_map/ppermute | solution.py:26
  64.2 26.7 %collective-permute-start.5 = (bf16[1024,512]{1,0:T(8,128)(2,1)}, bf16[1024,512]{1,0:T(8,128)(2,1)}, u32[]{:S(2)}, u32[]{:S(2)}) collective-permute-start(bf16[1024,512]{1,0:T(8,128)(2,1)} %collective-permute-done.3.refs_2_), channel_id=1, source_target_pairs={{0,28},{4,0},{8,4},{12,8},{16,12},{20,16},{24,20},{28,24},{1,29},{... | collective-permute-start | bytes 3145736 | tf_op jit(solution)/shard_map/ppermute | solution.py:26
  71.9 22.9 %all-to-all-start.1 = ((f32[8,64,128]{2,1,0:T(8,128)}), f32[8,64,128]{2,1,0:T(8,128)S(1)}, u32[]{:S(2)}, u32[]{:S(2)}) async-start(f32[8,64,128]{2,1,0:T(8,128)} %shard_map.122), calls=%async_computation.1 | async-start | bytes 524288 | tf_op jit(solution)/shard_map/all_to_all | solution.py:445
  92.2 32.0 %collective-permute-start.7 = (bf16[512,512]{1,0:T(8,128)(2,1)S(1)}, bf16[512,512]{1,0:T(8,128)(2,1)S(1)}, u32[]{:S(2)}, u32[]{:S(2)}) collective-permute-start(bf16[512,512]{1,0:T(8,128)(2,1)S(1)} %get-tuple-element.24.refs_2_), channel_id=1, source_target_pairs={{0,28},{4,0},{8,4},{12,8},{16,12},{20,16},{24,20},{28,24},{1,29},{... | collective-permute-start | bytes 1572872 | tf_op jit(solution)/shard_map/ppermute | solution.py:26
  93.8 15.1 %collective-permute-start.6 = (bf16[512,512]{1,0:T(8,128)(2,1)S(1)}, bf16[512,512]{1,0:T(8,128)(2,1)S(1)}, u32[]{:S(2)}, u32[]{:S(2)}) collective-permute-start(bf16[512,512]{1,0:T(8,128)(2,1)S(1)} %get-tuple-element.23.refs_1_), channel_id=1, source_target_pairs={{0,4},{4,8},{8,12},{12,16},{16,20},{20,24},{24,28},{28,0},{1,5},{5... | collective-permute-start | bytes 1572872 | tf_op jit(solution)/shard_map/ppermute | solution.py:26
  95.5 13.5 %all-to-all-start.2 = ((bf16[8,64,128]{2,1,0:T(8,128)(2,1)}), bf16[8,64,128]{2,1,0:T(8,128)(2,1)S(1)}, u32[]{:S(2)}, u32[]{:S(2)}) async-start(bf16[8,64,128]{2,1,0:T(8,128)(2,1)} %shard_map.123), calls=%async_computation.2 | async-start | bytes 262144 | tf_op jit(solution)/shard_map/all_to_all | solution.py:447
  114.5 15.3 %copy-start.3 = (f32[384,256]{1,0:T(8,128)S(1)}, f32[384,256]{1,0:T(8,128)}, u32[]{:S(2)}) copy-start(f32[384,256]{1,0:T(8,128)} %fusion.spectrum_ref.more_ref) | copy-start | bytes 1179652
  114.5 15.2 %collective-permute-start.16 = (bf16[176,256]{1,0:T(8,128)(2,1)S(1)}, bf16[176,256]{1,0:T(8,128)(2,1)S(1)}, u32[]{:S(2)}, u32[]{:S(2)}) collective-permute-start(bf16[176,256]{1,0:T(8,128)(2,1)S(1)} %get-tuple-element.28), channel_id=1, source_target_pairs={{0,32},{32,64},{64,96},{96,128},{128,160},{160,192},{192,224},{1,3... | collective-permute-start | bytes 270344 | tf_op jit(solution)/shard_map/ppermute | solution.py:467
  133.1 7.6 %collective-permute-start.17 = (bf16[512,256]{1,0:T(8,128)(2,1)S(1)}, bf16[512,256]{1,0:T(8,128)(2,1)S(1)}, u32[]{:S(2)}, u32[]{:S(2)}) collective-permute-start(bf16[512,256]{1,0:T(8,128)(2,1)S(1)} %shard_map.128.refs_0_), channel_id=1, source_target_pairs={{0,4},{4,8},{8,12},{12,16},{16,20},{20,24},{24,28},{28,0},{1,5},{5... | collective-permute-start | bytes 786440 | tf_op jit(solution)/shard_map/ppermute | solution.py:26
  136.5 8.8 %collective-permute-start.9 = (bf16[512,256]{1,0:T(8,128)(2,1)S(1)}, bf16[512,256]{1,0:T(8,128)(2,1)S(1)}, u32[]{:S(2)}, u32[]{:S(2)}) collective-permute-start(bf16[512,256]{1,0:T(8,128)(2,1)S(1)} %shard_map.126.refs_0_), channel_id=1, source_target_pairs={{0,28},{4,0},{8,4},{12,8},{16,12},{20,16},{24,20},{28,24},{1,29},{... | collective-permute-start | bytes 786440 | tf_op jit(solution)/shard_map/ppermute | solution.py:26
  139.2 11.8 %collective-permute-start.18 = (bf16[512,256]{1,0:T(8,128)(2,1)S(1)}, bf16[512,256]{1,0:T(8,128)(2,1)S(1)}, u32[]{:S(2)}, u32[]{:S(2)}) collective-permute-start(bf16[512,256]{1,0:T(8,128)(2,1)S(1)} %shard_map.128.refs_0_), channel_id=1, source_target_pairs={{0,28},{4,0},{8,4},{12,8},{16,12},{20,16},{24,20},{28,24},{1,29},{... | collective-permute-start | bytes 786440 | tf_op jit(solution)/shard_map/ppermute | solution.py:26
  140.7 13.7 %collective-permute-start.19 = (bf16[512,256]{1,0:T(8,128)(2,1)S(1)}, bf16[512,256]{1,0:T(8,128)(2,1)S(1)}, u32[]{:S(2)}, u32[]{:S(2)}) collective-permute-start(bf16[512,256]{1,0:T(8,128)(2,1)S(1)} %collective-permute-done.17.refs_1_), channel_id=1, source_target_pairs={{0,4},{4,8},{8,12},{12,16},{16,20},{20,24},{24,28},{28,0},{1,5},{5... | collective-permute-start | bytes 786440 | tf_op jit(solution)/shard_map/ppermute | solution.py:26
  140.7 14.2 %collective-permute-start.8 = (bf16[512,256]{1,0:T(8,128)(2,1)S(1)}, bf16[512,256]{1,0:T(8,128)(2,1)S(1)}, u32[]{:S(2)}, u32[]{:S(2)}) collective-permute-start(bf16[512,256]{1,0:T(8,128)(2,1)S(1)} %shard_map.126.refs_0_), channel_id=1, source_target_pairs={{0,4},{4,8},{8,12},{12,16},{16,20},{20,24},{24,28},{28,0},{1,5},{5... | collective-permute-start | bytes 786440 | tf_op jit(solution)/shard_map/ppermute | solution.py:26
  145.4 11.2 %collective-permute-start.11 = (bf16[512,256]{1,0:T(8,128)(2,1)S(1)}, bf16[512,256]{1,0:T(8,128)(2,1)S(1)}, u32[]{:S(2)}, u32[]{:S(2)}) collective-permute-start(bf16[512,256]{1,0:T(8,128)(2,1)S(1)} %collective-permute-done.9.refs_2_), channel_id=1, source_target_pairs={{0,28},{4,0},{8,4},{12,8},{16,12},{20,16},{24,20},{28,24},{1,29},{... | collective-permute-start | bytes 786440 | tf_op jit(solution)/shard_map/ppermute | solution.py:26
  151.0 11.2 %collective-permute-start.20 = (bf16[512,256]{1,0:T(8,128)(2,1)S(1)}, bf16[512,256]{1,0:T(8,128)(2,1)S(1)}, u32[]{:S(2)}, u32[]{:S(2)}) collective-permute-start(bf16[512,256]{1,0:T(8,128)(2,1)S(1)} %collective-permute-done.18.refs_2_), channel_id=1, source_target_pairs={{0,28},{4,0},{8,4},{12,8},{16,12},{20,16},{24,20},{28,24},{1,29},{... | collective-permute-start | bytes 786440 | tf_op jit(solution)/shard_map/ppermute | solution.py:26
  154.4 11.2 %collective-permute-start.21 = (bf16[512,256]{1,0:T(8,128)(2,1)S(1)}, bf16[512,256]{1,0:T(8,128)(2,1)S(1)}, u32[]{:S(2)}, u32[]{:S(2)}) collective-permute-start(bf16[512,256]{1,0:T(8,128)(2,1)S(1)} %collective-permute-done.19.refs_3_), channel_id=1, source_target_pairs={{0,4},{4,8},{8,12},{12,16},{16,20},{20,24},{24,28},{28,0},{1,5},{5... | collective-permute-start | bytes 786440 | tf_op jit(solution)/shard_map/ppermute | solution.py:26
  154.9 12.5 %collective-permute-start.10 = (bf16[512,256]{1,0:T(8,128)(2,1)S(1)}, bf16[512,256]{1,0:T(8,128)(2,1)S(1)}, u32[]{:S(2)}, u32[]{:S(2)}) collective-permute-start(bf16[512,256]{1,0:T(8,128)(2,1)S(1)} %collective-permute-done.8.refs_1_), channel_id=1, source_target_pairs={{0,4},{4,8},{8,12},{12,16},{16,20},{20,24},{24,28},{28,0},{1,5},{5... | collective-permute-start | bytes 786440 | tf_op jit(solution)/shard_map/ppermute | solution.py:26
  156.6 11.2 %collective-permute-start.13 = (bf16[512,256]{1,0:T(8,128)(2,1)S(1)}, bf16[512,256]{1,0:T(8,128)(2,1)S(1)}, u32[]{:S(2)}, u32[]{:S(2)}) collective-permute-start(bf16[512,256]{1,0:T(8,128)(2,1)S(1)} %collective-permute-done.11.refs_4_), channel_id=1, source_target_pairs={{0,28},{4,0},{8,4},{12,8},{16,12},{20,16},{24,20},{28,24},{1,29},{... | collective-permute-start | bytes 786440 | tf_op jit(solution)/shard_map/ppermute | solution.py:26
  162.2 11.2 %collective-permute-start.22 = (bf16[512,256]{1,0:T(8,128)(2,1)S(1)}, bf16[512,256]{1,0:T(8,128)(2,1)}, u32[]{:S(2)}, u32[]{:S(2)}) collective-permute-start(bf16[512,256]{1,0:T(8,128)(2,1)S(1)} %collective-permute-done.20.refs_4_), channel_id=1, source_target_pairs={{0,28},{4,0},{8,4},{12,8},{16,12},{20,16},{24,20},{28,24},{1,29},{... | collective-permute-start | bytes 786440 | tf_op jit(solution)/shard_map/ppermute | solution.py:26
  165.6 9.6 %collective-permute-start.23 = (bf16[512,256]{1,0:T(8,128)(2,1)S(1)}, bf16[512,256]{1,0:T(8,128)(2,1)}, u32[]{:S(2)}, u32[]{:S(2)}) collective-permute-start(bf16[512,256]{1,0:T(8,128)(2,1)S(1)} %collective-permute-done.21.refs_5_), channel_id=1, source_target_pairs={{0,4},{4,8},{8,12},{12,16},{16,20},{20,24},{24,28},{28,0},{1,5},{5... | collective-permute-start | bytes 786440 | tf_op jit(solution)/shard_map/ppermute | solution.py:26
  167.4 11.7 %collective-permute-start.12 = (bf16[512,256]{1,0:T(8,128)(2,1)S(1)}, bf16[512,256]{1,0:T(8,128)(2,1)S(1)}, u32[]{:S(2)}, u32[]{:S(2)}) collective-permute-start(bf16[512,256]{1,0:T(8,128)(2,1)S(1)} %collective-permute-done.10.refs_3_), channel_id=1, source_target_pairs={{0,4},{4,8},{8,12},{12,16},{16,20},{20,24},{24,28},{28,0},{1,5},{5... | collective-permute-start | bytes 786440 | tf_op jit(solution)/shard_map/ppermute | solution.py:26
  167.8 11.3 %collective-permute-start.14 = (bf16[512,256]{1,0:T(8,128)(2,1)S(1)}, bf16[512,256]{1,0:T(8,128)(2,1)}, u32[]{:S(2)}, u32[]{:S(2)}) collective-permute-start(bf16[512,256]{1,0:T(8,128)(2,1)S(1)} %collective-permute-done.13.refs_6_), channel_id=1, source_target_pairs={{0,28},{4,0},{8,4},{12,8},{16,12},{20,16},{24,20},{28,24},{1,29},{... | collective-permute-start | bytes 786440 | tf_op jit(solution)/shard_map/ppermute | solution.py:26
  (13 other events, 94.0 us)
Sparse Core Ops, SparseCore 0:
  9.9 67.7 all-gather.3
  80.3 48.2 all-gather.5

commit v2 on v1

--- a/solution.py
+++ b/solution.py
@@ -43,7 +43,7 @@
                 ids == side * (half // 64) + own, products[own * 64 : own * 64 + 64], 0.0
             )
     for j in range(out_ref.shape[0]):
-        out_ref[j] = total[:, 128 * j : 128 * j + 128]
+        out_ref[j] = total[:, 128 * j : 128 * j + 128].astype(BF16)
 
 
 def partial_codes(tok, ids, down, after):
@@ -59,7 +59,7 @@
         ]
         + [pl.BlockSpec(memory_space=pl.ANY) for _ in after],
         out_specs=pl.BlockSpec((block // 128, 64, 128), lambda i: (i, 0, 0)),
-        out_shape=jax.ShapeDtypeStruct((rows // 128, 64, 128), F32),
+        out_shape=jax.ShapeDtypeStruct((rows // 128, 64, 128), BF16),
         compiler_params=PARAMS,
         cost_estimate=cost(4.0),
     )(in_hbm(tok), ids, down, *[in_hbm(a) for a in after])
@@ -67,9 +67,9 @@
 
 def sum_kernel(parts_ref, *refs):
     out_ref = refs[-1]
-    total = parts_ref[0]
+    total = parts_ref[0].astype(F32)
     for j in range(1, parts_ref.shape[0]):
-        total = total + parts_ref[j]
+        total = total + parts_ref[j].astype(F32)
     total = total.astype(BF16)
     for j in range(out_ref.shape[0]):
         out_ref[j] = total
@@ -305,13 +305,15 @@
 
 
 def out_kernel(*refs):
-    pieces, (low_ref, high_ref), out_ref = refs[:8], refs[8:10], refs[-1]
+    pieces, (low_ref, high_ref), out_ref = refs[:9], refs[9:11], refs[-1]
     channels = low_ref.shape[2]
+    opposite = jnp.where(pl.program_id(0) == 0, pieces[8][...], pieces[7][...])
+    blocks = [piece[...] for piece in pieces[:7]] + [opposite]
     for side, ref in enumerate((low_ref, high_ref)):
         total = jnp.zeros((out_ref.shape[0], channels), F32)
-        for k, piece in zip((0, 1, 7, 2, 6, 3, 5, 4), pieces):
+        for k, block in zip((0, 1, 7, 2, 6, 3, 5, 4), blocks):
             weight = ref[4 * k : 4 * k + 4].reshape(-1, channels)
-            total = total + jnp.dot(piece[...], weight, preferred_element_type=F32)
+            total = total + jnp.dot(block, weight, preferred_element_type=F32)
         out_ref[:, side * channels : (side + 1) * channels] = total.astype(BF16)
 
 
@@ -320,7 +322,8 @@
     block = rows // 2
     operands = [*pieces, in_hbm(gathered), in_hbm(gathered)]
     in_specs = (
-        [pl.BlockSpec((block, channels), lambda i: (i, 0))] * 8
+        [pl.BlockSpec((block, channels), lambda i: (i, 0))] * 7
+        + [pl.BlockSpec((block, channels), lambda i: (0, 0))] * 2
         + [
             pl.BlockSpec((32, 64, channels), lambda i: (0, 0, 0)),
             pl.BlockSpec((32, 64, channels), lambda i: (0, 1, 0)),
@@ -362,7 +365,7 @@
         out_shape=[jax.ShapeDtypeStruct((rows // 2, depth), BF16)] * 2,
         compiler_params=PARAMS,
         cost_estimate=cost(0.5),
-    )(in_hbm(ahead), in_hbm(back))
+    )(ahead, back)
 
 
 def folding_kernel(rows_ref, after_ref, more_ref, out_ref):
@@ -393,13 +396,13 @@
     return moved(ahead, "tensor", 1), moved(back, "tensor", -1)
 
 
-def ring(block, last):
+def ring(block):
     ahead = back = block
     pieces = [block]
     for _ in range(3):
         ahead, back = both_ways(ahead, back)
         pieces += [ahead, back]
-    return pieces + [moved(ahead if last > 0 else back, "tensor", last)]
+    return pieces + list(both_ways(*halves(ahead, back)))
 
 
 def per_device(
@@ -427,7 +430,7 @@
     f1, b1 = both_ways(tok, tok)
     f2, b2 = both_ways(f1, b1)
     f3, b3 = both_ways(f2, b2)
-    f3_half, b3_half = halves(f3, b3)
+    f3_half, b3_half = halves(in_hbm(f3), in_hbm(b3))
     f4, b4 = both_ways(f3_half, b3_half)
 
     up = adapter_up_maps[0].transpose(1, 0, 2).reshape(-1, channels)
@@ -468,8 +471,8 @@
     mixed_early, rim_early = mixing(place, acc, b4, 4, *shared, 0)
 
     filters = (taps, spectrum, split(forward), split(inverse))
-    gated_early = ring(filtering(mixed_early, rim_in, *filters), 1)
-    gated_late = ring(filtering(mixed_late, rim_early, *filters), -1)
+    gated_early = ring(filtering(mixed_early, rim_in, *filters))
+    gated_late = ring(filtering(mixed_late, rim_early, *filters))
     out = out_projection(gated_early, out_all, None, 0, rows)
     out = out_projection(gated_late, out_all, out, 2, rows)
     return out[None]

time: 191 us -> 190 us (level)
  waiting for transfers between devices: 54 us -> 47.6 us
  starting transfers between devices: 63.2 us -> 65.3 us
    ppermute x22 -> x24, waiting for transfers between devices: 38.7 us -> 33.7 us  [moved(): lax.ppermute(block, axis, [(i, (i + distance) % n) for i in range(n)])]
    ppermute x22 -> x24, starting transfers between devices: 34 us -> 36.3 us  [moved(): lax.ppermute(block, axis, [(i, (i + distance) % n) for i in range(n)])]
    unnamed x33 -> x37, local copies, waits for them, and re-layouts: 6.58 us -> 7.55 us
  transfers between devices with their start and end apart: 29 -> 31, of which waited for: 15 -> 9; matrix products, arithmetic and copies ran while one was open for 2% -> 2% of each run, Pallas kernels for 23% -> 24%
where the time goes in v2:
time: 190 us; the launch traced here: 188 us
  starting transfers between devices  65.3 us (34%)
  Pallas kernels  49.2 us (26%)
  waiting for transfers between devices  47.6 us (25%)
  between operations  13.8 us (7%)
  local copies, waits for them, and re-layouts  10.9 us (6%)
    ppermute x24, starting transfers between devices, moved(): lax.ppermute(block, axis, [(i, (i + distance) % n) for i in range(n)])  36.3 us
    ppermute x24, waiting for transfers between devices, moved(): lax.ppermute(block, axis, [(i, (i + distance) % n) for i in range(n)])  33.7 us
    pallas_call x3, Pallas kernels, projecting(): pl.pallas_call(kernel, grid_spec=pltpu.PrefetchScalarGridSpec(num_scalar_...  15.5 us
    ppermute x1, waiting for transfers between devices, per_device(): lax.ppermute(folded(out_rows, first_acc, spectrum), ('seq', 'tensor'), [(...  12.2 us
    pallas_call x2, Pallas kernels, mixing(): pl.pallas_call(kernel, grid_spec=pltpu.PrefetchScalarGridSpec(num_scalar_...  11.1 us
    ppermute x1, starting transfers between devices, per_device(): rim_in = lax.ppermute(rim_late, 'seq', [(i, i + 1) for i in range(7)])  9.6 us
    all_to_all x1, starting transfers between devices, per_device(): lax.all_to_all(jnp.broadcast_to(adapter_down_maps[0].T[None], (32, rank,...  8.04 us
    pallas_call x2, Pallas kernels, out_projection(): pl.pallas_call(out_kernel, grid=(2,), in_specs=in_specs, out_specs=pl.Blo...  7.66 us
  transfers between devices with their start and end apart: 31, of which 9 were waited for; matrix products, arithmetic and copies ran while one was open for 2% of the time, Pallas kernels for 24%

profile of v2, /device:TPU:1, one launch (start us, length us, event | category | flops | bytes accessed | tf_op | source)
XLA Modules:
  0.0 188.0 jit_solution(7245274625478933084)
XLA Ops:
  7.5 2.5 %collective-permute-start = (bf16[1024,512]{1,0:T(8,128)(2,1)}, bf16[1024,512]{1,0:T(8,128)(2,1)}, u32[]{:S(2)}, u32[]{:S(2)}) collective-permute-start(bf16[1024,512]{1,0:T(8,128)(2,1)} %bitcast.43), channel_id=1, source_target_pairs={{0,4},{4,8},{8,12},{12,16},{16,20},{20,24},{24,28},{28,0},{1,5},{5... | collective-permute-start | bytes 3145736 | tf_op jit(solution)/shard_map/ppermute | solution.py:26
  10.0 4.0 %collective-permute-start.1 = (bf16[1024,512]{1,0:T(8,128)(2,1)}, bf16[1024,512]{1,0:T(8,128)(2,1)}, u32[]{:S(2)}, u32[]{:S(2)}) collective-permute-start(bf16[1024,512]{1,0:T(8,128)(2,1)} %bitcast.44), channel_id=1, source_target_pairs={{0,28},{4,0},{8,4},{12,8},{16,12},{20,16},{24,20},{28,24},{1,29},{... | collective-permute-start | bytes 3145736 | tf_op jit(solution)/shard_map/ppermute | solution.py:26
  16.5 8.0 %all-to-all-start = ((bf16[32,64,512]{2,1,0:T(8,128)(2,1)}), bf16[32,64,512]{2,1,0:T(8,128)(2,1)S(1)}, u32[]{:S(2)}, u32[]{:S(2)}) async-start(bf16[32,64,512]{2,1,0:T(8,128)(2,1)} %broadcast_in_dim.4), calls=%async_computation | async-start | bytes 4194304 | tf_op jit(solution)/shard_map/all_to_all | solution.py:439
  24.6 12.5 %collective-permute-done.refs_1_ = bf16[1024,512]{1,0:T(8,128)(2,1)} collective-permute-done((bf16[1024,512]{1,0:T(8,128)(2,1)}, bf16[1024,512]{1,0:T(8,128)(2,1)}, u32[]{:S(2)}, u32[]{:S(2)}) %collective-permute-start) | collective-permute-done | bytes 1048608 | tf_op jit(solution)/shard_map/ppermute | solution.py:26
  37.2 2.7 %collective-permute-start.3 = (bf16[1024,512]{1,0:T(8,128)(2,1)}, bf16[1024,512]{1,0:T(8,128)(2,1)}, u32[]{:S(2)}, u32[]{:S(2)}) collective-permute-start(bf16[1024,512]{1,0:T(8,128)(2,1)} %collective-permute-done.1.refs_2_), channel_id=1, source_target_pairs={{0,28},{4,0},{8,4},{12,8},{16,12},{20,16},{24,20},{28,24},{1,29},{... | collective-permute-start | bytes 3145736 | tf_op jit(solution)/shard_map/ppermute | solution.py:26
  41.9 5.5 %shard_map.118.refs_0_.after_ref = f32[1024,768]{1,0:T(8,128)S(1)} custom-call(s32[1]{0:T(128)} %bitcast.place_ref, bf16[1024,512]{1,0:T(8,128)(2,1)} %bitcast.45, bf16[1024,512]{1,0:T(8,128)(2,1)} %collective-permute-done.refs_1_, bf16[1024,512]{1,0:T(8,128)(2,1)} %collective-permute-done.1.refs_2_, bf16[3,4096,256]{2,1,0:T(8,128)(2,1)} %bitcast.30, ...), custom_call_target="tpu_custom_call" | custom-call | flops 9216000000 | bytes 9216000 | tf_op jit(solution)/shard_map/pallas_call | solution.py:120
  51.2 12.2 %collective-permute-done.16 = bf16[128,256]{1,0:T(8,128)(2,1)S(1)} collective-permute-done((bf16[128,256]{1,0:T(8,128)(2,1)S(1)}, bf16[128,256]{1,0:T(8,128)(2,1)S(1)}, u32[]{:S(2)}, u32[]{:S(2)}) %collective-permute-start.16) | collective-permute-done | bytes 65568 | tf_op jit(solution)/shard_map/ppermute | solution.py:461
  64.2 2.7 %collective-permute-start.5 = (bf16[1024,512]{1,0:T(8,128)(2,1)}, bf16[1024,512]{1,0:T(8,128)(2,1)}, u32[]{:S(2)}, u32[]{:S(2)}) collective-permute-start(bf16[1024,512]{1,0:T(8,128)(2,1)} %collective-permute-done.3.refs_2_), channel_id=1, source_target_pairs={{0,28},{4,0},{8,4},{12,8},{16,12},{20,16},{24,20},{28,24},{1,29},{... | collective-permute-start | bytes 3145736 | tf_op jit(solution)/shard_map/ppermute | solution.py:26
  66.9 5.0 %shard_map.122 = bf16[8,64,128]{2,1,0:T(8,128)(2,1)} custom-call(bf16[1024,512]{1,0:T(8,128)(2,1)} %bitcast.46, s32[1,1024]{1,0:T(1,128)S(1)} %bitcast.24, bf16[2048,512]{1,0:T(8,128)(2,1)S(1)} %bitcast.19, f32[1024,768]{1,0:T(8,128)} %copy-done.12, bf16[1024,512]{1,0:T(8,128)(2,1)} %copy-done.17, bf16[1024,512]{1,0:T(8,128)(2,1)} %collective-permute-done.3.refs_2_), custom_call_target="tpu_custom_call" | custom-call | flops 8000000000 | bytes 8000000 | tf_op jit(solution)/shard_map/pallas_call | solution.py:52
  71.9 4.7 %all-to-all-start.1 = ((bf16[8,64,128]{2,1,0:T(8,128)(2,1)}), bf16[8,64,128]{2,1,0:T(8,128)(2,1)S(1)}, u32[]{:S(2)}, u32[]{:S(2)}) async-start(bf16[8,64,128]{2,1,0:T(8,128)(2,1)} %shard_map.122), calls=%async_computation.1 | async-start | bytes 262144 | tf_op jit(solution)/shard_map/all_to_all | solution.py:448
  76.5 5.0 %shard_map.119.refs_0_ = f32[1024,768]{1,0:T(8,128)S(1)} custom-call(s32[1]{0:T(128)} %bitcast.place_ref, f32[1024,768]{1,0:T(8,128)} %copy-done.12, bf16[1024,512]{1,0:T(8,128)(2,1)} %copy-done.17, bf16[1024,512]{1,0:T(8,128)(2,1)} %collective-permute-done.3.refs_2_, bf16[3,4096,256]{2,1,0:T(8,128)(2,1)} %bitcast.33, bf16[3,4096,256]{2,1,0:T(8,128)(2,1)} %bitcast.34), custom_call_target="tpu_custom_call" | custom-call | flops 9216000000 | bytes 9216000 | tf_op jit(solution)/shard_map/pallas_call | solution.py:120
  83.2 7.3 %collective-permute-done.4.refs_1_.ahead_ref = bf16[1024,512]{1,0:T(8,128)(2,1)} collective-permute-done((bf16[1024,512]{1,0:T(8,128)(2,1)S(1)}, bf16[1024,512]{1,0:T(8,128)(2,1)}, u32[]{:S(2)}, u32[]{:S(2)}) %collective-permute-start.4) | collective-permute-done | bytes 1048608 | tf_op jit(solution)/shard_map/ppermute | solution.py:26
  94.8 4.6 %all-to-all-start.2 = ((bf16[8,64,128]{2,1,0:T(8,128)(2,1)}), bf16[8,64,128]{2,1,0:T(8,128)(2,1)S(1)}, u32[]{:S(2)}, u32[]{:S(2)}) async-start(bf16[8,64,128]{2,1,0:T(8,128)(2,1)} %shard_map.123), calls=%async_computation.2 | async-start | bytes 262144 | tf_op jit(solution)/shard_map/all_to_all | solution.py:450
  99.4 5.0 %shard_map.120.acc_ref = f32[1024,768]{1,0:T(8,128)S(1)} custom-call(s32[1]{0:T(128)} %bitcast.place_ref, f32[1024,768]{1,0:T(8,128)} %copy-done, bf16[1024,512]{1,0:T(8,128)(2,1)} %collective-permute-done.4.refs_1_.ahead_ref, bf16[1024,512]{1,0:T(8,128)(2,1)} %collective-permute-done.5.refs_2_.back_ref, bf16[3,4096,256]{2,1,0:T(8,128)(2,1)} %bitcast.35, ...), custom_call_target="tpu_custom_call" | custom-call | flops 9216000000 | bytes 9216000 | tf_op jit(solution)/shard_map/pallas_call | solution.py:120
  107.8 5.5 %shard_map.124 = (bf16[512,768]{1,0:T(8,128)(2,1)S(1)}, bf16[176,256]{1,0:T(8,128)(2,1)S(1)}) custom-call(s32[1]{0:T(128)} %bitcast.place_ref, f32[1024,768]{1,0:T(8,128)} %copy-done.13, bf16[512,512]{1,0:T(8,128)(2,1)S(1)} %collective-permute-done.6.last_ref, bf16[3,4096,256]{2,1,0:T(8,128)(2,1)} %bitcast.37, ...), custom_call_target="tpu_custom_call" | custom-call | flops 8000000000 | bytes 8000000 | tf_op jit(solution)/shard_map/pallas_call | solution.py:187
  113.4 9.6 %collective-permute-start.17 = (bf16[176,256]{1,0:T(8,128)(2,1)S(1)}, bf16[176,256]{1,0:T(8,128)(2,1)S(1)}, u32[]{:S(2)}, u32[]{:S(2)}) collective-permute-start(bf16[176,256]{1,0:T(8,128)(2,1)S(1)} %get-tuple-element.34), channel_id=1, source_target_pairs={{0,32},{32,64},{64,96},{96,128},{128,160},{160,192},{192,224},{1,3... | collective-permute-start | bytes 270344 | tf_op jit(solution)/shard_map/ppermute | solution.py:470
  123.0 5.6 %shard_map.125 = (bf16[512,768]{1,0:T(8,128)(2,1)S(1)}, bf16[176,256]{1,0:T(8,128)(2,1)S(1)}) custom-call(s32[1]{0:T(128)} %bitcast.place_ref, f32[1024,768]{1,0:T(8,128)} %copy-done.13, bf16[512,512]{1,0:T(8,128)(2,1)S(1)} %collective-permute-done.7.last_ref, bf16[3,4096,256]{2,1,0:T(8,128)(2,1)} %bitcast.38, ...), custom_call_target="tpu_custom_call" | custom-call | flops 8000000000 | bytes 8000000 | tf_op jit(solution)/shard_map/pallas_call | solution.py:187
  128.6 3.3 %shard_map.129.refs_0_ = bf16[512,256]{1,0:T(8,128)(2,1)S(1)} custom-call(bf16[512,768]{1,0:T(8,128)(2,1)S(1)} %get-tuple-element.33.mixed_ref, bf16[176,256]{1,0:T(8,128)(2,1)S(1)} %collective-permute-done.17.rim_ref, f32[3,7,256]{2,1,0:T(8,128)S(1)} %bitcast.22, f32[384,256]{1,0:T(8,128)S(1)} %copy-done.3, bf16[256,256]{1,0:T(8,128)(2,1)S(1)} %copy-done.8, ...), custom_call_target="tpu_custom_call" | custom-call | flops 7000000000 | bytes 7000000 | tf_op jit(solution)/shard_map/pallas_call | solution.py:292
  134.7 3.2 %shard_map.126.refs_0_ = bf16[512,256]{1,0:T(8,128)(2,1)S(1)} custom-call(bf16[512,768]{1,0:T(8,128)(2,1)S(1)} %get-tuple-element.29.mixed_ref, bf16[176,256]{1,0:T(8,128)(2,1)S(1)} %get-tuple-element.30.rim_ref, f32[3,7,256]{2,1,0:T(8,128)S(1)} %bitcast.23, f32[384,256]{1,0:T(8,128)S(1)} %copy-done.3, bf16[256,256]{1,0:T(8,128)(2,1)S(1)} %copy-done.8, ...), custom_call_target="tpu_custom_call" | custom-call | flops 7000000000 | bytes 7000000 | tf_op jit(solution)/shard_map/pallas_call | solution.py:292
  138.0 2.7 %collective-permute-start.9 = (bf16[512,256]{1,0:T(8,128)(2,1)S(1)}, bf16[512,256]{1,0:T(8,128)(2,1)S(1)}, u32[]{:S(2)}, u32[]{:S(2)}) collective-permute-start(bf16[512,256]{1,0:T(8,128)(2,1)S(1)} %shard_map.126.refs_0_), channel_id=1, source_target_pairs={{0,28},{4,0},{8,4},{12,8},{16,12},{20,16},{24,20},{28,24},{1,29},{... | collective-permute-start | bytes 786440 | tf_op jit(solution)/shard_map/ppermute | solution.py:26
  140.7 2.7 %collective-permute-start.21 = (bf16[512,256]{1,0:T(8,128)(2,1)S(1)}, bf16[512,256]{1,0:T(8,128)(2,1)S(1)}, u32[]{:S(2)}, u32[]{:S(2)}) collective-permute-start(bf16[512,256]{1,0:T(8,128)(2,1)S(1)} %collective-permute-done.19.refs_2_), channel_id=1, source_target_pairs={{0,28},{4,0},{8,4},{12,8},{16,12},{20,16},{24,20},{28,24},{1,29},{... | collective-permute-start | bytes 786440 | tf_op jit(solution)/shard_map/ppermute | solution.py:26
  143.4 4.2 %collective-permute-done.8.refs_1_ = bf16[512,256]{1,0:T(8,128)(2,1)S(1)} collective-permute-done((bf16[512,256]{1,0:T(8,128)(2,1)S(1)}, bf16[512,256]{1,0:T(8,128)(2,1)S(1)}, u32[]{:S(2)}, u32[]{:S(2)}) %collective-permute-start.8) | collective-permute-done | bytes 262176 | tf_op jit(solution)/shard_map/ppermute | solution.py:26
  147.6 2.7 %collective-permute-start.11 = (bf16[512,256]{1,0:T(8,128)(2,1)S(1)}, bf16[512,256]{1,0:T(8,128)(2,1)S(1)}, u32[]{:S(2)}, u32[]{:S(2)}) collective-permute-start(bf16[512,256]{1,0:T(8,128)(2,1)S(1)} %collective-permute-done.9.refs_2_), channel_id=1, source_target_pairs={{0,28},{4,0},{8,4},{12,8},{16,12},{20,16},{24,20},{28,24},{1,29},{... | collective-permute-start | bytes 786440 | tf_op jit(solution)/shard_map/ppermute | solution.py:26
  150.3 2.9 %collective-permute-done.20.refs_3_ = bf16[512,256]{1,0:T(8,128)(2,1)S(1)} collective-permute-done((bf16[512,256]{1,0:T(8,128)(2,1)S(1)}, bf16[512,256]{1,0:T(8,128)(2,1)S(1)}, u32[]{:S(2)}, u32[]{:S(2)}) %collective-permute-start.20) | collective-permute-done | bytes 262176 | tf_op jit(solution)/shard_map/ppermute | solution.py:26
  153.2 2.7 %collective-permute-start.23 = (bf16[512,256]{1,0:T(8,128)(2,1)S(1)}, bf16[512,256]{1,0:T(8,128)(2,1)S(1)}, u32[]{:S(2)}, u32[]{:S(2)}) collective-permute-start(bf16[512,256]{1,0:T(8,128)(2,1)S(1)} %collective-permute-done.21.refs_4_), channel_id=1, source_target_pairs={{0,28},{4,0},{8,4},{12,8},{16,12},{20,16},{24,20},{28,24},{1,29},{... | collective-permute-start | bytes 786440 | tf_op jit(solution)/shard_map/ppermute | solution.py:26
  155.9 2.9 %collective-permute-done.10.refs_3_ = bf16[512,256]{1,0:T(8,128)(2,1)S(1)} collective-permute-done((bf16[512,256]{1,0:T(8,128)(2,1)S(1)}, bf16[512,256]{1,0:T(8,128)(2,1)S(1)}, u32[]{:S(2)}, u32[]{:S(2)}) %collective-permute-start.10) | collective-permute-done | bytes 262176 | tf_op jit(solution)/shard_map/ppermute | solution.py:26
  158.8 2.7 %collective-permute-start.13 = (bf16[512,256]{1,0:T(8,128)(2,1)S(1)}, bf16[512,256]{1,0:T(8,128)(2,1)S(1)}, u32[]{:S(2)}, u32[]{:S(2)}) collective-permute-start(bf16[512,256]{1,0:T(8,128)(2,1)S(1)} %collective-permute-done.11.refs_4_), channel_id=1, source_target_pairs={{0,28},{4,0},{8,4},{12,8},{16,12},{20,16},{24,20},{28,24},{1,29},{... | collective-permute-start | bytes 786440 | tf_op jit(solution)/shard_map/ppermute | solution.py:26
  161.5 2.9 %collective-permute-done.22.ahead_ref.refs_5_ = bf16[512,256]{1,0:T(8,128)(2,1)S(1)} collective-permute-done((bf16[512,256]{1,0:T(8,128)(2,1)S(1)}, bf16[512,256]{1,0:T(8,128)(2,1)S(1)}, u32[]{:S(2)}, u32[]{:S(2)}) %collective-permute-start.22) | collective-permute-done | bytes 262176 | tf_op jit(solution)/shard_map/ppermute | solution.py:26
  165.2 2.7 %collective-permute-start.25 = (bf16[256,256]{1,0:T(8,128)(2,1)}, bf16[256,256]{1,0:T(8,128)(2,1)}, u32[]{:S(2)}, u32[]{:S(2)}) collective-permute-start(bf16[256,256]{1,0:T(8,128)(2,1)} %get-tuple-element.36), channel_id=1, source_target_pairs={{0,28},{4,0},{8,4},{12,8},{16,12},{20,16},{24,20},{28,24},{1,29},{... | collective-permute-start | bytes 393224 | tf_op jit(solution)/shard_map/ppermute | solution.py:26
  169.5 3.0 %collective-permute-start.15 = (bf16[256,256]{1,0:T(8,128)(2,1)}, bf16[256,256]{1,0:T(8,128)(2,1)}, u32[]{:S(2)}, u32[]{:S(2)}) collective-permute-start(bf16[256,256]{1,0:T(8,128)(2,1)} %get-tuple-element.32), channel_id=1, source_target_pairs={{0,28},{4,0},{8,4},{12,8},{16,12},{20,16},{24,20},{28,24},{1,29},{... | collective-permute-start | bytes 393224 | tf_op jit(solution)/shard_map/ppermute | solution.py:26
  173.5 3.8 %shard_map.131.refs_11_ = bf16[1024,512]{1,0:T(8,128)(2,1)} custom-call(bf16[512,256]{1,0:T(8,128)(2,1)S(1)} %shard_map.129.refs_0_, bf16[512,256]{1,0:T(8,128)(2,1)S(1)} %collective-permute-done.18.refs_1_, bf16[512,256]{1,0:T(8,128)(2,1)S(1)} %collective-permute-done.19.refs_2_, bf16[512,256]{1,0:T(8,128)(2,1)S(1)} %collective-permute-done.20.refs_3_, ...), custom_call_target="tpu_custom_call" | custom-call | flops 4600000000 | bytes 4600000 | tf_op jit(solution)/shard_map/pallas_call | solution.py:337
  177.3 3.8 %shard_map.132 = bf16[1024,512]{1,0:T(8,128)(2,1)} custom-call(bf16[512,256]{1,0:T(8,128)(2,1)S(1)} %shard_map.126.refs_0_, bf16[512,256]{1,0:T(8,128)(2,1)S(1)} %collective-permute-done.8.refs_1_, bf16[512,256]{1,0:T(8,128)(2,1)S(1)} %collective-permute-done.9.refs_2_, ...), custom_call_target="tpu_custom_call", output_to_operand_aliasing={{}: (11, {})} | custom-call | flops 4600000000 | bytes 4600000 | tf_op jit(solution)/shard_map/pallas_call | solution.py:337
  (89 shorter events, 25.5 us)
Async XLA Ops:
  6.5 101.3 %all-gather.4.cloned.1.call-start = ((), (), s32[]{:S(2)}) async-start(), calls=%async_computation.3 | async-start | bytes 3244032 | tf_op jit(solution)/shard_map/all_gather | solution.py:437
  7.5 29.7 %collective-permute-start = (bf16[1024,512]{1,0:T(8,128)(2,1)}, bf16[1024,512]{1,0:T(8,128)(2,1)}, u32[]{:S(2)}, u32[]{:S(2)}) collective-permute-start(bf16[1024,512]{1,0:T(8,128)(2,1)} %bitcast.43), channel_id=1, source_target_pairs={{0,4},{4,8},{8,12},{12,16},{16,20},{20,24},{24,28},{28,0},{1,5},{5... | collective-permute-start | bytes 3145736 | tf_op jit(solution)/shard_map/ppermute | solution.py:26
  10.0 27.1 %collective-permute-start.1 = (bf16[1024,512]{1,0:T(8,128)(2,1)}, bf16[1024,512]{1,0:T(8,128)(2,1)}, u32[]{:S(2)}, u32[]{:S(2)}) collective-permute-start(bf16[1024,512]{1,0:T(8,128)(2,1)} %bitcast.44), channel_id=1, source_target_pairs={{0,28},{4,0},{8,4},{12,8},{16,12},{20,16},{24,20},{28,24},{1,29},{... | collective-permute-start | bytes 3145736 | tf_op jit(solution)/shard_map/ppermute | solution.py:26
  14.0 25.8 %copy-start.14 = (f32[384,128]{1,0:T(8,128)S(1)}, f32[384,128]{1,0:T(8,128)}, u32[]{:S(2)}) copy-start(f32[384,128]{1,0:T(8,128)} %constant.69.clone) | copy-start | bytes 589828
  16.5 50.4 %all-to-all-start = ((bf16[32,64,512]{2,1,0:T(8,128)(2,1)}), bf16[32,64,512]{2,1,0:T(8,128)(2,1)S(1)}, u32[]{:S(2)}, u32[]{:S(2)}) async-start(bf16[32,64,512]{2,1,0:T(8,128)(2,1)} %broadcast_in_dim.4), calls=%async_computation | async-start | bytes 4194304 | tf_op jit(solution)/shard_map/all_to_all | solution.py:439
  24.5 148.0 %all-gather.6.cloned.1.call-start = ((), (), s32[]{:S(2)}) async-start(), calls=%async_computation.4 | async-start | bytes 2162688 | tf_op jit(solution)/shard_map/all_gather | solution.py:466
  37.2 26.9 %collective-permute-start.2 = (bf16[1024,512]{1,0:T(8,128)(2,1)}, bf16[1024,512]{1,0:T(8,128)(2,1)S(1)}, u32[]{:S(2)}, u32[]{:S(2)}) collective-permute-start(bf16[1024,512]{1,0:T(8,128)(2,1)} %collective-permute-done.refs_1_), channel_id=1, source_target_pairs={{0,4},{4,8},{8,12},{12,16},{16,20},{20,24},{24,28},{28,0},{1,5},{5... | collective-permute-start | bytes 3145736 | tf_op jit(solution)/shard_map/ppermute | solution.py:26
  37.2 27.0 %collective-permute-start.3 = (bf16[1024,512]{1,0:T(8,128)(2,1)}, bf16[1024,512]{1,0:T(8,128)(2,1)}, u32[]{:S(2)}, u32[]{:S(2)}) collective-permute-start(bf16[1024,512]{1,0:T(8,128)(2,1)} %collective-permute-done.1.refs_2_), channel_id=1, source_target_pairs={{0,28},{4,0},{8,4},{12,8},{16,12},{20,16},{24,20},{28,24},{1,29},{... | collective-permute-start | bytes 3145736 | tf_op jit(solution)/shard_map/ppermute | solution.py:26
  49.1 14.3 %collective-permute-start.16 = (bf16[128,256]{1,0:T(8,128)(2,1)S(1)}, bf16[128,256]{1,0:T(8,128)(2,1)S(1)}, u32[]{:S(2)}, u32[]{:S(2)}) collective-permute-start(bf16[128,256]{1,0:T(8,128)(2,1)S(1)} %shard_map.128), channel_id=1, source_target_pairs={{0,0},{4,4},{8,8},{12,12},{16,16},{20,20},{24,24},{28,28},{32,36},... | collective-permute-start | bytes 196616 | tf_op jit(solution)/shard_map/ppermute | solution.py:461
  64.1 26.4 %collective-permute-start.4 = (bf16[1024,512]{1,0:T(8,128)(2,1)S(1)}, bf16[1024,512]{1,0:T(8,128)(2,1)}, u32[]{:S(2)}, u32[]{:S(2)}) collective-permute-start(bf16[1024,512]{1,0:T(8,128)(2,1)S(1)} %collective-permute-done.2.refs_1_), channel_id=1, source_target_pairs={{0,4},{4,8},{8,12},{12,16},{16,20},{20,24},{24,28},{28,0},{1,5},{5... | collective-permute-start | bytes 3145736 | tf_op jit(solution)/shard_map/ppermute | solution.py:26
  64.2 26.3 %collective-permute-start.5 = (bf16[1024,512]{1,0:T(8,128)(2,1)}, bf16[1024,512]{1,0:T(8,128)(2,1)}, u32[]{:S(2)}, u32[]{:S(2)}) collective-permute-start(bf16[1024,512]{1,0:T(8,128)(2,1)} %collective-permute-done.3.refs_2_), channel_id=1, source_target_pairs={{0,28},{4,0},{8,4},{12,8},{16,12},{20,16},{24,20},{28,24},{1,29},{... | collective-permute-start | bytes 3145736 | tf_op jit(solution)/shard_map/ppermute | solution.py:26
  71.9 22.2 %all-to-all-start.1 = ((bf16[8,64,128]{2,1,0:T(8,128)(2,1)}), bf16[8,64,128]{2,1,0:T(8,128)(2,1)S(1)}, u32[]{:S(2)}, u32[]{:S(2)}) async-start(bf16[8,64,128]{2,1,0:T(8,128)(2,1)} %shard_map.122), calls=%async_computation.1 | async-start | bytes 262144 | tf_op jit(solution)/shard_map/all_to_all | solution.py:448
  91.8 31.2 %collective-permute-start.7 = (bf16[512,512]{1,0:T(8,128)(2,1)S(1)}, bf16[512,512]{1,0:T(8,128)(2,1)S(1)}, u32[]{:S(2)}, u32[]{:S(2)}) collective-permute-start(bf16[512,512]{1,0:T(8,128)(2,1)S(1)} %get-tuple-element.28.refs_2_), channel_id=1, source_target_pairs={{0,28},{4,0},{8,4},{12,8},{16,12},{20,16},{24,20},{28,24},{1,29},{... | collective-permute-start | bytes 1572872 | tf_op jit(solution)/shard_map/ppermute | solution.py:26
  94.1 13.7 %collective-permute-start.6 = (bf16[512,512]{1,0:T(8,128)(2,1)S(1)}, bf16[512,512]{1,0:T(8,128)(2,1)S(1)}, u32[]{:S(2)}, u32[]{:S(2)}) collective-permute-start(bf16[512,512]{1,0:T(8,128)(2,1)S(1)} %get-tuple-element.27.refs_1_), channel_id=1, source_target_pairs={{0,4},{4,8},{8,12},{12,16},{16,20},{20,24},{24,28},{28,0},{1,5},{5... | collective-permute-start | bytes 1572872 | tf_op jit(solution)/shard_map/ppermute | solution.py:26
  94.8 13.0 %all-to-all-start.2 = ((bf16[8,64,128]{2,1,0:T(8,128)(2,1)}), bf16[8,64,128]{2,1,0:T(8,128)(2,1)S(1)}, u32[]{:S(2)}, u32[]{:S(2)}) async-start(bf16[8,64,128]{2,1,0:T(8,128)(2,1)} %shard_map.123), calls=%async_computation.2 | async-start | bytes 262144 | tf_op jit(solution)/shard_map/all_to_all | solution.py:450
  113.4 15.2 %collective-permute-start.17 = (bf16[176,256]{1,0:T(8,128)(2,1)S(1)}, bf16[176,256]{1,0:T(8,128)(2,1)S(1)}, u32[]{:S(2)}, u32[]{:S(2)}) collective-permute-start(bf16[176,256]{1,0:T(8,128)(2,1)S(1)} %get-tuple-element.34), channel_id=1, source_target_pairs={{0,32},{32,64},{64,96},{96,128},{128,160},{160,192},{192,224},{1,3... | collective-permute-start | bytes 270344 | tf_op jit(solution)/shard_map/ppermute | solution.py:470
  131.9 8.8 %collective-permute-start.18 = (bf16[512,256]{1,0:T(8,128)(2,1)S(1)}, bf16[512,256]{1,0:T(8,128)(2,1)S(1)}, u32[]{:S(2)}, u32[]{:S(2)}) collective-permute-start(bf16[512,256]{1,0:T(8,128)(2,1)S(1)} %shard_map.129.refs_0_), channel_id=1, source_target_pairs={{0,4},{4,8},{8,12},{12,16},{16,20},{20,24},{24,28},{28,0},{1,5},{5... | collective-permute-start | bytes 786440 | tf_op jit(solution)/shard_map/ppermute | solution.py:26
  133.0 7.7 %collective-permute-start.19 = (bf16[512,256]{1,0:T(8,128)(2,1)S(1)}, bf16[512,256]{1,0:T(8,128)(2,1)S(1)}, u32[]{:S(2)}, u32[]{:S(2)}) collective-permute-start(bf16[512,256]{1,0:T(8,128)(2,1)S(1)} %shard_map.129.refs_0_), channel_id=1, source_target_pairs={{0,28},{4,0},{8,4},{12,8},{16,12},{20,16},{24,20},{28,24},{1,29},{... | collective-permute-start | bytes 786440 | tf_op jit(solution)/shard_map/ppermute | solution.py:26
  137.9 9.7 %collective-permute-start.8 = (bf16[512,256]{1,0:T(8,128)(2,1)S(1)}, bf16[512,256]{1,0:T(8,128)(2,1)S(1)}, u32[]{:S(2)}, u32[]{:S(2)}) collective-permute-start(bf16[512,256]{1,0:T(8,128)(2,1)S(1)} %shard_map.126.refs_0_), channel_id=1, source_target_pairs={{0,4},{4,8},{8,12},{12,16},{16,20},{20,24},{24,28},{28,0},{1,5},{5... | collective-permute-start | bytes 786440 | tf_op jit(solution)/shard_map/ppermute | solution.py:26
  138.0 9.6 %collective-permute-start.9 = (bf16[512,256]{1,0:T(8,128)(2,1)S(1)}, bf16[512,256]{1,0:T(8,128)(2,1)S(1)}, u32[]{:S(2)}, u32[]{:S(2)}) collective-permute-start(bf16[512,256]{1,0:T(8,128)(2,1)S(1)} %shard_map.126.refs_0_), channel_id=1, source_target_pairs={{0,28},{4,0},{8,4},{12,8},{16,12},{20,16},{24,20},{28,24},{1,29},{... | collective-permute-start | bytes 786440 | tf_op jit(solution)/shard_map/ppermute | solution.py:26
  140.7 12.5 %collective-permute-start.20 = (bf16[512,256]{1,0:T(8,128)(2,1)S(1)}, bf16[512,256]{1,0:T(8,128)(2,1)S(1)}, u32[]{:S(2)}, u32[]{:S(2)}) collective-permute-start(bf16[512,256]{1,0:T(8,128)(2,1)S(1)} %collective-permute-done.18.refs_1_), channel_id=1, source_target_pairs={{0,4},{4,8},{8,12},{12,16},{16,20},{20,24},{24,28},{28,0},{1,5},{5... | collective-permute-start | bytes 786440 | tf_op jit(solution)/shard_map/ppermute | solution.py:26
  140.7 12.5 %collective-permute-start.21 = (bf16[512,256]{1,0:T(8,128)(2,1)S(1)}, bf16[512,256]{1,0:T(8,128)(2,1)S(1)}, u32[]{:S(2)}, u32[]{:S(2)}) collective-permute-start(bf16[512,256]{1,0:T(8,128)(2,1)S(1)} %collective-permute-done.19.refs_2_), channel_id=1, source_target_pairs={{0,28},{4,0},{8,4},{12,8},{16,12},{20,16},{24,20},{28,24},{1,29},{... | collective-permute-start | bytes 786440 | tf_op jit(solution)/shard_map/ppermute | solution.py:26
  147.6 11.2 %collective-permute-start.10 = (bf16[512,256]{1,0:T(8,128)(2,1)S(1)}, bf16[512,256]{1,0:T(8,128)(2,1)S(1)}, u32[]{:S(2)}, u32[]{:S(2)}) collective-permute-start(bf16[512,256]{1,0:T(8,128)(2,1)S(1)} %collective-permute-done.8.refs_1_), channel_id=1, source_target_pairs={{0,4},{4,8},{8,12},{12,16},{16,20},{20,24},{24,28},{28,0},{1,5},{5... | collective-permute-start | bytes 786440 | tf_op jit(solution)/shard_map/ppermute | solution.py:26
  147.6 11.2 %collective-permute-start.11 = (bf16[512,256]{1,0:T(8,128)(2,1)S(1)}, bf16[512,256]{1,0:T(8,128)(2,1)S(1)}, u32[]{:S(2)}, u32[]{:S(2)}) collective-permute-start(bf16[512,256]{1,0:T(8,128)(2,1)S(1)} %collective-permute-done.9.refs_2_), channel_id=1, source_target_pairs={{0,28},{4,0},{8,4},{12,8},{16,12},{20,16},{24,20},{28,24},{1,29},{... | collective-permute-start | bytes 786440 | tf_op jit(solution)/shard_map/ppermute | solution.py:26
  153.2 11.2 %collective-permute-start.22 = (bf16[512,256]{1,0:T(8,128)(2,1)S(1)}, bf16[512,256]{1,0:T(8,128)(2,1)S(1)}, u32[]{:S(2)}, u32[]{:S(2)}) collective-permute-start(bf16[512,256]{1,0:T(8,128)(2,1)S(1)} %collective-permute-done.20.refs_3_), channel_id=1, source_target_pairs={{0,4},{4,8},{8,12},{12,16},{16,20},{20,24},{24,28},{28,0},{1,5},{5... | collective-permute-start | bytes 786440 | tf_op jit(solution)/shard_map/ppermute | solution.py:26
  153.2 11.2 %collective-permute-start.23 = (bf16[512,256]{1,0:T(8,128)(2,1)S(1)}, bf16[512,256]{1,0:T(8,128)(2,1)S(1)}, u32[]{:S(2)}, u32[]{:S(2)}) collective-permute-start(bf16[512,256]{1,0:T(8,128)(2,1)S(1)} %collective-permute-done.21.refs_4_), channel_id=1, source_target_pairs={{0,28},{4,0},{8,4},{12,8},{16,12},{20,16},{24,20},{28,24},{1,29},{... | collective-permute-start | bytes 786440 | tf_op jit(solution)/shard_map/ppermute | solution.py:26
  158.8 10.0 %collective-permute-start.12 = (bf16[512,256]{1,0:T(8,128)(2,1)S(1)}, bf16[512,256]{1,0:T(8,128)(2,1)S(1)}, u32[]{:S(2)}, u32[]{:S(2)}) collective-permute-start(bf16[512,256]{1,0:T(8,128)(2,1)S(1)} %collective-permute-done.10.refs_3_), channel_id=1, source_target_pairs={{0,4},{4,8},{8,12},{12,16},{16,20},{20,24},{24,28},{28,0},{1,5},{5... | collective-permute-start | bytes 786440 | tf_op jit(solution)/shard_map/ppermute | solution.py:26
  158.8 9.9 %collective-permute-start.13 = (bf16[512,256]{1,0:T(8,128)(2,1)S(1)}, bf16[512,256]{1,0:T(8,128)(2,1)S(1)}, u32[]{:S(2)}, u32[]{:S(2)}) collective-permute-start(bf16[512,256]{1,0:T(8,128)(2,1)S(1)} %collective-permute-done.11.refs_4_), channel_id=1, source_target_pairs={{0,28},{4,0},{8,4},{12,8},{16,12},{20,16},{24,20},{28,24},{1,29},{... | collective-permute-start | bytes 786440 | tf_op jit(solution)/shard_map/ppermute | solution.py:26
  165.2 7.3 %collective-permute-start.24 = (bf16[256,256]{1,0:T(8,128)(2,1)}, bf16[256,256]{1,0:T(8,128)(2,1)}, u32[]{:S(2)}, u32[]{:S(2)}) collective-permute-start(bf16[256,256]{1,0:T(8,128)(2,1)} %get-tuple-element.35), channel_id=1, source_target_pairs={{0,4},{4,8},{8,12},{12,16},{16,20},{20,24},{24,28},{28,0},{1,5},{5... | collective-permute-start | bytes 393224 | tf_op jit(solution)/shard_map/ppermute | solution.py:26
  165.2 7.3 %collective-permute-start.25 = (bf16[256,256]{1,0:T(8,128)(2,1)}, bf16[256,256]{1,0:T(8,128)(2,1)}, u32[]{:S(2)}, u32[]{:S(2)}) collective-permute-start(bf16[256,256]{1,0:T(8,128)(2,1)} %get-tuple-element.36), channel_id=1, source_target_pairs={{0,28},{4,0},{8,4},{12,8},{16,12},{20,16},{24,20},{28,24},{1,29},{... | collective-permute-start | bytes 393224 | tf_op jit(solution)/shard_map/ppermute | solution.py:26
  169.5 7.8 %collective-permute-start.14 = (bf16[256,256]{1,0:T(8,128)(2,1)}, bf16[256,256]{1,0:T(8,128)(2,1)S(1)}, u32[]{:S(2)}, u32[]{:S(2)}) collective-permute-start(bf16[256,256]{1,0:T(8,128)(2,1)} %get-tuple-element.31), channel_id=1, source_target_pairs={{0,4},{4,8},{8,12},{12,16},{16,20},{20,24},{24,28},{28,0},{1,5},{5... | collective-permute-start | bytes 393224 | tf_op jit(solution)/shard_map/ppermute | solution.py:26
  169.5 7.8 %collective-permute-start.15 = (bf16[256,256]{1,0:T(8,128)(2,1)}, bf16[256,256]{1,0:T(8,128)(2,1)}, u32[]{:S(2)}, u32[]{:S(2)}) collective-permute-start(bf16[256,256]{1,0:T(8,128)(2,1)} %get-tuple-element.32), channel_id=1, source_target_pairs={{0,28},{4,0},{8,4},{12,8},{16,12},{20,16},{24,20},{28,24},{1,29},{... | collective-permute-start | bytes 393224 | tf_op jit(solution)/shard_map/ppermute | solution.py:26
  (17 other events, 132.1 us)
Sparse Core Ops, SparseCore 0:
  9.9 67.7 all-gather.3
  80.3 48.2 all-gather.5

commit v3 on v2

--- a/solution.py
+++ b/solution.py
@@ -43,7 +43,7 @@
                 ids == side * (half // 64) + own, products[own * 64 : own * 64 + 64], 0.0
             )
     for j in range(out_ref.shape[0]):
-        out_ref[j] = total[:, 128 * j : 128 * j + 128].astype(BF16)
+        out_ref[j] = total[:, 128 * j : 128 * j + 128]
 
 
 def partial_codes(tok, ids, down, after):
@@ -59,7 +59,7 @@
         ]
         + [pl.BlockSpec(memory_space=pl.ANY) for _ in after],
         out_specs=pl.BlockSpec((block // 128, 64, 128), lambda i: (i, 0, 0)),
-        out_shape=jax.ShapeDtypeStruct((rows // 128, 64, 128), BF16),
+        out_shape=jax.ShapeDtypeStruct((rows // 128, 64, 128), F32),
         compiler_params=PARAMS,
         cost_estimate=cost(4.0),
     )(in_hbm(tok), ids, down, *[in_hbm(a) for a in after])
@@ -67,9 +67,9 @@
 
 def sum_kernel(parts_ref, *refs):
     out_ref = refs[-1]
-    total = parts_ref[0].astype(F32)
+    total = parts_ref[0]
     for j in range(1, parts_ref.shape[0]):
-        total = total + parts_ref[j].astype(F32)
+        total = total + parts_ref[j]
     total = total.astype(BF16)
     for j in range(out_ref.shape[0]):
         out_ref[j] = total
@@ -239,7 +239,7 @@
 
 
 def filtering(mixed, rim, taps, spectrum, forward, inverse):
-    block = 128
+    block = 256
     rows, width = mixed.shape
     channels = width // 3
     steps = rows // block
@@ -272,20 +272,22 @@
                 running = running + taps_ref[c, tap : tap + 1, :] * extended[16 - tap : 16 - tap + block]
             filtered.append(running)
         before_ref[...] = current[block - 16 :]
-        window_ref[block:] = (filtered[1] * filtered[2]).astype(BF16)
-        window = window_ref[...]
-        waves_in = jnp.dot(fwd_hi_ref[...], window, preferred_element_type=F32)
-        waves_in = waves_in + jnp.dot(fwd_lo_ref[...], window, preferred_element_type=F32)
-        real, imaginary = waves_in[:128], waves_in[128:]
+        window_ref[128:] = (filtered[1] * filtered[2]).astype(BF16)
         first, second, third = (spectrum_ref[128 * j : 128 * j + 128] for j in range(3))
-        product = jnp.concatenate(
-            [real * first - imaginary * second, real * second + imaginary * third], axis=0
-        )
-        high, low = split(product)
-        out = jnp.dot(inv_hi_ref[...], high, preferred_element_type=F32)
-        out = out + jnp.dot(inv_hi_ref[...], low, preferred_element_type=F32)
-        out = out + jnp.dot(inv_lo_ref[...], high, preferred_element_type=F32)
-        gated_ref[...] = (filtered[0] * out).astype(BF16)
+        for start in range(0, block, 128):
+            window = window_ref[start : start + 256]
+            waves_in = jnp.dot(fwd_hi_ref[...], window, preferred_element_type=F32)
+            waves_in = waves_in + jnp.dot(fwd_lo_ref[...], window, preferred_element_type=F32)
+            real, imaginary = waves_in[:128], waves_in[128:]
+            product = jnp.concatenate(
+                [real * first - imaginary * second, real * second + imaginary * third], axis=0
+            )
+            high, low = split(product)
+            out = jnp.dot(inv_hi_ref[...], high, preferred_element_type=F32)
+            out = out + jnp.dot(inv_hi_ref[...], low, preferred_element_type=F32)
+            out = out + jnp.dot(inv_lo_ref[...], high, preferred_element_type=F32)
+            query = filtered[0][start : start + 128]
+            gated_ref[start : start + 128] = (query * out).astype(BF16)
 
     whole = lambda a: pl.BlockSpec(a.shape, lambda i: (0,) * a.ndim)
     operands = [rim, taps, spectrum, *forward, *inverse]
@@ -297,7 +299,7 @@
         out_shape=jax.ShapeDtypeStruct((rows, channels), BF16),
         scratch_shapes=[
             pltpu.VMEM((16, width), F32),
-            pltpu.VMEM((256, channels), BF16),
+            pltpu.VMEM((128 + block, channels), BF16),
         ],
         compiler_params=PARAMS,
         cost_estimate=cost(3.5),
@@ -441,9 +443,8 @@
         ("seq", "adapter"), split_axis=0, concat_axis=0, tiled=True,
     )
     forward, of_taps, inverse = (jnp.asarray(a) for a in waves())
-    spectrum = jnp.dot(
-        of_taps, long_filter.at[0].add(skip), precision=lax.Precision.HIGHEST
-    )
+    spectrum = jnp.dot(of_taps, long_filter, precision=lax.Precision.HIGHEST)
+    spectrum = spectrum + of_taps[:, :1] * skip[None]
     partials = partial_codes(tok, ids, down_all.reshape(-1, depth), (acc, f2, b2))
     received = lax.all_to_all(partials, "tensor", split_axis=0, concat_axis=0, tiled=True)
     acc = projecting(place, acc, (f2, b2), (2, 6), weight)

time: 190 us -> 191 us (level)
  waiting for transfers between devices: 47.6 us -> 50.9 us
    unnamed x37 -> x40, local copies, waits for them, and re-layouts: 7.55 us -> 6.67 us
  transfers between devices with their start and end apart: 31 -> 31, of which waited for: 9 -> 10; matrix products, arithmetic and copies ran while one was open for 2% -> 2% of each run, Pallas kernels for 24% -> 24%
where the time goes in v3:
time: 191 us; the launch traced here: 189 us
  starting transfers between devices  64.7 us (34%)
  waiting for transfers between devices  50.9 us (27%)
  Pallas kernels  48.4 us (25%)
  between operations  13.7 us (7%)
  local copies, waits for them, and re-layouts  9.94 us (5%)
    ppermute x24, starting transfers between devices, moved(): lax.ppermute(block, axis, [(i, (i + distance) % n) for i in range(n)])  35.5 us
    ppermute x24, waiting for transfers between devices, moved(): lax.ppermute(block, axis, [(i, (i + distance) % n) for i in range(n)])  35 us
    pallas_call x3, Pallas kernels, projecting(): pl.pallas_call(kernel, grid_spec=pltpu.PrefetchScalarGridSpec(num_scalar_...  15.5 us
    ppermute x1, waiting for transfers between devices, per_device(): lax.ppermute(folded(out_rows, first_acc, spectrum), ('seq', 'tensor'), [(...  12.2 us
    pallas_call x2, Pallas kernels, mixing(): pl.pallas_call(kernel, grid_spec=pltpu.PrefetchScalarGridSpec(num_scalar_...  11 us
    ppermute x1, starting transfers between devices, per_device(): rim_in = lax.ppermute(rim_late, 'seq', [(i, i + 1) for i in range(7)])  9.64 us
    all_to_all x1, starting transfers between devices, per_device(): lax.all_to_all(jnp.broadcast_to(adapter_down_maps[0].T[None], (32, rank,...  8.04 us
    pallas_call x2, Pallas kernels, out_projection(): pl.pallas_call(out_kernel, grid=(2,), in_specs=in_specs, out_specs=pl.Blo...  7.73 us
  transfers between devices with their start and end apart: 31, of which 10 were waited for; matrix products, arithmetic and copies ran while one was open for 2% of the time, Pallas kernels for 24%

profile of v3, /device:TPU:1, one launch (start us, length us, event | category | flops | bytes accessed | tf_op | source)
XLA Modules:
  0.0 188.9 jit_solution(14373445038821507423)
XLA Ops:
  9.8 4.0 %collective-permute-start.1 = (bf16[1024,512]{1,0:T(8,128)(2,1)}, bf16[1024,512]{1,0:T(8,128)(2,1)}, u32[]{:S(2)}, u32[]{:S(2)}) collective-permute-start(bf16[1024,512]{1,0:T(8,128)(2,1)} %bitcast.42), channel_id=1, source_target_pairs={{0,28},{4,0},{8,4},{12,8},{16,12},{20,16},{24,20},{28,24},{1,29},{... | collective-permute-start | bytes 3145736 | tf_op jit(solution)/shard_map/ppermute | solution.py:26
  16.3 8.0 %all-to-all-start = ((bf16[32,64,512]{2,1,0:T(8,128)(2,1)}), bf16[32,64,512]{2,1,0:T(8,128)(2,1)S(1)}, u32[]{:S(2)}, u32[]{:S(2)}) async-start(bf16[32,64,512]{2,1,0:T(8,128)(2,1)} %broadcast_in_dim.4), calls=%async_computation | async-start | bytes 4194304 | tf_op jit(solution)/shard_map/all_to_all | solution.py:441
  24.4 12.6 %collective-permute-done.refs_1_ = bf16[1024,512]{1,0:T(8,128)(2,1)} collective-permute-done((bf16[1024,512]{1,0:T(8,128)(2,1)}, bf16[1024,512]{1,0:T(8,128)(2,1)}, u32[]{:S(2)}, u32[]{:S(2)}) %collective-permute-start) | collective-permute-done | bytes 1048608 | tf_op jit(solution)/shard_map/ppermute | solution.py:26
  37.0 2.7 %collective-permute-start.3 = (bf16[1024,512]{1,0:T(8,128)(2,1)}, bf16[1024,512]{1,0:T(8,128)(2,1)}, u32[]{:S(2)}, u32[]{:S(2)}) collective-permute-start(bf16[1024,512]{1,0:T(8,128)(2,1)} %collective-permute-done.1.refs_2_), channel_id=1, source_target_pairs={{0,28},{4,0},{8,4},{12,8},{16,12},{20,16},{24,20},{28,24},{1,29},{... | collective-permute-start | bytes 3145736 | tf_op jit(solution)/shard_map/ppermute | solution.py:26
  41.7 5.5 %shard_map.118.refs_0_.after_ref = f32[1024,768]{1,0:T(8,128)S(1)} custom-call(s32[1]{0:T(128)} %bitcast.place_ref, bf16[1024,512]{1,0:T(8,128)(2,1)} %bitcast.43, bf16[1024,512]{1,0:T(8,128)(2,1)} %collective-permute-done.refs_1_, bf16[1024,512]{1,0:T(8,128)(2,1)} %collective-permute-done.1.refs_2_, bf16[3,4096,256]{2,1,0:T(8,128)(2,1)} %bitcast.28, ...), custom_call_target="tpu_custom_call" | custom-call | flops 9216000000 | bytes 9216000 | tf_op jit(solution)/shard_map/pallas_call | solution.py:120
  51.0 12.2 %collective-permute-done.16 = bf16[128,256]{1,0:T(8,128)(2,1)S(1)} collective-permute-done((bf16[128,256]{1,0:T(8,128)(2,1)S(1)}, bf16[128,256]{1,0:T(8,128)(2,1)S(1)}, u32[]{:S(2)}, u32[]{:S(2)}) %collective-permute-start.16) | collective-permute-done | bytes 65568 | tf_op jit(solution)/shard_map/ppermute | solution.py:462
  64.0 2.7 %collective-permute-start.5 = (bf16[1024,512]{1,0:T(8,128)(2,1)}, bf16[1024,512]{1,0:T(8,128)(2,1)}, u32[]{:S(2)}, u32[]{:S(2)}) collective-permute-start(bf16[1024,512]{1,0:T(8,128)(2,1)} %collective-permute-done.3.refs_2_), channel_id=1, source_target_pairs={{0,28},{4,0},{8,4},{12,8},{16,12},{20,16},{24,20},{28,24},{1,29},{... | collective-permute-start | bytes 3145736 | tf_op jit(solution)/shard_map/ppermute | solution.py:26
  66.6 5.1 %shard_map.122 = f32[8,64,128]{2,1,0:T(8,128)} custom-call(bf16[1024,512]{1,0:T(8,128)(2,1)} %bitcast.44, s32[1,1024]{1,0:T(1,128)S(1)} %bitcast.23, bf16[2048,512]{1,0:T(8,128)(2,1)S(1)} %bitcast.18, f32[1024,768]{1,0:T(8,128)} %copy-done.13, bf16[1024,512]{1,0:T(8,128)(2,1)} %copy-done.19, bf16[1024,512]{1,0:T(8,128)(2,1)} %collective-permute-done.3.refs_2_), custom_call_target="tpu_custom_call" | custom-call | flops 8000000000 | bytes 8000000 | tf_op jit(solution)/shard_map/pallas_call | solution.py:52
  71.7 4.6 %all-to-all-start.1 = ((f32[8,64,128]{2,1,0:T(8,128)}), f32[8,64,128]{2,1,0:T(8,128)S(1)}, u32[]{:S(2)}, u32[]{:S(2)}) async-start(f32[8,64,128]{2,1,0:T(8,128)} %shard_map.122), calls=%async_computation.1 | async-start | bytes 524288 | tf_op jit(solution)/shard_map/all_to_all | solution.py:449
  76.3 5.0 %shard_map.119.refs_0_ = f32[1024,768]{1,0:T(8,128)S(1)} custom-call(s32[1]{0:T(128)} %bitcast.place_ref, f32[1024,768]{1,0:T(8,128)} %copy-done.13, bf16[1024,512]{1,0:T(8,128)(2,1)} %copy-done.19, bf16[1024,512]{1,0:T(8,128)(2,1)} %collective-permute-done.3.refs_2_, bf16[3,4096,256]{2,1,0:T(8,128)(2,1)} %bitcast.31, bf16[3,4096,256]{2,1,0:T(8,128)(2,1)} %bitcast.32), custom_call_target="tpu_custom_call" | custom-call | flops 9216000000 | bytes 9216000 | tf_op jit(solution)/shard_map/pallas_call | solution.py:120
  83.0 7.6 %collective-permute-done.4.refs_1_.ahead_ref = bf16[1024,512]{1,0:T(8,128)(2,1)} collective-permute-done((bf16[1024,512]{1,0:T(8,128)(2,1)S(1)}, bf16[1024,512]{1,0:T(8,128)(2,1)}, u32[]{:S(2)}, u32[]{:S(2)}) %collective-permute-start.4) | collective-permute-done | bytes 1048608 | tf_op jit(solution)/shard_map/ppermute | solution.py:26
  95.2 4.8 %all-to-all-start.2 = ((bf16[8,64,128]{2,1,0:T(8,128)(2,1)}), bf16[8,64,128]{2,1,0:T(8,128)(2,1)S(1)}, u32[]{:S(2)}, u32[]{:S(2)}) async-start(bf16[8,64,128]{2,1,0:T(8,128)(2,1)} %shard_map.123), calls=%async_computation.2 | async-start | bytes 262144 | tf_op jit(solution)/shard_map/all_to_all | solution.py:451
  100.0 5.0 %shard_map.120.acc_ref = f32[1024,768]{1,0:T(8,128)S(1)} custom-call(s32[1]{0:T(128)} %bitcast.place_ref, f32[1024,768]{1,0:T(8,128)} %copy-done.1, bf16[1024,512]{1,0:T(8,128)(2,1)} %collective-permute-done.4.refs_1_.ahead_ref, bf16[1024,512]{1,0:T(8,128)(2,1)} %collective-permute-done.5.refs_2_.back_ref, bf16[3,4096,256]{2,1,0:T(8,128)(2,1)} %bitcast.33, ...), custom_call_target="tpu_custom_call" | custom-call | flops 9216000000 | bytes 9216000 | tf_op jit(solution)/shard_map/pallas_call | solution.py:120
  108.7 5.5 %shard_map.124 = (bf16[512,768]{1,0:T(8,128)(2,1)S(1)}, bf16[176,256]{1,0:T(8,128)(2,1)S(1)}) custom-call(s32[1]{0:T(128)} %bitcast.place_ref, f32[1024,768]{1,0:T(8,128)} %copy-done.14, bf16[512,512]{1,0:T(8,128)(2,1)S(1)} %collective-permute-done.6.last_ref, bf16[3,4096,256]{2,1,0:T(8,128)(2,1)} %bitcast.35, ...), custom_call_target="tpu_custom_call" | custom-call | flops 8000000000 | bytes 8000000 | tf_op jit(solution)/shard_map/pallas_call | solution.py:187
  114.3 9.6 %collective-permute-start.17 = (bf16[176,256]{1,0:T(8,128)(2,1)S(1)}, bf16[176,256]{1,0:T(8,128)(2,1)S(1)}, u32[]{:S(2)}, u32[]{:S(2)}) collective-permute-start(bf16[176,256]{1,0:T(8,128)(2,1)S(1)} %get-tuple-element.22), channel_id=1, source_target_pairs={{0,32},{32,64},{64,96},{96,128},{128,160},{160,192},{192,224},{1,3... | collective-permute-start | bytes 270344 | tf_op jit(solution)/shard_map/ppermute | solution.py:471
  124.0 5.5 %shard_map.125 = (bf16[512,768]{1,0:T(8,128)(2,1)S(1)}, bf16[176,256]{1,0:T(8,128)(2,1)S(1)}) custom-call(s32[1]{0:T(128)} %bitcast.place_ref, f32[1024,768]{1,0:T(8,128)} %copy-done.14, bf16[512,512]{1,0:T(8,128)(2,1)S(1)} %collective-permute-done.7.last_ref, bf16[3,4096,256]{2,1,0:T(8,128)(2,1)} %bitcast.36, ...), custom_call_target="tpu_custom_call" | custom-call | flops 8000000000 | bytes 8000000 | tf_op jit(solution)/shard_map/pallas_call | solution.py:187
  129.5 2.8 %shard_map.129.refs_0_ = bf16[512,256]{1,0:T(8,128)(2,1)S(1)} custom-call(bf16[512,768]{1,0:T(8,128)(2,1)S(1)} %get-tuple-element.21.mixed_ref, bf16[176,256]{1,0:T(8,128)(2,1)S(1)} %collective-permute-done.17.rim_ref, f32[3,7,256]{2,1,0:T(8,128)S(1)} %bitcast.21, f32[384,256]{1,0:T(8,128)S(1)} %copy-done.4, bf16[256,256]{1,0:T(8,128)(2,1)S(1)} %copy-done.9, ...), custom_call_target="tpu_custom_call" | custom-call | flops 7000000000 | bytes 7000000 | tf_op jit(solution)/shard_map/pallas_call | solution.py:294
  132.4 2.7 %collective-permute-start.19 = (bf16[512,256]{1,0:T(8,128)(2,1)S(1)}, bf16[512,256]{1,0:T(8,128)(2,1)S(1)}, u32[]{:S(2)}, u32[]{:S(2)}) collective-permute-start(bf16[512,256]{1,0:T(8,128)(2,1)S(1)} %shard_map.129.refs_0_), channel_id=1, source_target_pairs={{0,28},{4,0},{8,4},{12,8},{16,12},{20,16},{24,20},{28,24},{1,29},{... | collective-permute-start | bytes 786440 | tf_op jit(solution)/shard_map/ppermute | solution.py:26
  135.1 2.8 %shard_map.126.refs_0_ = bf16[512,256]{1,0:T(8,128)(2,1)S(1)} custom-call(bf16[512,768]{1,0:T(8,128)(2,1)S(1)} %get-tuple-element.17.mixed_ref, bf16[176,256]{1,0:T(8,128)(2,1)S(1)} %get-tuple-element.18.rim_ref, f32[3,7,256]{2,1,0:T(8,128)S(1)} %bitcast.22, f32[384,256]{1,0:T(8,128)S(1)} %copy-done.4, bf16[256,256]{1,0:T(8,128)(2,1)S(1)} %copy-done.9, ...), custom_call_target="tpu_custom_call" | custom-call | flops 7000000000 | bytes 7000000 | tf_op jit(solution)/shard_map/pallas_call | solution.py:294
  138.0 2.7 %collective-permute-start.9 = (bf16[512,256]{1,0:T(8,128)(2,1)S(1)}, bf16[512,256]{1,0:T(8,128)(2,1)S(1)}, u32[]{:S(2)}, u32[]{:S(2)}) collective-permute-start(bf16[512,256]{1,0:T(8,128)(2,1)S(1)} %shard_map.126.refs_0_), channel_id=1, source_target_pairs={{0,28},{4,0},{8,4},{12,8},{16,12},{20,16},{24,20},{28,24},{1,29},{... | collective-permute-start | bytes 786440 | tf_op jit(solution)/shard_map/ppermute | solution.py:26
  140.7 2.7 %collective-permute-start.21 = (bf16[512,256]{1,0:T(8,128)(2,1)S(1)}, bf16[512,256]{1,0:T(8,128)(2,1)S(1)}, u32[]{:S(2)}, u32[]{:S(2)}) collective-permute-start(bf16[512,256]{1,0:T(8,128)(2,1)S(1)} %collective-permute-done.19.refs_2_), channel_id=1, source_target_pairs={{0,28},{4,0},{8,4},{12,8},{16,12},{20,16},{24,20},{28,24},{1,29},{... | collective-permute-start | bytes 786440 | tf_op jit(solution)/shard_map/ppermute | solution.py:26
  143.3 4.2 %collective-permute-done.8.refs_1_ = bf16[512,256]{1,0:T(8,128)(2,1)S(1)} collective-permute-done((bf16[512,256]{1,0:T(8,128)(2,1)S(1)}, bf16[512,256]{1,0:T(8,128)(2,1)S(1)}, u32[]{:S(2)}, u32[]{:S(2)}) %collective-permute-start.8) | collective-permute-done | bytes 262176 | tf_op jit(solution)/shard_map/ppermute | solution.py:26
  147.5 2.7 %collective-permute-start.11 = (bf16[512,256]{1,0:T(8,128)(2,1)S(1)}, bf16[512,256]{1,0:T(8,128)(2,1)S(1)}, u32[]{:S(2)}, u32[]{:S(2)}) collective-permute-start(bf16[512,256]{1,0:T(8,128)(2,1)S(1)} %collective-permute-done.9.refs_2_), channel_id=1, source_target_pairs={{0,28},{4,0},{8,4},{12,8},{16,12},{20,16},{24,20},{28,24},{1,29},{... | collective-permute-start | bytes 786440 | tf_op jit(solution)/shard_map/ppermute | solution.py:26
  150.2 2.9 %collective-permute-done.20.refs_3_ = bf16[512,256]{1,0:T(8,128)(2,1)S(1)} collective-permute-done((bf16[512,256]{1,0:T(8,128)(2,1)S(1)}, bf16[512,256]{1,0:T(8,128)(2,1)S(1)}, u32[]{:S(2)}, u32[]{:S(2)}) %collective-permute-start.20) | collective-permute-done | bytes 262176 | tf_op jit(solution)/shard_map/ppermute | solution.py:26
  153.1 2.7 %collective-permute-start.23 = (bf16[512,256]{1,0:T(8,128)(2,1)S(1)}, bf16[512,256]{1,0:T(8,128)(2,1)S(1)}, u32[]{:S(2)}, u32[]{:S(2)}) collective-permute-start(bf16[512,256]{1,0:T(8,128)(2,1)S(1)} %collective-permute-done.21.refs_4_), channel_id=1, source_target_pairs={{0,28},{4,0},{8,4},{12,8},{16,12},{20,16},{24,20},{28,24},{1,29},{... | collective-permute-start | bytes 786440 | tf_op jit(solution)/shard_map/ppermute | solution.py:26
  155.8 2.9 %collective-permute-done.10.refs_3_ = bf16[512,256]{1,0:T(8,128)(2,1)S(1)} collective-permute-done((bf16[512,256]{1,0:T(8,128)(2,1)S(1)}, bf16[512,256]{1,0:T(8,128)(2,1)S(1)}, u32[]{:S(2)}, u32[]{:S(2)}) %collective-permute-start.10) | collective-permute-done | bytes 262176 | tf_op jit(solution)/shard_map/ppermute | solution.py:26
  158.8 2.7 %collective-permute-start.13 = (bf16[512,256]{1,0:T(8,128)(2,1)S(1)}, bf16[512,256]{1,0:T(8,128)(2,1)S(1)}, u32[]{:S(2)}, u32[]{:S(2)}) collective-permute-start(bf16[512,256]{1,0:T(8,128)(2,1)S(1)} %collective-permute-done.11.refs_4_), channel_id=1, source_target_pairs={{0,28},{4,0},{8,4},{12,8},{16,12},{20,16},{24,20},{28,24},{1,29},{... | collective-permute-start | bytes 786440 | tf_op jit(solution)/shard_map/ppermute | solution.py:26
  161.4 2.9 %collective-permute-done.22.ahead_ref.refs_5_ = bf16[512,256]{1,0:T(8,128)(2,1)S(1)} collective-permute-done((bf16[512,256]{1,0:T(8,128)(2,1)S(1)}, bf16[512,256]{1,0:T(8,128)(2,1)S(1)}, u32[]{:S(2)}, u32[]{:S(2)}) %collective-permute-start.22) | collective-permute-done | bytes 262176 | tf_op jit(solution)/shard_map/ppermute | solution.py:26
  165.1 2.7 %collective-permute-start.25 = (bf16[256,256]{1,0:T(8,128)(2,1)}, bf16[256,256]{1,0:T(8,128)(2,1)}, u32[]{:S(2)}, u32[]{:S(2)}) collective-permute-start(bf16[256,256]{1,0:T(8,128)(2,1)} %get-tuple-element.24), channel_id=1, source_target_pairs={{0,28},{4,0},{8,4},{12,8},{16,12},{20,16},{24,20},{28,24},{1,29},{... | collective-permute-start | bytes 393224 | tf_op jit(solution)/shard_map/ppermute | solution.py:26
  170.3 3.0 %collective-permute-start.15 = (bf16[256,256]{1,0:T(8,128)(2,1)}, bf16[256,256]{1,0:T(8,128)(2,1)}, u32[]{:S(2)}, u32[]{:S(2)}) collective-permute-start(bf16[256,256]{1,0:T(8,128)(2,1)} %get-tuple-element.20), channel_id=1, source_target_pairs={{0,28},{4,0},{8,4},{12,8},{16,12},{20,16},{24,20},{28,24},{1,29},{... | collective-permute-start | bytes 393224 | tf_op jit(solution)/shard_map/ppermute | solution.py:26
  174.3 3.8 %shard_map.131.refs_11_ = bf16[1024,512]{1,0:T(8,128)(2,1)} custom-call(bf16[512,256]{1,0:T(8,128)(2,1)S(1)} %shard_map.129.refs_0_, bf16[512,256]{1,0:T(8,128)(2,1)S(1)} %collective-permute-done.18.refs_1_, bf16[512,256]{1,0:T(8,128)(2,1)S(1)} %collective-permute-done.19.refs_2_, bf16[512,256]{1,0:T(8,128)(2,1)S(1)} %collective-permute-done.20.refs_3_, ...), custom_call_target="tpu_custom_call" | custom-call | flops 4600000000 | bytes 4600000 | tf_op jit(solution)/shard_map/pallas_call | solution.py:339
  178.1 3.9 %shard_map.132 = bf16[1024,512]{1,0:T(8,128)(2,1)} custom-call(bf16[512,256]{1,0:T(8,128)(2,1)S(1)} %shard_map.126.refs_0_, bf16[512,256]{1,0:T(8,128)(2,1)S(1)} %collective-permute-done.8.refs_1_, bf16[512,256]{1,0:T(8,128)(2,1)S(1)} %collective-permute-done.9.refs_2_, ...), custom_call_target="tpu_custom_call", output_to_operand_aliasing={{}: (11, {})} | custom-call | flops 4600000000 | bytes 4600000 | tf_op jit(solution)/shard_map/pallas_call | solution.py:339
  (90 shorter events, 26.6 us)
Async XLA Ops:
  6.5 33.1 %copy-start = (f32[128,256]{1,0:T(8,128)S(1)}, f32[128,256]{1,0:T(8,128)}, u32[]{:S(2)}) copy-start(f32[128,256]{1,0:T(8,128)} %param.17) | copy-start | bytes 393220
  6.5 102.2 %all-gather.4.cloned.1.call-start = ((), (), s32[]{:S(2)}) async-start(), calls=%async_computation.3 | async-start | bytes 3244032 | tf_op jit(solution)/shard_map/all_gather | solution.py:439
  7.3 29.7 %collective-permute-start = (bf16[1024,512]{1,0:T(8,128)(2,1)}, bf16[1024,512]{1,0:T(8,128)(2,1)}, u32[]{:S(2)}, u32[]{:S(2)}) collective-permute-start(bf16[1024,512]{1,0:T(8,128)(2,1)} %bitcast.41), channel_id=1, source_target_pairs={{0,4},{4,8},{8,12},{12,16},{16,20},{20,24},{24,28},{28,0},{1,5},{5... | collective-permute-start | bytes 3145736 | tf_op jit(solution)/shard_map/ppermute | solution.py:26
  9.8 27.1 %collective-permute-start.1 = (bf16[1024,512]{1,0:T(8,128)(2,1)}, bf16[1024,512]{1,0:T(8,128)(2,1)}, u32[]{:S(2)}, u32[]{:S(2)}) collective-permute-start(bf16[1024,512]{1,0:T(8,128)(2,1)} %bitcast.42), channel_id=1, source_target_pairs={{0,28},{4,0},{8,4},{12,8},{16,12},{20,16},{24,20},{28,24},{1,29},{... | collective-permute-start | bytes 3145736 | tf_op jit(solution)/shard_map/ppermute | solution.py:26
  16.3 50.4 %all-to-all-start = ((bf16[32,64,512]{2,1,0:T(8,128)(2,1)}), bf16[32,64,512]{2,1,0:T(8,128)(2,1)S(1)}, u32[]{:S(2)}, u32[]{:S(2)}) async-start(bf16[32,64,512]{2,1,0:T(8,128)(2,1)} %broadcast_in_dim.4), calls=%async_computation | async-start | bytes 4194304 | tf_op jit(solution)/shard_map/all_to_all | solution.py:441
  24.3 149.0 %all-gather.6.cloned.1.call-start = ((), (), s32[]{:S(2)}) async-start(), calls=%async_computation.4 | async-start | bytes 2162688 | tf_op jit(solution)/shard_map/all_gather | solution.py:467
  36.9 26.9 %collective-permute-start.2 = (bf16[1024,512]{1,0:T(8,128)(2,1)}, bf16[1024,512]{1,0:T(8,128)(2,1)S(1)}, u32[]{:S(2)}, u32[]{:S(2)}) collective-permute-start(bf16[1024,512]{1,0:T(8,128)(2,1)} %collective-permute-done.refs_1_), channel_id=1, source_target_pairs={{0,4},{4,8},{8,12},{12,16},{16,20},{20,24},{24,28},{28,0},{1,5},{5... | collective-permute-start | bytes 3145736 | tf_op jit(solution)/shard_map/ppermute | solution.py:26
  37.0 27.0 %collective-permute-start.3 = (bf16[1024,512]{1,0:T(8,128)(2,1)}, bf16[1024,512]{1,0:T(8,128)(2,1)}, u32[]{:S(2)}, u32[]{:S(2)}) collective-permute-start(bf16[1024,512]{1,0:T(8,128)(2,1)} %collective-permute-done.1.refs_2_), channel_id=1, source_target_pairs={{0,28},{4,0},{8,4},{12,8},{16,12},{20,16},{24,20},{28,24},{1,29},{... | collective-permute-start | bytes 3145736 | tf_op jit(solution)/shard_map/ppermute | solution.py:26
  48.9 14.3 %collective-permute-start.16 = (bf16[128,256]{1,0:T(8,128)(2,1)S(1)}, bf16[128,256]{1,0:T(8,128)(2,1)S(1)}, u32[]{:S(2)}, u32[]{:S(2)}) collective-permute-start(bf16[128,256]{1,0:T(8,128)(2,1)S(1)} %shard_map.128), channel_id=1, source_target_pairs={{0,0},{4,4},{8,8},{12,12},{16,16},{20,20},{24,24},{28,28},{32,36},... | collective-permute-start | bytes 196616 | tf_op jit(solution)/shard_map/ppermute | solution.py:462
  63.9 26.8 %collective-permute-start.4 = (bf16[1024,512]{1,0:T(8,128)(2,1)S(1)}, bf16[1024,512]{1,0:T(8,128)(2,1)}, u32[]{:S(2)}, u32[]{:S(2)}) collective-permute-start(bf16[1024,512]{1,0:T(8,128)(2,1)S(1)} %collective-permute-done.2.refs_1_), channel_id=1, source_target_pairs={{0,4},{4,8},{8,12},{12,16},{16,20},{20,24},{24,28},{28,0},{1,5},{5... | collective-permute-start | bytes 3145736 | tf_op jit(solution)/shard_map/ppermute | solution.py:26
  64.0 26.7 %collective-permute-start.5 = (bf16[1024,512]{1,0:T(8,128)(2,1)}, bf16[1024,512]{1,0:T(8,128)(2,1)}, u32[]{:S(2)}, u32[]{:S(2)}) collective-permute-start(bf16[1024,512]{1,0:T(8,128)(2,1)} %collective-permute-done.3.refs_2_), channel_id=1, source_target_pairs={{0,28},{4,0},{8,4},{12,8},{16,12},{20,16},{24,20},{28,24},{1,29},{... | collective-permute-start | bytes 3145736 | tf_op jit(solution)/shard_map/ppermute | solution.py:26
  71.7 22.8 %all-to-all-start.1 = ((f32[8,64,128]{2,1,0:T(8,128)}), f32[8,64,128]{2,1,0:T(8,128)S(1)}, u32[]{:S(2)}, u32[]{:S(2)}) async-start(f32[8,64,128]{2,1,0:T(8,128)} %shard_map.122), calls=%async_computation.1 | async-start | bytes 524288 | tf_op jit(solution)/shard_map/all_to_all | solution.py:449
  92.0 32.0 %collective-permute-start.7 = (bf16[512,512]{1,0:T(8,128)(2,1)S(1)}, bf16[512,512]{1,0:T(8,128)(2,1)S(1)}, u32[]{:S(2)}, u32[]{:S(2)}) collective-permute-start(bf16[512,512]{1,0:T(8,128)(2,1)S(1)} %get-tuple-element.16.refs_2_), channel_id=1, source_target_pairs={{0,28},{4,0},{8,4},{12,8},{16,12},{20,16},{24,20},{28,24},{1,29},{... | collective-permute-start | bytes 1572872 | tf_op jit(solution)/shard_map/ppermute | solution.py:26
  93.5 15.2 %collective-permute-start.6 = (bf16[512,512]{1,0:T(8,128)(2,1)S(1)}, bf16[512,512]{1,0:T(8,128)(2,1)S(1)}, u32[]{:S(2)}, u32[]{:S(2)}) collective-permute-start(bf16[512,512]{1,0:T(8,128)(2,1)S(1)} %get-tuple-element.15.refs_1_), channel_id=1, source_target_pairs={{0,4},{4,8},{8,12},{12,16},{16,20},{20,24},{24,28},{28,0},{1,5},{5... | collective-permute-start | bytes 1572872 | tf_op jit(solution)/shard_map/ppermute | solution.py:26
  95.2 13.5 %all-to-all-start.2 = ((bf16[8,64,128]{2,1,0:T(8,128)(2,1)}), bf16[8,64,128]{2,1,0:T(8,128)(2,1)S(1)}, u32[]{:S(2)}, u32[]{:S(2)}) async-start(bf16[8,64,128]{2,1,0:T(8,128)(2,1)} %shard_map.123), calls=%async_computation.2 | async-start | bytes 262144 | tf_op jit(solution)/shard_map/all_to_all | solution.py:451
  114.3 15.2 %collective-permute-start.17 = (bf16[176,256]{1,0:T(8,128)(2,1)S(1)}, bf16[176,256]{1,0:T(8,128)(2,1)S(1)}, u32[]{:S(2)}, u32[]{:S(2)}) collective-permute-start(bf16[176,256]{1,0:T(8,128)(2,1)S(1)} %get-tuple-element.22), channel_id=1, source_target_pairs={{0,32},{32,64},{64,96},{96,128},{128,160},{160,192},{192,224},{1,3... | collective-permute-start | bytes 270344 | tf_op jit(solution)/shard_map/ppermute | solution.py:471
  132.3 8.3 %collective-permute-start.18 = (bf16[512,256]{1,0:T(8,128)(2,1)S(1)}, bf16[512,256]{1,0:T(8,128)(2,1)S(1)}, u32[]{:S(2)}, u32[]{:S(2)}) collective-permute-start(bf16[512,256]{1,0:T(8,128)(2,1)S(1)} %shard_map.129.refs_0_), channel_id=1, source_target_pairs={{0,4},{4,8},{8,12},{12,16},{16,20},{20,24},{24,28},{28,0},{1,5},{5... | collective-permute-start | bytes 786440 | tf_op jit(solution)/shard_map/ppermute | solution.py:26
  132.4 8.2 %collective-permute-start.19 = (bf16[512,256]{1,0:T(8,128)(2,1)S(1)}, bf16[512,256]{1,0:T(8,128)(2,1)S(1)}, u32[]{:S(2)}, u32[]{:S(2)}) collective-permute-start(bf16[512,256]{1,0:T(8,128)(2,1)S(1)} %shard_map.129.refs_0_), channel_id=1, source_target_pairs={{0,28},{4,0},{8,4},{12,8},{16,12},{20,16},{24,20},{28,24},{1,29},{... | collective-permute-start | bytes 786440 | tf_op jit(solution)/shard_map/ppermute | solution.py:26
  137.9 9.6 %collective-permute-start.8 = (bf16[512,256]{1,0:T(8,128)(2,1)S(1)}, bf16[512,256]{1,0:T(8,128)(2,1)S(1)}, u32[]{:S(2)}, u32[]{:S(2)}) collective-permute-start(bf16[512,256]{1,0:T(8,128)(2,1)S(1)} %shard_map.126.refs_0_), channel_id=1, source_target_pairs={{0,4},{4,8},{8,12},{12,16},{16,20},{20,24},{24,28},{28,0},{1,5},{5... | collective-permute-start | bytes 786440 | tf_op jit(solution)/shard_map/ppermute | solution.py:26
  138.0 9.5 %collective-permute-start.9 = (bf16[512,256]{1,0:T(8,128)(2,1)S(1)}, bf16[512,256]{1,0:T(8,128)(2,1)S(1)}, u32[]{:S(2)}, u32[]{:S(2)}) collective-permute-start(bf16[512,256]{1,0:T(8,128)(2,1)S(1)} %shard_map.126.refs_0_), channel_id=1, source_target_pairs={{0,28},{4,0},{8,4},{12,8},{16,12},{20,16},{24,20},{28,24},{1,29},{... | collective-permute-start | bytes 786440 | tf_op jit(solution)/shard_map/ppermute | solution.py:26
  140.7 12.5 %collective-permute-start.20 = (bf16[512,256]{1,0:T(8,128)(2,1)S(1)}, bf16[512,256]{1,0:T(8,128)(2,1)S(1)}, u32[]{:S(2)}, u32[]{:S(2)}) collective-permute-start(bf16[512,256]{1,0:T(8,128)(2,1)S(1)} %collective-permute-done.18.refs_1_), channel_id=1, source_target_pairs={{0,4},{4,8},{8,12},{12,16},{16,20},{20,24},{24,28},{28,0},{1,5},{5... | collective-permute-start | bytes 786440 | tf_op jit(solution)/shard_map/ppermute | solution.py:26
  140.7 12.5 %collective-permute-start.21 = (bf16[512,256]{1,0:T(8,128)(2,1)S(1)}, bf16[512,256]{1,0:T(8,128)(2,1)S(1)}, u32[]{:S(2)}, u32[]{:S(2)}) collective-permute-start(bf16[512,256]{1,0:T(8,128)(2,1)S(1)} %collective-permute-done.19.refs_2_), channel_id=1, source_target_pairs={{0,28},{4,0},{8,4},{12,8},{16,12},{20,16},{24,20},{28,24},{1,29},{... | collective-permute-start | bytes 786440 | tf_op jit(solution)/shard_map/ppermute | solution.py:26
  147.5 11.2 %collective-permute-start.10 = (bf16[512,256]{1,0:T(8,128)(2,1)S(1)}, bf16[512,256]{1,0:T(8,128)(2,1)S(1)}, u32[]{:S(2)}, u32[]{:S(2)}) collective-permute-start(bf16[512,256]{1,0:T(8,128)(2,1)S(1)} %collective-permute-done.8.refs_1_), channel_id=1, source_target_pairs={{0,4},{4,8},{8,12},{12,16},{16,20},{20,24},{24,28},{28,0},{1,5},{5... | collective-permute-start | bytes 786440 | tf_op jit(solution)/shard_map/ppermute | solution.py:26
  147.5 11.2 %collective-permute-start.11 = (bf16[512,256]{1,0:T(8,128)(2,1)S(1)}, bf16[512,256]{1,0:T(8,128)(2,1)S(1)}, u32[]{:S(2)}, u32[]{:S(2)}) collective-permute-start(bf16[512,256]{1,0:T(8,128)(2,1)S(1)} %collective-permute-done.9.refs_2_), channel_id=1, source_target_pairs={{0,28},{4,0},{8,4},{12,8},{16,12},{20,16},{24,20},{28,24},{1,29},{... | collective-permute-start | bytes 786440 | tf_op jit(solution)/shard_map/ppermute | solution.py:26
  153.1 11.2 %collective-permute-start.22 = (bf16[512,256]{1,0:T(8,128)(2,1)S(1)}, bf16[512,256]{1,0:T(8,128)(2,1)S(1)}, u32[]{:S(2)}, u32[]{:S(2)}) collective-permute-start(bf16[512,256]{1,0:T(8,128)(2,1)S(1)} %collective-permute-done.20.refs_3_), channel_id=1, source_target_pairs={{0,4},{4,8},{8,12},{12,16},{16,20},{20,24},{24,28},{28,0},{1,5},{5... | collective-permute-start | bytes 786440 | tf_op jit(solution)/shard_map/ppermute | solution.py:26
  153.1 11.2 %collective-permute-start.23 = (bf16[512,256]{1,0:T(8,128)(2,1)S(1)}, bf16[512,256]{1,0:T(8,128)(2,1)S(1)}, u32[]{:S(2)}, u32[]{:S(2)}) collective-permute-start(bf16[512,256]{1,0:T(8,128)(2,1)S(1)} %collective-permute-done.21.refs_4_), channel_id=1, source_target_pairs={{0,28},{4,0},{8,4},{12,8},{16,12},{20,16},{24,20},{28,24},{1,29},{... | collective-permute-start | bytes 786440 | tf_op jit(solution)/shard_map/ppermute | solution.py:26
  158.7 10.8 %collective-permute-start.12 = (bf16[512,256]{1,0:T(8,128)(2,1)S(1)}, bf16[512,256]{1,0:T(8,128)(2,1)S(1)}, u32[]{:S(2)}, u32[]{:S(2)}) collective-permute-start(bf16[512,256]{1,0:T(8,128)(2,1)S(1)} %collective-permute-done.10.refs_3_), channel_id=1, source_target_pairs={{0,4},{4,8},{8,12},{12,16},{16,20},{20,24},{24,28},{28,0},{1,5},{5... | collective-permute-start | bytes 786440 | tf_op jit(solution)/shard_map/ppermute | solution.py:26
  158.8 10.8 %collective-permute-start.13 = (bf16[512,256]{1,0:T(8,128)(2,1)S(1)}, bf16[512,256]{1,0:T(8,128)(2,1)S(1)}, u32[]{:S(2)}, u32[]{:S(2)}) collective-permute-start(bf16[512,256]{1,0:T(8,128)(2,1)S(1)} %collective-permute-done.11.refs_4_), channel_id=1, source_target_pairs={{0,28},{4,0},{8,4},{12,8},{16,12},{20,16},{24,20},{28,24},{1,29},{... | collective-permute-start | bytes 786440 | tf_op jit(solution)/shard_map/ppermute | solution.py:26
  165.1 8.2 %collective-permute-start.24 = (bf16[256,256]{1,0:T(8,128)(2,1)}, bf16[256,256]{1,0:T(8,128)(2,1)}, u32[]{:S(2)}, u32[]{:S(2)}) collective-permute-start(bf16[256,256]{1,0:T(8,128)(2,1)} %get-tuple-element.23), channel_id=1, source_target_pairs={{0,4},{4,8},{8,12},{12,16},{16,20},{20,24},{24,28},{28,0},{1,5},{5... | collective-permute-start | bytes 393224 | tf_op jit(solution)/shard_map/ppermute | solution.py:26
  165.1 8.2 %collective-permute-start.25 = (bf16[256,256]{1,0:T(8,128)(2,1)}, bf16[256,256]{1,0:T(8,128)(2,1)}, u32[]{:S(2)}, u32[]{:S(2)}) collective-permute-start(bf16[256,256]{1,0:T(8,128)(2,1)} %get-tuple-element.24), channel_id=1, source_target_pairs={{0,28},{4,0},{8,4},{12,8},{16,12},{20,16},{24,20},{28,24},{1,29},{... | collective-permute-start | bytes 393224 | tf_op jit(solution)/shard_map/ppermute | solution.py:26
  170.3 7.8 %collective-permute-start.14 = (bf16[256,256]{1,0:T(8,128)(2,1)}, bf16[256,256]{1,0:T(8,128)(2,1)}, u32[]{:S(2)}, u32[]{:S(2)}) collective-permute-start(bf16[256,256]{1,0:T(8,128)(2,1)} %get-tuple-element.19), channel_id=1, source_target_pairs={{0,4},{4,8},{8,12},{12,16},{16,20},{20,24},{24,28},{28,0},{1,5},{5... | collective-permute-start | bytes 393224 | tf_op jit(solution)/shard_map/ppermute | solution.py:26
  170.3 7.8 %collective-permute-start.15 = (bf16[256,256]{1,0:T(8,128)(2,1)}, bf16[256,256]{1,0:T(8,128)(2,1)}, u32[]{:S(2)}, u32[]{:S(2)}) collective-permute-start(bf16[256,256]{1,0:T(8,128)(2,1)} %get-tuple-element.20), channel_id=1, source_target_pairs={{0,28},{4,0},{8,4},{12,8},{16,12},{20,16},{24,20},{28,24},{1,29},{... | collective-permute-start | bytes 393224 | tf_op jit(solution)/shard_map/ppermute | solution.py:26
  (19 other events, 200.5 us)
Sparse Core Ops, SparseCore 0:
  9.9 66.4 all-gather.3
  78.9 48.2 all-gather.5

commit v4 on v3

--- a/solution.py
+++ b/solution.py
@@ -13,7 +13,7 @@
 
 def cost(micros):
     return pl.CostEstimate(
-        flops=int(micros * 2e9), transcendentals=0, bytes_accessed=int(micros * 2e6)
+        flops=int(micros * 2.4e9), transcendentals=0, bytes_accessed=int(micros * 2.4e6)
     )
 
 
@@ -445,11 +445,11 @@
     forward, of_taps, inverse = (jnp.asarray(a) for a in waves())
     spectrum = jnp.dot(of_taps, long_filter, precision=lax.Precision.HIGHEST)
     spectrum = spectrum + of_taps[:, :1] * skip[None]
-    partials = partial_codes(tok, ids, down_all.reshape(-1, depth), (acc, f2, b2))
+    partials = partial_codes(tok, ids, down_all.reshape(-1, depth), (acc,))
     received = lax.all_to_all(partials, "tensor", split_axis=0, concat_axis=0, tiled=True)
     acc = projecting(place, acc, (f2, b2), (2, 6), weight)
     codes = lax.all_to_all(
-        summed_codes(received, (acc, f3_half, b3_half)), "tensor", split_axis=0, concat_axis=0, tiled=True
+        summed_codes(received, (acc,)), "tensor", split_axis=0, concat_axis=0, tiled=True
     )
 
     acc = projecting(place, acc, (f3, b3), (3, 5), weight)

time: 191 us -> 199 us (1.042)
  the two profiles are of different devices: /device:TPU:1 before, /device:TPU:9 now
where the time goes in v4:
time: 199 us; the launch traced here: 198 us
  starting transfers between devices  69.2 us (35%)
  waiting for transfers between devices  54.9 us (28%)
  Pallas kernels  48.5 us (24%)
  between operations  13.7 us (7%)
  local copies, waits for them, and re-layouts  10.9 us (5%)
    ppermute x24, waiting for transfers between devices, moved(): lax.ppermute(block, axis, [(i, (i + distance) % n) for i in range(n)])  42.4 us
    ppermute x24, starting transfers between devices, moved(): lax.ppermute(block, axis, [(i, (i + distance) % n) for i in range(n)])  34.6 us
    pallas_call x3, Pallas kernels, projecting(): pl.pallas_call(kernel, grid_spec=pltpu.PrefetchScalarGridSpec(num_scalar_...  15.6 us
    ppermute x1, waiting for transfers between devices, per_device(): lax.ppermute(folded(out_rows, first_acc, spectrum), ('seq', 'tensor'), [(...  11.8 us
    pallas_call x2, Pallas kernels, mixing(): pl.pallas_call(kernel, grid_spec=pltpu.PrefetchScalarGridSpec(num_scalar_...  11.1 us
    ppermute x1, starting transfers between devices, per_device(): rim_in = lax.ppermute(rim_late, 'seq', [(i, i + 1) for i in range(7)])  8.81 us
    all_to_all x1, starting transfers between devices, per_device(): lax.all_to_all(jnp.broadcast_to(adapter_down_maps[0].T[None], (32, rank,...  8.13 us
    pallas_call x2, Pallas kernels, out_projection(): pl.pallas_call(out_kernel, grid=(2,), in_specs=in_specs, out_specs=pl.Blo...  7.73 us
  transfers between devices with their start and end apart: 31, of which 9 were waited for; matrix products, arithmetic and copies ran while one was open for 2% of the time, Pallas kernels for 23%

profile of v4, /device:TPU:9, one launch (start us, length us, event | category | flops | bytes accessed | tf_op | source)
XLA Modules:
  0.0 198.4 jit_solution(3108172026513706023)
XLA Ops:
  9.0 4.0 %collective-permute-start.1 = (bf16[1024,512]{1,0:T(8,128)(2,1)}, bf16[1024,512]{1,0:T(8,128)(2,1)S(1)}, u32[]{:S(2)}, u32[]{:S(2)}) collective-permute-start(bf16[1024,512]{1,0:T(8,128)(2,1)} %bitcast.42), channel_id=1, source_target_pairs={{0,28},{4,0},{8,4},{12,8},{16,12},{20,16},{24,20},{28,24},{1,29},{... | collective-permute-start | bytes 3145736 | tf_op jit(solution)/shard_map/ppermute | solution.py:26
  15.4 8.1 %all-to-all-start = ((bf16[32,64,512]{2,1,0:T(8,128)(2,1)}), bf16[32,64,512]{2,1,0:T(8,128)(2,1)S(1)}, u32[]{:S(2)}, u32[]{:S(2)}) async-start(bf16[32,64,512]{2,1,0:T(8,128)(2,1)} %broadcast_in_dim.4), calls=%async_computation | async-start | bytes 4194304 | tf_op jit(solution)/shard_map/all_to_all | solution.py:441
  25.8 10.4 %collective-permute-done.refs_1_ = bf16[1024,512]{1,0:T(8,128)(2,1)} collective-permute-done((bf16[1024,512]{1,0:T(8,128)(2,1)}, bf16[1024,512]{1,0:T(8,128)(2,1)}, u32[]{:S(2)}, u32[]{:S(2)}) %collective-permute-start) | collective-permute-done | bytes 1048608 | tf_op jit(solution)/shard_map/ppermute | solution.py:26
  36.1 2.7 %collective-permute-start.3 = (bf16[1024,512]{1,0:T(8,128)(2,1)S(1)}, bf16[1024,512]{1,0:T(8,128)(2,1)}, u32[]{:S(2)}, u32[]{:S(2)}) collective-permute-start(bf16[1024,512]{1,0:T(8,128)(2,1)S(1)} %collective-permute-done.1.refs_2_), channel_id=1, source_target_pairs={{0,28},{4,0},{8,4},{12,8},{16,12},{20,16},{24,20},{28,24},{1,29},{... | collective-permute-start | bytes 3145736 | tf_op jit(solution)/shard_map/ppermute | solution.py:26
  38.8 5.5 %shard_map.118.refs_0_.after_ref = f32[1024,768]{1,0:T(8,128)S(1)} custom-call(s32[1]{0:T(128)} %bitcast.place_ref, bf16[1024,512]{1,0:T(8,128)(2,1)} %bitcast.43, bf16[1024,512]{1,0:T(8,128)(2,1)} %collective-permute-done.refs_1_, bf16[1024,512]{1,0:T(8,128)(2,1)} %copy-done.17, bf16[3,4096,256]{2,1,0:T(8,128)(2,1)} %bitcast.28, ...), custom_call_target="tpu_custom_call" | custom-call | flops 11059200000 | bytes 11059200 | tf_op jit(solution)/shard_map/pallas_call | solution.py:120
  46.0 4.3 %collective-permute-start.16 = (bf16[128,256]{1,0:T(8,128)(2,1)S(1)}, bf16[128,256]{1,0:T(8,128)(2,1)S(1)}, u32[]{:S(2)}, u32[]{:S(2)}) collective-permute-start(bf16[128,256]{1,0:T(8,128)(2,1)S(1)} %shard_map.128), channel_id=1, source_target_pairs={{0,0},{4,4},{8,8},{12,12},{16,16},{20,20},{24,24},{28,28},{32,36},... | collective-permute-start | bytes 196616 | tf_op jit(solution)/shard_map/ppermute | solution.py:462
  50.3 11.8 %collective-permute-done.16 = bf16[128,256]{1,0:T(8,128)(2,1)S(1)} collective-permute-done((bf16[128,256]{1,0:T(8,128)(2,1)S(1)}, bf16[128,256]{1,0:T(8,128)(2,1)S(1)}, u32[]{:S(2)}, u32[]{:S(2)}) %collective-permute-start.16) | collective-permute-done | bytes 65568 | tf_op jit(solution)/shard_map/ppermute | solution.py:462
  62.7 5.1 %shard_map.122 = f32[8,64,128]{2,1,0:T(8,128)} custom-call(bf16[1024,512]{1,0:T(8,128)(2,1)} %bitcast.44, s32[1,1024]{1,0:T(1,128)S(1)} %bitcast.23, bf16[2048,512]{1,0:T(8,128)(2,1)S(1)} %bitcast.18, f32[1024,768]{1,0:T(8,128)} %copy-done.10), custom_call_target="tpu_custom_call" | custom-call | flops 9600000000 | bytes 9600000 | tf_op jit(solution)/shard_map/pallas_call | solution.py:52
  67.8 6.8 %all-to-all-start.1 = ((f32[8,64,128]{2,1,0:T(8,128)}), f32[8,64,128]{2,1,0:T(8,128)S(1)}, u32[]{:S(2)}, u32[]{:S(2)}) async-start(f32[8,64,128]{2,1,0:T(8,128)} %shard_map.122), calls=%async_computation.1 | async-start | bytes 524288 | tf_op jit(solution)/shard_map/all_to_all | solution.py:449
  77.3 5.0 %shard_map.119.refs_0_ = f32[1024,768]{1,0:T(8,128)S(1)} custom-call(s32[1]{0:T(128)} %bitcast.place_ref, f32[1024,768]{1,0:T(8,128)} %copy-done.10, bf16[1024,512]{1,0:T(8,128)(2,1)} %collective-permute-done.2.refs_1_, bf16[1024,512]{1,0:T(8,128)(2,1)} %collective-permute-done.3.refs_2_, bf16[3,4096,256]{2,1,0:T(8,128)(2,1)} %bitcast.31, ...), custom_call_target="tpu_custom_call" | custom-call | flops 11059200000 | bytes 11059200 | tf_op jit(solution)/shard_map/pallas_call | solution.py:120
  84.6 6.6 %all-to-all-start.2 = ((bf16[8,64,128]{2,1,0:T(8,128)(2,1)}), bf16[8,64,128]{2,1,0:T(8,128)(2,1)S(1)}, u32[]{:S(2)}, u32[]{:S(2)}) async-start(bf16[8,64,128]{2,1,0:T(8,128)(2,1)} %shard_map.123), calls=%async_computation.2 | async-start | bytes 262144 | tf_op jit(solution)/shard_map/all_to_all | solution.py:451
  91.2 13.4 %collective-permute-done.4.refs_1_.ahead_ref = bf16[1024,512]{1,0:T(8,128)(2,1)} collective-permute-done((bf16[1024,512]{1,0:T(8,128)(2,1)}, bf16[1024,512]{1,0:T(8,128)(2,1)}, u32[]{:S(2)}, u32[]{:S(2)}) %collective-permute-start.4) | collective-permute-done | bytes 1048608 | tf_op jit(solution)/shard_map/ppermute | solution.py:26
  108.4 5.2 %shard_map.120.acc_ref = f32[1024,768]{1,0:T(8,128)S(1)} custom-call(s32[1]{0:T(128)} %bitcast.place_ref, f32[1024,768]{1,0:T(8,128)} %copy-done.11, bf16[1024,512]{1,0:T(8,128)(2,1)} %collective-permute-done.4.refs_1_.ahead_ref, bf16[1024,512]{1,0:T(8,128)(2,1)} %copy-done.18, bf16[3,4096,256]{2,1,0:T(8,128)(2,1)} %bitcast.33, bf16[3,4096,256]{2,1,0:T(8,128)(2,1)} %bitcast.34), custom_call_target="tpu_custom_call" | custom-call | flops 11059200000 | bytes 11059200 | tf_op jit(solution)/shard_map/pallas_call | solution.py:120
  115.3 3.8 %collective-permute-done.6.last_ref = bf16[512,512]{1,0:T(8,128)(2,1)S(1)} collective-permute-done((bf16[512,512]{1,0:T(8,128)(2,1)S(1)}, bf16[512,512]{1,0:T(8,128)(2,1)S(1)}, u32[]{:S(2)}, u32[]{:S(2)}) %collective-permute-start.6) | collective-permute-done | bytes 524320 | tf_op jit(solution)/shard_map/ppermute | solution.py:26
  119.1 5.6 %shard_map.124 = (bf16[512,768]{1,0:T(8,128)(2,1)S(1)}, bf16[176,256]{1,0:T(8,128)(2,1)S(1)}) custom-call(s32[1]{0:T(128)} %bitcast.place_ref, f32[1024,768]{1,0:T(8,128)} %copy-done.12, bf16[512,512]{1,0:T(8,128)(2,1)S(1)} %collective-permute-done.6.last_ref, bf16[3,4096,256]{2,1,0:T(8,128)(2,1)} %bitcast.35, ...), custom_call_target="tpu_custom_call" | custom-call | flops 9600000000 | bytes 9600000 | tf_op jit(solution)/shard_map/pallas_call | solution.py:187
  124.7 8.8 %collective-permute-start.17 = (bf16[176,256]{1,0:T(8,128)(2,1)S(1)}, bf16[176,256]{1,0:T(8,128)(2,1)S(1)}, u32[]{:S(2)}, u32[]{:S(2)}) collective-permute-start(bf16[176,256]{1,0:T(8,128)(2,1)S(1)} %get-tuple-element.22), channel_id=1, source_target_pairs={{0,32},{32,64},{64,96},{96,128},{128,160},{160,192},{192,224},{1,3... | collective-permute-start | bytes 270344 | tf_op jit(solution)/shard_map/ppermute | solution.py:471
  133.5 5.5 %shard_map.125 = (bf16[512,768]{1,0:T(8,128)(2,1)S(1)}, bf16[176,256]{1,0:T(8,128)(2,1)S(1)}) custom-call(s32[1]{0:T(128)} %bitcast.place_ref, f32[1024,768]{1,0:T(8,128)} %copy-done.12, bf16[512,512]{1,0:T(8,128)(2,1)S(1)} %collective-permute-done.7.last_ref, bf16[3,4096,256]{2,1,0:T(8,128)(2,1)} %bitcast.36, ...), custom_call_target="tpu_custom_call" | custom-call | flops 9600000000 | bytes 9600000 | tf_op jit(solution)/shard_map/pallas_call | solution.py:187
  139.1 2.8 %shard_map.129.refs_0_ = bf16[512,256]{1,0:T(8,128)(2,1)S(1)} custom-call(bf16[512,768]{1,0:T(8,128)(2,1)S(1)} %get-tuple-element.21.mixed_ref, bf16[176,256]{1,0:T(8,128)(2,1)S(1)} %collective-permute-done.17.rim_ref, f32[3,7,256]{2,1,0:T(8,128)S(1)} %bitcast.21, f32[384,256]{1,0:T(8,128)S(1)} %copy-done.1, bf16[256,256]{1,0:T(8,128)(2,1)S(1)} %copy-done.6, ...), custom_call_target="tpu_custom_call" | custom-call | flops 8400000000 | bytes 8400000 | tf_op jit(solution)/shard_map/pallas_call | solution.py:294
  142.0 2.7 %collective-permute-start.19 = (bf16[512,256]{1,0:T(8,128)(2,1)S(1)}, bf16[512,256]{1,0:T(8,128)(2,1)S(1)}, u32[]{:S(2)}, u32[]{:S(2)}) collective-permute-start(bf16[512,256]{1,0:T(8,128)(2,1)S(1)} %shard_map.129.refs_0_), channel_id=1, source_target_pairs={{0,28},{4,0},{8,4},{12,8},{16,12},{20,16},{24,20},{28,24},{1,29},{... | collective-permute-start | bytes 786440 | tf_op jit(solution)/shard_map/ppermute | solution.py:26
  144.7 2.8 %shard_map.126.refs_0_ = bf16[512,256]{1,0:T(8,128)(2,1)S(1)} custom-call(bf16[512,768]{1,0:T(8,128)(2,1)S(1)} %get-tuple-element.16.mixed_ref, bf16[176,256]{1,0:T(8,128)(2,1)S(1)} %get-tuple-element.18.rim_ref, f32[3,7,256]{2,1,0:T(8,128)S(1)} %bitcast.22, f32[384,256]{1,0:T(8,128)S(1)} %copy-done.1, bf16[256,256]{1,0:T(8,128)(2,1)S(1)} %copy-done.6, ...), custom_call_target="tpu_custom_call" | custom-call | flops 8400000000 | bytes 8400000 | tf_op jit(solution)/shard_map/pallas_call | solution.py:294
  147.6 2.7 %collective-permute-start.9 = (bf16[512,256]{1,0:T(8,128)(2,1)S(1)}, bf16[512,256]{1,0:T(8,128)(2,1)S(1)}, u32[]{:S(2)}, u32[]{:S(2)}) collective-permute-start(bf16[512,256]{1,0:T(8,128)(2,1)S(1)} %shard_map.126.refs_0_), channel_id=1, source_target_pairs={{0,28},{4,0},{8,4},{12,8},{16,12},{20,16},{24,20},{28,24},{1,29},{... | collective-permute-start | bytes 786440 | tf_op jit(solution)/shard_map/ppermute | solution.py:26
  150.3 2.7 %collective-permute-start.21 = (bf16[512,256]{1,0:T(8,128)(2,1)S(1)}, bf16[512,256]{1,0:T(8,128)(2,1)S(1)}, u32[]{:S(2)}, u32[]{:S(2)}) collective-permute-start(bf16[512,256]{1,0:T(8,128)(2,1)S(1)} %collective-permute-done.19.refs_2_), channel_id=1, source_target_pairs={{0,28},{4,0},{8,4},{12,8},{16,12},{20,16},{24,20},{28,24},{1,29},{... | collective-permute-start | bytes 786440 | tf_op jit(solution)/shard_map/ppermute | solution.py:26
  153.0 4.1 %collective-permute-done.8.refs_1_ = bf16[512,256]{1,0:T(8,128)(2,1)S(1)} collective-permute-done((bf16[512,256]{1,0:T(8,128)(2,1)S(1)}, bf16[512,256]{1,0:T(8,128)(2,1)S(1)}, u32[]{:S(2)}, u32[]{:S(2)}) %collective-permute-start.8) | collective-permute-done | bytes 262176 | tf_op jit(solution)/shard_map/ppermute | solution.py:26
  157.1 2.7 %collective-permute-start.11 = (bf16[512,256]{1,0:T(8,128)(2,1)S(1)}, bf16[512,256]{1,0:T(8,128)(2,1)S(1)}, u32[]{:S(2)}, u32[]{:S(2)}) collective-permute-start(bf16[512,256]{1,0:T(8,128)(2,1)S(1)} %collective-permute-done.9.refs_2_), channel_id=1, source_target_pairs={{0,28},{4,0},{8,4},{12,8},{16,12},{20,16},{24,20},{28,24},{1,29},{... | collective-permute-start | bytes 786440 | tf_op jit(solution)/shard_map/ppermute | solution.py:26
  159.8 2.9 %collective-permute-done.20.refs_3_ = bf16[512,256]{1,0:T(8,128)(2,1)S(1)} collective-permute-done((bf16[512,256]{1,0:T(8,128)(2,1)S(1)}, bf16[512,256]{1,0:T(8,128)(2,1)S(1)}, u32[]{:S(2)}, u32[]{:S(2)}) %collective-permute-start.20) | collective-permute-done | bytes 262176 | tf_op jit(solution)/shard_map/ppermute | solution.py:26
  162.7 2.7 %collective-permute-start.23 = (bf16[512,256]{1,0:T(8,128)(2,1)S(1)}, bf16[512,256]{1,0:T(8,128)(2,1)S(1)}, u32[]{:S(2)}, u32[]{:S(2)}) collective-permute-start(bf16[512,256]{1,0:T(8,128)(2,1)S(1)} %collective-permute-done.21.refs_4_), channel_id=1, source_target_pairs={{0,28},{4,0},{8,4},{12,8},{16,12},{20,16},{24,20},{28,24},{1,29},{... | collective-permute-start | bytes 786440 | tf_op jit(solution)/shard_map/ppermute | solution.py:26
  165.4 2.9 %collective-permute-done.10.refs_3_ = bf16[512,256]{1,0:T(8,128)(2,1)S(1)} collective-permute-done((bf16[512,256]{1,0:T(8,128)(2,1)S(1)}, bf16[512,256]{1,0:T(8,128)(2,1)S(1)}, u32[]{:S(2)}, u32[]{:S(2)}) %collective-permute-start.10) | collective-permute-done | bytes 262176 | tf_op jit(solution)/shard_map/ppermute | solution.py:26
  168.3 2.7 %collective-permute-start.13 = (bf16[512,256]{1,0:T(8,128)(2,1)S(1)}, bf16[512,256]{1,0:T(8,128)(2,1)S(1)}, u32[]{:S(2)}, u32[]{:S(2)}) collective-permute-start(bf16[512,256]{1,0:T(8,128)(2,1)S(1)} %collective-permute-done.11.refs_4_), channel_id=1, source_target_pairs={{0,28},{4,0},{8,4},{12,8},{16,12},{20,16},{24,20},{28,24},{1,29},{... | collective-permute-start | bytes 786440 | tf_op jit(solution)/shard_map/ppermute | solution.py:26
  171.0 2.9 %collective-permute-done.22.ahead_ref.refs_5_ = bf16[512,256]{1,0:T(8,128)(2,1)S(1)} collective-permute-done((bf16[512,256]{1,0:T(8,128)(2,1)S(1)}, bf16[512,256]{1,0:T(8,128)(2,1)S(1)}, u32[]{:S(2)}, u32[]{:S(2)}) %collective-permute-start.22) | collective-permute-done | bytes 262176 | tf_op jit(solution)/shard_map/ppermute | solution.py:26
  179.9 3.0 %collective-permute-start.15 = (bf16[256,256]{1,0:T(8,128)(2,1)}, bf16[256,256]{1,0:T(8,128)(2,1)}, u32[]{:S(2)}, u32[]{:S(2)}) collective-permute-start(bf16[256,256]{1,0:T(8,128)(2,1)} %get-tuple-element.20), channel_id=1, source_target_pairs={{0,28},{4,0},{8,4},{12,8},{16,12},{20,16},{24,20},{28,24},{1,29},{... | collective-permute-start | bytes 393224 | tf_op jit(solution)/shard_map/ppermute | solution.py:26
  183.9 3.8 %shard_map.131.refs_11_ = bf16[1024,512]{1,0:T(8,128)(2,1)} custom-call(bf16[512,256]{1,0:T(8,128)(2,1)S(1)} %shard_map.129.refs_0_, bf16[512,256]{1,0:T(8,128)(2,1)S(1)} %collective-permute-done.18.refs_1_, bf16[512,256]{1,0:T(8,128)(2,1)S(1)} %collective-permute-done.19.refs_2_, bf16[512,256]{1,0:T(8,128)(2,1)S(1)} %collective-permute-done.20.refs_3_, ...), custom_call_target="tpu_custom_call" | custom-call | flops 5520000000 | bytes 5520000 | tf_op jit(solution)/shard_map/pallas_call | solution.py:339
  187.7 3.9 %shard_map.132 = bf16[1024,512]{1,0:T(8,128)(2,1)} custom-call(bf16[512,256]{1,0:T(8,128)(2,1)S(1)} %shard_map.126.refs_0_, bf16[512,256]{1,0:T(8,128)(2,1)S(1)} %collective-permute-done.8.refs_1_, bf16[512,256]{1,0:T(8,128)(2,1)S(1)} %collective-permute-done.9.refs_2_, ...), custom_call_target="tpu_custom_call", output_to_operand_aliasing={{}: (11, {})} | custom-call | flops 5520000000 | bytes 5520000 | tf_op jit(solution)/shard_map/pallas_call | solution.py:339
  (88 shorter events, 27.0 us)
Async XLA Ops:
  6.5 18.0 %copy-start = (f32[128,256]{1,0:T(8,128)S(1)}, f32[128,256]{1,0:T(8,128)}, u32[]{:S(2)}) copy-start(f32[128,256]{1,0:T(8,128)} %param.17) | copy-start | bytes 393220
  6.5 112.5 %all-gather.4.cloned.1.call-start = ((), (), s32[]{:S(2)}) async-start(), calls=%async_computation.3 | async-start | bytes 3244032 | tf_op jit(solution)/shard_map/all_gather | solution.py:439
  7.3 28.9 %collective-permute-start = (bf16[1024,512]{1,0:T(8,128)(2,1)}, bf16[1024,512]{1,0:T(8,128)(2,1)}, u32[]{:S(2)}, u32[]{:S(2)}) collective-permute-start(bf16[1024,512]{1,0:T(8,128)(2,1)} %bitcast.41), channel_id=1, source_target_pairs={{0,4},{4,8},{8,12},{12,16},{16,20},{20,24},{24,28},{28,0},{1,5},{5... | collective-permute-start | bytes 3145736 | tf_op jit(solution)/shard_map/ppermute | solution.py:26
  9.0 27.1 %collective-permute-start.1 = (bf16[1024,512]{1,0:T(8,128)(2,1)}, bf16[1024,512]{1,0:T(8,128)(2,1)S(1)}, u32[]{:S(2)}, u32[]{:S(2)}) collective-permute-start(bf16[1024,512]{1,0:T(8,128)(2,1)} %bitcast.42), channel_id=1, source_target_pairs={{0,28},{4,0},{8,4},{12,8},{16,12},{20,16},{24,20},{28,24},{1,29},{... | collective-permute-start | bytes 3145736 | tf_op jit(solution)/shard_map/ppermute | solution.py:26
  15.4 47.3 %all-to-all-start = ((bf16[32,64,512]{2,1,0:T(8,128)(2,1)}), bf16[32,64,512]{2,1,0:T(8,128)(2,1)S(1)}, u32[]{:S(2)}, u32[]{:S(2)}) async-start(bf16[32,64,512]{2,1,0:T(8,128)(2,1)} %broadcast_in_dim.4), calls=%async_computation | async-start | bytes 4194304 | tf_op jit(solution)/shard_map/all_to_all | solution.py:441
  23.6 159.3 %all-gather.6.cloned.1.call-start = ((), (), s32[]{:S(2)}) async-start(), calls=%async_computation.4 | async-start | bytes 2162688 | tf_op jit(solution)/shard_map/all_gather | solution.py:467
  36.1 38.4 %collective-permute-start.2 = (bf16[1024,512]{1,0:T(8,128)(2,1)}, bf16[1024,512]{1,0:T(8,128)(2,1)}, u32[]{:S(2)}, u32[]{:S(2)}) collective-permute-start(bf16[1024,512]{1,0:T(8,128)(2,1)} %collective-permute-done.refs_1_), channel_id=1, source_target_pairs={{0,4},{4,8},{8,12},{12,16},{16,20},{20,24},{24,28},{28,0},{1,5},{5... | collective-permute-start | bytes 3145736 | tf_op jit(solution)/shard_map/ppermute | solution.py:26
  36.1 39.9 %collective-permute-start.3 = (bf16[1024,512]{1,0:T(8,128)(2,1)S(1)}, bf16[1024,512]{1,0:T(8,128)(2,1)}, u32[]{:S(2)}, u32[]{:S(2)}) collective-permute-start(bf16[1024,512]{1,0:T(8,128)(2,1)S(1)} %collective-permute-done.1.refs_2_), channel_id=1, source_target_pairs={{0,28},{4,0},{8,4},{12,8},{16,12},{20,16},{24,20},{28,24},{1,29},{... | collective-permute-start | bytes 3145736 | tf_op jit(solution)/shard_map/ppermute | solution.py:26
  46.0 16.1 %collective-permute-start.16 = (bf16[128,256]{1,0:T(8,128)(2,1)S(1)}, bf16[128,256]{1,0:T(8,128)(2,1)S(1)}, u32[]{:S(2)}, u32[]{:S(2)}) collective-permute-start(bf16[128,256]{1,0:T(8,128)(2,1)S(1)} %shard_map.128), channel_id=1, source_target_pairs={{0,0},{4,4},{8,8},{12,12},{16,16},{20,20},{24,24},{28,28},{32,36},... | collective-permute-start | bytes 196616 | tf_op jit(solution)/shard_map/ppermute | solution.py:462
  67.8 16.2 %all-to-all-start.1 = ((f32[8,64,128]{2,1,0:T(8,128)}), f32[8,64,128]{2,1,0:T(8,128)S(1)}, u32[]{:S(2)}, u32[]{:S(2)}) async-start(f32[8,64,128]{2,1,0:T(8,128)} %shard_map.122), calls=%async_computation.1 | async-start | bytes 524288 | tf_op jit(solution)/shard_map/all_to_all | solution.py:449
  74.5 30.1 %collective-permute-start.4 = (bf16[1024,512]{1,0:T(8,128)(2,1)}, bf16[1024,512]{1,0:T(8,128)(2,1)}, u32[]{:S(2)}, u32[]{:S(2)}) collective-permute-start(bf16[1024,512]{1,0:T(8,128)(2,1)} %collective-permute-done.2.refs_1_), channel_id=1, source_target_pairs={{0,4},{4,8},{8,12},{12,16},{16,20},{20,24},{24,28},{28,0},{1,5},{5... | collective-permute-start | bytes 3145736 | tf_op jit(solution)/shard_map/ppermute | solution.py:26
  76.0 28.6 %collective-permute-start.5 = (bf16[1024,512]{1,0:T(8,128)(2,1)}, bf16[1024,512]{1,0:T(8,128)(2,1)S(1)}, u32[]{:S(2)}, u32[]{:S(2)}) collective-permute-start(bf16[1024,512]{1,0:T(8,128)(2,1)} %collective-permute-done.3.refs_2_), channel_id=1, source_target_pairs={{0,28},{4,0},{8,4},{12,8},{16,12},{20,16},{24,20},{28,24},{1,29},{... | collective-permute-start | bytes 3145736 | tf_op jit(solution)/shard_map/ppermute | solution.py:26
  84.6 30.6 %all-to-all-start.2 = ((bf16[8,64,128]{2,1,0:T(8,128)(2,1)}), bf16[8,64,128]{2,1,0:T(8,128)(2,1)S(1)}, u32[]{:S(2)}, u32[]{:S(2)}) async-start(bf16[8,64,128]{2,1,0:T(8,128)(2,1)} %shard_map.123), calls=%async_computation.2 | async-start | bytes 262144 | tf_op jit(solution)/shard_map/all_to_all | solution.py:451
  106.9 26.7 %collective-permute-start.7 = (bf16[512,512]{1,0:T(8,128)(2,1)S(1)}, bf16[512,512]{1,0:T(8,128)(2,1)S(1)}, u32[]{:S(2)}, u32[]{:S(2)}) collective-permute-start(bf16[512,512]{1,0:T(8,128)(2,1)S(1)} %get-tuple-element.17), channel_id=1, source_target_pairs={{0,28},{4,0},{8,4},{12,8},{16,12},{20,16},{24,20},{28,24},{1,29},{... | collective-permute-start | bytes 1572872 | tf_op jit(solution)/shard_map/ppermute | solution.py:26
  108.2 10.9 %collective-permute-start.6 = (bf16[512,512]{1,0:T(8,128)(2,1)S(1)}, bf16[512,512]{1,0:T(8,128)(2,1)S(1)}, u32[]{:S(2)}, u32[]{:S(2)}) collective-permute-start(bf16[512,512]{1,0:T(8,128)(2,1)S(1)} %get-tuple-element.15), channel_id=1, source_target_pairs={{0,4},{4,8},{8,12},{12,16},{16,20},{20,24},{24,28},{28,0},{1,5},{5... | collective-permute-start | bytes 1572872 | tf_op jit(solution)/shard_map/ppermute | solution.py:26
  124.7 14.3 %collective-permute-start.17 = (bf16[176,256]{1,0:T(8,128)(2,1)S(1)}, bf16[176,256]{1,0:T(8,128)(2,1)S(1)}, u32[]{:S(2)}, u32[]{:S(2)}) collective-permute-start(bf16[176,256]{1,0:T(8,128)(2,1)S(1)} %get-tuple-element.22), channel_id=1, source_target_pairs={{0,32},{32,64},{64,96},{96,128},{128,160},{160,192},{192,224},{1,3... | collective-permute-start | bytes 270344 | tf_op jit(solution)/shard_map/ppermute | solution.py:471
  141.9 8.3 %collective-permute-start.18 = (bf16[512,256]{1,0:T(8,128)(2,1)S(1)}, bf16[512,256]{1,0:T(8,128)(2,1)S(1)}, u32[]{:S(2)}, u32[]{:S(2)}) collective-permute-start(bf16[512,256]{1,0:T(8,128)(2,1)S(1)} %shard_map.129.refs_0_), channel_id=1, source_target_pairs={{0,4},{4,8},{8,12},{12,16},{16,20},{20,24},{24,28},{28,0},{1,5},{5... | collective-permute-start | bytes 786440 | tf_op jit(solution)/shard_map/ppermute | solution.py:26
  142.0 8.2 %collective-permute-start.19 = (bf16[512,256]{1,0:T(8,128)(2,1)S(1)}, bf16[512,256]{1,0:T(8,128)(2,1)S(1)}, u32[]{:S(2)}, u32[]{:S(2)}) collective-permute-start(bf16[512,256]{1,0:T(8,128)(2,1)S(1)} %shard_map.129.refs_0_), channel_id=1, source_target_pairs={{0,28},{4,0},{8,4},{12,8},{16,12},{20,16},{24,20},{28,24},{1,29},{... | collective-permute-start | bytes 786440 | tf_op jit(solution)/shard_map/ppermute | solution.py:26
  147.5 9.6 %collective-permute-start.8 = (bf16[512,256]{1,0:T(8,128)(2,1)S(1)}, bf16[512,256]{1,0:T(8,128)(2,1)S(1)}, u32[]{:S(2)}, u32[]{:S(2)}) collective-permute-start(bf16[512,256]{1,0:T(8,128)(2,1)S(1)} %shard_map.126.refs_0_), channel_id=1, source_target_pairs={{0,4},{4,8},{8,12},{12,16},{16,20},{20,24},{24,28},{28,0},{1,5},{5... | collective-permute-start | bytes 786440 | tf_op jit(solution)/shard_map/ppermute | solution.py:26
  147.6 9.5 %collective-permute-start.9 = (bf16[512,256]{1,0:T(8,128)(2,1)S(1)}, bf16[512,256]{1,0:T(8,128)(2,1)S(1)}, u32[]{:S(2)}, u32[]{:S(2)}) collective-permute-start(bf16[512,256]{1,0:T(8,128)(2,1)S(1)} %shard_map.126.refs_0_), channel_id=1, source_target_pairs={{0,28},{4,0},{8,4},{12,8},{16,12},{20,16},{24,20},{28,24},{1,29},{... | collective-permute-start | bytes 786440 | tf_op jit(solution)/shard_map/ppermute | solution.py:26
  150.3 12.4 %collective-permute-start.20 = (bf16[512,256]{1,0:T(8,128)(2,1)S(1)}, bf16[512,256]{1,0:T(8,128)(2,1)S(1)}, u32[]{:S(2)}, u32[]{:S(2)}) collective-permute-start(bf16[512,256]{1,0:T(8,128)(2,1)S(1)} %collective-permute-done.18.refs_1_), channel_id=1, source_target_pairs={{0,4},{4,8},{8,12},{12,16},{16,20},{20,24},{24,28},{28,0},{1,5},{5... | collective-permute-start | bytes 786440 | tf_op jit(solution)/shard_map/ppermute | solution.py:26
  150.3 12.4 %collective-permute-start.21 = (bf16[512,256]{1,0:T(8,128)(2,1)S(1)}, bf16[512,256]{1,0:T(8,128)(2,1)S(1)}, u32[]{:S(2)}, u32[]{:S(2)}) collective-permute-start(bf16[512,256]{1,0:T(8,128)(2,1)S(1)} %collective-permute-done.19.refs_2_), channel_id=1, source_target_pairs={{0,28},{4,0},{8,4},{12,8},{16,12},{20,16},{24,20},{28,24},{1,29},{... | collective-permute-start | bytes 786440 | tf_op jit(solution)/shard_map/ppermute | solution.py:26
  157.1 11.2 %collective-permute-start.10 = (bf16[512,256]{1,0:T(8,128)(2,1)S(1)}, bf16[512,256]{1,0:T(8,128)(2,1)S(1)}, u32[]{:S(2)}, u32[]{:S(2)}) collective-permute-start(bf16[512,256]{1,0:T(8,128)(2,1)S(1)} %collective-permute-done.8.refs_1_), channel_id=1, source_target_pairs={{0,4},{4,8},{8,12},{12,16},{16,20},{20,24},{24,28},{28,0},{1,5},{5... | collective-permute-start | bytes 786440 | tf_op jit(solution)/shard_map/ppermute | solution.py:26
  157.1 11.2 %collective-permute-start.11 = (bf16[512,256]{1,0:T(8,128)(2,1)S(1)}, bf16[512,256]{1,0:T(8,128)(2,1)S(1)}, u32[]{:S(2)}, u32[]{:S(2)}) collective-permute-start(bf16[512,256]{1,0:T(8,128)(2,1)S(1)} %collective-permute-done.9.refs_2_), channel_id=1, source_target_pairs={{0,28},{4,0},{8,4},{12,8},{16,12},{20,16},{24,20},{28,24},{1,29},{... | collective-permute-start | bytes 786440 | tf_op jit(solution)/shard_map/ppermute | solution.py:26
  162.7 11.2 %collective-permute-start.22 = (bf16[512,256]{1,0:T(8,128)(2,1)S(1)}, bf16[512,256]{1,0:T(8,128)(2,1)S(1)}, u32[]{:S(2)}, u32[]{:S(2)}) collective-permute-start(bf16[512,256]{1,0:T(8,128)(2,1)S(1)} %collective-permute-done.20.refs_3_), channel_id=1, source_target_pairs={{0,4},{4,8},{8,12},{12,16},{16,20},{20,24},{24,28},{28,0},{1,5},{5... | collective-permute-start | bytes 786440 | tf_op jit(solution)/shard_map/ppermute | solution.py:26
  162.7 11.2 %collective-permute-start.23 = (bf16[512,256]{1,0:T(8,128)(2,1)S(1)}, bf16[512,256]{1,0:T(8,128)(2,1)S(1)}, u32[]{:S(2)}, u32[]{:S(2)}) collective-permute-start(bf16[512,256]{1,0:T(8,128)(2,1)S(1)} %collective-permute-done.21.refs_4_), channel_id=1, source_target_pairs={{0,28},{4,0},{8,4},{12,8},{16,12},{20,16},{24,20},{28,24},{1,29},{... | collective-permute-start | bytes 786440 | tf_op jit(solution)/shard_map/ppermute | solution.py:26
  168.3 10.8 %collective-permute-start.12 = (bf16[512,256]{1,0:T(8,128)(2,1)S(1)}, bf16[512,256]{1,0:T(8,128)(2,1)S(1)}, u32[]{:S(2)}, u32[]{:S(2)}) collective-permute-start(bf16[512,256]{1,0:T(8,128)(2,1)S(1)} %collective-permute-done.10.refs_3_), channel_id=1, source_target_pairs={{0,4},{4,8},{8,12},{12,16},{16,20},{20,24},{24,28},{28,0},{1,5},{5... | collective-permute-start | bytes 786440 | tf_op jit(solution)/shard_map/ppermute | solution.py:26
  168.3 10.8 %collective-permute-start.13 = (bf16[512,256]{1,0:T(8,128)(2,1)S(1)}, bf16[512,256]{1,0:T(8,128)(2,1)S(1)}, u32[]{:S(2)}, u32[]{:S(2)}) collective-permute-start(bf16[512,256]{1,0:T(8,128)(2,1)S(1)} %collective-permute-done.11.refs_4_), channel_id=1, source_target_pairs={{0,28},{4,0},{8,4},{12,8},{16,12},{20,16},{24,20},{28,24},{1,29},{... | collective-permute-start | bytes 786440 | tf_op jit(solution)/shard_map/ppermute | solution.py:26
  174.7 8.2 %collective-permute-start.24 = (bf16[256,256]{1,0:T(8,128)(2,1)}, bf16[256,256]{1,0:T(8,128)(2,1)}, u32[]{:S(2)}, u32[]{:S(2)}) collective-permute-start(bf16[256,256]{1,0:T(8,128)(2,1)} %get-tuple-element.23), channel_id=1, source_target_pairs={{0,4},{4,8},{8,12},{12,16},{16,20},{20,24},{24,28},{28,0},{1,5},{5... | collective-permute-start | bytes 393224 | tf_op jit(solution)/shard_map/ppermute | solution.py:26
  175.1 7.8 %collective-permute-start.25 = (bf16[256,256]{1,0:T(8,128)(2,1)}, bf16[256,256]{1,0:T(8,128)(2,1)}, u32[]{:S(2)}, u32[]{:S(2)}) collective-permute-start(bf16[256,256]{1,0:T(8,128)(2,1)} %get-tuple-element.24), channel_id=1, source_target_pairs={{0,28},{4,0},{8,4},{12,8},{16,12},{20,16},{24,20},{28,24},{1,29},{... | collective-permute-start | bytes 393224 | tf_op jit(solution)/shard_map/ppermute | solution.py:26
  179.9 7.8 %collective-permute-start.14 = (bf16[256,256]{1,0:T(8,128)(2,1)}, bf16[256,256]{1,0:T(8,128)(2,1)}, u32[]{:S(2)}, u32[]{:S(2)}) collective-permute-start(bf16[256,256]{1,0:T(8,128)(2,1)} %get-tuple-element.19), channel_id=1, source_target_pairs={{0,4},{4,8},{8,12},{12,16},{16,20},{20,24},{24,28},{28,0},{1,5},{5... | collective-permute-start | bytes 393224 | tf_op jit(solution)/shard_map/ppermute | solution.py:26
  179.9 7.8 %collective-permute-start.15 = (bf16[256,256]{1,0:T(8,128)(2,1)}, bf16[256,256]{1,0:T(8,128)(2,1)}, u32[]{:S(2)}, u32[]{:S(2)}) collective-permute-start(bf16[256,256]{1,0:T(8,128)(2,1)} %get-tuple-element.20), channel_id=1, source_target_pairs={{0,28},{4,0},{8,4},{12,8},{16,12},{20,16},{24,20},{28,24},{1,29},{... | collective-permute-start | bytes 393224 | tf_op jit(solution)/shard_map/ppermute | solution.py:26
  (18 other events, 150.2 us)
Sparse Core Ops, SparseCore 0:
  9.9 65.1 all-gather.3
  77.6 48.1 all-gather.5
